TPU v7x, 256 devices: a whole 4x4x8 slice. The times are simulated.
256 devices in a mesh: section: 32 (over x, z_hi, core), dp: 8 (over z_lo, y).
Axes of the slice: x: 4, y: 4, z: 8 (z_hi: 4, z_lo: 2; z = z_hi * 2 + z_lo), core: 2. Of those that a mesh axis runs over, the one named last changes fastest.
Arguments:
- x_fwd: bfloat16 [32, 512, 5120], P('section', 'dp'), may hold values from -45 to 45
- x_bwd: bfloat16 [32, 512, 5120], P('section', 'dp'), may hold values from -45 to 45
- grad_in: bfloat16 [32, 512, 5120], P('section', 'dp'), may hold values from -25 to 25
- gain: float32 [32, 5120], P('section'), may hold values from 0.1 to 1.9
- weight: bfloat16 [32, 5120, 3072], P('section', 'dp'), may hold values from -0.078125 to 0.078125
- damping: float32 [32], P('section'), may hold values from 0.1 to 1
Outputs:
- next_fwd: bfloat16 [32, 512, 5120], P('section', 'dp')
- next_grad: bfloat16 [32, 512, 5120], P('section', 'dp')
- update: bfloat16 [32, 5120, 3072], P('section', 'dp')
All inputs are finite; a program needn't handle non-finite values.
Results may differ from a plain program's by a relative error of at most 0.012.
The roundings to bfloat16 on the way count: a program that leaves them out, or rounds other values in their place, can miss the bound.
Values may be sent and summed in bfloat16 or wider, within the bound.
No kernel may reach another device: no remote copies, remote signals or barrier semaphores. Data moves between devices by JAX's collectives and lax.ppermute only.
A program may use at most 128 MiB of HBM per device.

v0:
```python
import jax
import jax.numpy as jnp
from jax import lax
from jax.experimental import pallas as pl
from jax.experimental.pallas import tpu as pltpu
from jax.sharding import PartitionSpec as P

BLOCK = 1024
EPS = 1e-06
F32 = jnp.float32
BF16 = jnp.bfloat16
EXACT = lax.Precision.HIGHEST


def dot(a, b, contract=(1, 0), precision=EXACT):
    return lax.dot_general(
        a,
        b,
        (((contract[0],), (contract[1],)), ((), ())),
        precision=precision,
        preferred_element_type=F32,
    )


def from_behind(value, axis, steps):
    count = lax.axis_size(axis)
    leading, last = (max(0, -steps), min(count, count - steps))
    return lax.ppermute(value, axis, [(source, source + steps) for source in range(leading, last)])


def normalize(x, gain):
    wide = x.astype(F32)
    scale = lax.rsqrt(jnp.mean(wide * wide, axis=-1, keepdims=True) + EPS)
    return ((wide * scale * gain).astype(BF16), scale)


def eye_mask(order):
    rows = lax.broadcasted_iota(jnp.int32, (order, order), 0)
    return rows == lax.broadcasted_iota(jnp.int32, (order, order), 1)


def step_coefficients(low, high):
    mid, half = (low + high) * 0.5, (high - low) * 0.5
    scale = 1.0 / (2.0 * mid * mid - half * half)
    return 4.0 * mid * scale, 2.0 * scale, half * half * scale


def split(value):
    high = value.astype(BF16)
    rest = value - high.astype(F32)
    middle = rest.astype(BF16)
    return high, middle, (rest - middle.astype(F32)).astype(BF16)


def dot_three(a, b):
    a_high, a_low, _ = split(a)
    b_high, b_low, _ = split(b)
    low = dot(a_low, b_high, precision=None) + dot(a_high, b_low, precision=None)
    return low + dot(a_high, b_high, precision=None)


def fourth_root(square):
    return jnp.sqrt(jnp.sqrt(jnp.sum(square * square)))


def by_rows(count, step, body):
    def one(index, carry):
        body(pl.ds(pl.multiple_of(index * step, step), step))
        return carry

    lax.fori_loop(0, count // step, one, 0)


def scaled_newton(spread, step):
    def once(spread):
        first, second, after = step_coefficients(1.0 - spread, 1.0 + spread)
        step(first, second)
        return after

    lax.while_loop(lambda spread: spread > 2e-2, once, spread)


def invert(matrix, low, state):
    order = matrix.shape[0]
    eye = eye_mask(order).astype(F32)
    square = dot(matrix, matrix)
    high = jnp.maximum(fourth_root(square), low) * 1.001
    first, second, spread = step_coefficients(low, high)
    state[:order] = first * eye - second * matrix
    state[order:] = first * matrix - second * square

    def step(first, second):
        both = state[...]
        state[...] = first * both - second * dot_three(both, both[order:])

    scaled_newton(spread, step)
    guess = state[:order]
    return guess + dot_three(guess, eye - dot(matrix, guess))


def invert_by_halves(factor, damping, state, parts):
    half = factor.shape[0] // 2
    parts[0] = factor[:half, :half]

    def stage(index, carry):
        inverse = invert(parts[index], damping, state)

        @pl.when(index == 0)
        def _():
            corner, upper = parts[0], factor[:half, half:]
            tall = dot(inverse, upper)

            parts[3] = tall - dot(inverse, dot(corner, tall) - upper)
            tall = parts[3]
            error = dot(corner, tall) - upper
            parts[1] = factor[half:, half:] - dot(tall.T, upper - error)

            parts[2] = inverse

        @pl.when(index == 1)
        def _():
            parts[1] = inverse

        return carry

    lax.fori_loop(0, 2, stage, 0)
    inverse, tall, rest = parts[2], parts[3], parts[1]
    cross = dot(tall, rest)
    factor[:half, :half] = inverse + dot(cross, tall.T)
    factor[:half, half:] = -cross
    factor[half:, :half] = -cross.T
    factor[half:, half:] = rest


def invert_whole(factor, damping, whole, spare):
    order = factor.shape[0]
    eye = eye_mask(order).astype(F32)

    def square(rows):
        spare[rows] = dot(factor[rows], factor[...])

    by_rows(order, 128, square)
    high = jnp.maximum(fourth_root(spare[...]), damping) * 1.001
    first, second, spread = step_coefficients(damping, high)
    whole[:order] = first * eye - second * factor[...]
    whole[order:] = first * factor[...] - second * spare[...]

    def step(first, second):
        spare[...] = whole[order:]

        def some(rows):
            whole[rows] = first * whole[rows] - second * dot(whole[rows], spare[...])

        by_rows(2 * order, 128, some)

    scaled_newton(spread, step)

    def polish(_, carry):
        def residual(rows):
            spare[rows] = dot(factor[rows], whole[:order])

        by_rows(order, 128, residual)
        spare[...] = eye - spare[...]

        def correct(rows):
            whole[rows] += dot(whole[rows], spare[...])

        by_rows(order, 128, correct)
        return carry

    lax.fori_loop(0, 3, polish, 0)


def apply_inverse(damping, rows_ref, columns, out_ref, out_columns, scratch):
    factor, state, parts, whole, spare = scratch
    count = rows_ref.shape[0]
    half = count // 2
    width = 256

    def gram(rows):
        factor[rows] = dot(rows_ref[rows, columns(0, BLOCK)], rows_ref[:, columns(0, BLOCK)], (1, 1), None) * (
            1.0 / count
        )

    by_rows(count, half, gram)
    squares = []
    for corner in (factor[:half, :half], factor[half:, half:]):
        corner = corner.astype(BF16)
        squares.append(jnp.abs(dot(corner, corner, precision=None)))
    easy = fourth_root(jnp.maximum(*squares)) < HARDEST * damping
    factor[...] = jnp.where(eye_mask(count), factor[...] + damping, factor[...])

    @pl.when(easy)
    def _():
        invert_by_halves(factor, damping, state, parts)

        def solve(rows):
            high, low, _ = split(factor[rows])
            block = rows_ref[:, columns(0, BLOCK)]
            solved = dot(low, block, precision=None) + dot(high, block, precision=None)
            out_ref[rows, out_columns(0, BLOCK)] = solved.astype(BF16)

        by_rows(count, half, solve)

    @pl.when(jnp.logical_not(easy))
    def _():
        invert_whole(factor, damping, whole, spare)

        def solve(index, carry):
            start = index * width
            exact = rows_ref[:, columns(start, width)].astype(F32)

            def guess(rows):
                spare[rows, :width] = dot(whole[rows], exact)

            def residual(rows):
                spare[rows, width:] = dot(factor[rows], spare[:, :width])

            def correct(rows):
                fixed = spare[rows, :width] + dot(whole[rows], spare[:, width:])
                out_ref[rows, out_columns(start, width)] = fixed.astype(BF16)

            by_rows(count, 128, guess)
            by_rows(count, 128, residual)
            spare[:, width:] = exact - spare[:, width:]
            by_rows(count, 128, correct)
            return carry

        lax.fori_loop(0, BLOCK // width, solve, 0)


HARDEST = 2e4
ACT_MIB = 18
GRAD_MIB = 24


def solver_scratch(count):
    half = count // 2
    return [
        pltpu.VMEM((count, count), F32),
        pltpu.VMEM((count, half), F32),
        pltpu.VMEM((4, half, half), F32),
        pltpu.VMEM((2 * count, count), F32),
        pltpu.VMEM((count, count), F32),
    ]


OWNERS = (0, 2, 4, 5, 7)
UNIT = 128
MOVES = (
    (5, {0: 0, 2: 2, 4: 3, 5: 1, 7: 3}, {0: 0, 2: 0, 4: -1, 5: 0, 7: 0}),
    (4, {0: 4, 4: 0, 7: 0}, {1: -1, 3: 1, 6: 2}),
    (2, {2: 0, 5: 6}, {1: 3, 6: 0}),
    (1, {2: 7, 5: 0}, {3: 0, 4: 4}),
)
PAIRS = (None, ((0, 1), (4, 3), (7, 6)), ((2, 1), (5, 6)), ((2, 3), (5, 4)))
WINDOW = 5


def lookup(table, missing, me):
    value = jnp.int32(missing)
    for device, entry in table.items():
        value = jnp.where(me == device, entry, value)
    return value


def act_kernel(damping_ref, me_ref, rows_ref, left_ref, *refs):
    moves, (solved_ref, *scratch) = refs[: len(MOVES)], refs[len(MOVES) :]

    def columns(start, size):
        return slice(start, start + size) if isinstance(start, int) else pl.ds(start, size)

    apply_inverse(damping_ref[0, 0], rows_ref, columns, solved_ref, columns, scratch)

    def compare(rows):
        left_ref[rows] = dot(solved_ref[rows, :], rows_ref[:, :BLOCK], (1, 1), None)

    by_rows(solved_ref.shape[0], 256, compare)
    for (units, first, _), out in zip(MOVES, moves):
        start = pl.multiple_of(lookup(first, 0, me_ref[0, 0]) * UNIT, UNIT)
        out[...] = solved_ref[:, pl.ds(start, units * UNIT)]


def assemble_kernel(me_ref, *refs):
    moves, (out_ref, buffer) = refs[: len(MOVES)], refs[len(MOVES) :]
    for (units, _, place), piece in zip(MOVES, moves):
        start = (lookup(place, WINDOW + 1, me_ref[0, 0]) + 1) * UNIT
        buffer[:, pl.ds(pl.multiple_of(start, UNIT), units * UNIT)] = piece[...]
    out_ref[...] = buffer[:, UNIT : (WINDOW + 1) * UNIT].T


def grad_kernel(damping_ref, rows_ref, left_ref, solved_ref, term_ref, right, *scratch):
    count, width = rows_ref.shape

    def one(index, carry):
        def columns(start, size):
            return pl.ds(pl.multiple_of(index * BLOCK + start, UNIT), size)

        apply_inverse(damping_ref[0, 0], rows_ref, columns, solved_ref, columns, scratch)
        return carry

    lax.fori_loop(0, width // BLOCK, one, 0)

    def compare(rows):
        product = dot(solved_ref[rows, :], rows_ref[...], (1, 1), None)
        right[rows] = product * left_ref[rows]

    by_rows(count, 256, compare)
    product = jnp.sum(right[...], axis=0, keepdims=True)
    term_ref[...] = jnp.sum(product, axis=1, keepdims=True)


VMEM = pl.BlockSpec(memory_space=pltpu.VMEM)
SMEM = pl.BlockSpec(memory_space=pltpu.SMEM)


def solve_act(damping, me, rows):
    count = rows.shape[0]
    return pl.pallas_call(
        act_kernel,
        out_shape=(jax.ShapeDtypeStruct((count, count), F32),)
        + tuple(jax.ShapeDtypeStruct((count, units * UNIT), BF16) for units, _, _ in MOVES),
        in_specs=[SMEM, SMEM, VMEM],
        out_specs=(VMEM,) * (len(MOVES) + 1),
        scratch_shapes=[pltpu.VMEM((count, BLOCK), BF16)] + solver_scratch(count),
        compiler_params=pltpu.CompilerParams(vmem_limit_bytes=ACT_MIB * 2**20),
        cost_estimate=pl.CostEstimate(
            flops=16 * 10**9, bytes_accessed=4 * 2**20, transcendentals=0
        ),
        name="solve_act",
    )(damping, me, rows)


def solve_grad(damping, rows, left):
    count, width = rows.shape
    return pl.pallas_call(
        grad_kernel,
        out_shape=(
            jax.ShapeDtypeStruct((count, width), BF16),
            jax.ShapeDtypeStruct((1, 1), F32),
        ),
        in_specs=[SMEM, VMEM, VMEM],
        out_specs=(VMEM, VMEM),
        scratch_shapes=[pltpu.VMEM((count, count), F32)] + solver_scratch(count),
        compiler_params=pltpu.CompilerParams(vmem_limit_bytes=GRAD_MIB * 2**20),
        cost_estimate=pl.CostEstimate(
            flops=45 * 10**9, bytes_accessed=8 * 2**20, transcendentals=0
        ),
        name="solve_grad",
    )(damping, rows, left)


def swap(value, offset):
    return lax.ppermute(value, "dp", [(i, i ^ offset) for i in range(8)])


def normalize_kernel(fwd_ref, bwd_ref, gain_ref, out_ref):
    gain = gain_ref[...]
    normed_b, _ = normalize(bwd_ref[...], gain)
    normed_f, _ = normalize(fwd_ref[...], gain)
    part = normed_f.shape[1] // out_ref.shape[0]
    for device in range(out_ref.shape[0]):
        if device in OWNERS:
            block = OWNERS.index(device)
            out_ref[device, :, :BLOCK] = normed_b[:, block * BLOCK : (block + 1) * BLOCK]
        else:
            out_ref[device, :, :BLOCK] = jnp.zeros((normed_b.shape[0], BLOCK), BF16)
        out_ref[device, :, BLOCK:] = normed_f[:, device * part : (device + 1) * part]


def product_kernel(me_ref, *refs):
    me = me_ref[0, 0]
    pieces, (rows_ref, weight_ref, gathered, out_ref) = refs[:-4], refs[-4:]
    groups, tokens, _ = out_ref.shape
    part, width = weight_ref.shape
    for offset, piece in enumerate(pieces):
        start = pl.multiple_of((me ^ offset) * tokens, tokens)
        gathered[pl.ds(start, tokens), :] = piece[...]
    for start in range(0, width, 512):
        columns = slice(start, start + 512)
        forward = dot(rows_ref[:, BLOCK:], weight_ref[:, columns], precision=None)
        out_ref[:, :, columns] = forward.astype(BF16).reshape(groups, tokens, 512)
    backward = dot(gathered[...], weight_ref[...], (1, 1), None)
    out_ref[:, :, width:] = backward.astype(BF16).reshape(groups, tokens, part)


def finish_kernel(parts_ref, fwd_ref, bwd_ref, grad_ref, gain_ref, next_ref, back_ref):
    groups = parts_ref.shape[0]
    width = fwd_ref.shape[1]
    part = width // groups
    out_width = parts_ref.shape[2] - part
    layer = parts_ref[0, :, :out_width].astype(F32)
    for group in range(1, groups):
        layer += parts_ref[group, :, :out_width].astype(F32)
    next_ref[0, :, :out_width] = (fwd_ref[:, :out_width].astype(F32) + layer).astype(BF16)
    next_ref[0, :, out_width:] = fwd_ref[:, out_width:]
    wide = bwd_ref[...].astype(F32)
    scale = lax.rsqrt(jnp.mean(wide * wide, axis=-1, keepdims=True) + EPS)
    back = jnp.concatenate([parts_ref[group, :, out_width:] for group in range(groups)], axis=1)
    scaled = back.astype(F32) * gain_ref[...]
    inner = jnp.mean(scaled * wide, axis=-1, keepdims=True)
    out = grad_ref[...].astype(F32) + scale * scaled - wide * scale**3 * inner
    back_ref[0] = out.astype(BF16)


def update_kernel(entries, terms_ref, turned_ref, grad_ref, out_ref):
    terms = terms_ref[...]
    total = jnp.sum(jnp.sum(terms, axis=0, keepdims=True)[:, :1], axis=1, keepdims=True)
    ratio = jnp.sqrt(entries / total)
    out_ref[...] = (ratio * dot(turned_ref[...], grad_ref[...], precision=None)).astype(BF16)


def shape(*dims, dtype=BF16):
    return jax.ShapeDtypeStruct(dims, dtype)


def cost(flops, moved):
    return pl.CostEstimate(flops=flops, bytes_accessed=moved, transcendentals=0)


def params(mib):
    return pltpu.CompilerParams(vmem_limit_bytes=mib * 2**20)


def per_device(x_fwd, x_bwd, grad_in, gain, weight, damping):
    fwd = x_fwd[0]
    bwd = x_bwd[0]
    grad = grad_in[0]
    local_w = weight[0]
    tokens, width = fwd.shape
    own_rows, out_width = local_w.shape
    groups = lax.axis_size("dp")
    group = groups * tokens
    me = lax.axis_index("dp")
    me_value = me.reshape(1, 1)
    damp_value = damping.reshape(1, 1)

    upstream = grad[:, :out_width]
    pieces = [upstream] + [swap(upstream, offset) for offset in range(1, groups)]

    sent = pl.pallas_call(
        normalize_kernel,
        out_shape=shape(groups, tokens, BLOCK + own_rows),
        in_specs=[VMEM] * 3,
        out_specs=VMEM,
        compiler_params=params(32),
        cost_estimate=cost(10**7, 3 * 10**6),
        name="normalize",
    )(fwd, bwd, gain)
    rows = lax.all_to_all(sent, "dp", 0, 0, tiled=True).reshape(group, BLOCK + own_rows)

    left, *moves = solve_act(damp_value, me_value, rows)

    ready = lax.optimization_barrier((me_value, *pieces, rows, left))
    group_grad, products = pl.pallas_call(
        product_kernel,
        out_shape=(shape(group, out_width), shape(groups, tokens, out_width + own_rows)),
        in_specs=[SMEM] + [VMEM] * (len(pieces) + 2),
        out_specs=(VMEM,) * 2,
        compiler_params=params(40),
        cost_estimate=cost(4 * 10**9, 10**7),
        name="products",
    )(*ready[:-1], local_w)
    parts = lax.all_to_all(products, "dp", 0, 0, tiled=True)

    moves = moves[:1] + [
        lax.ppermute(piece, "dp", pairs) for piece, pairs in zip(moves[1:], PAIRS[1:])
    ]
    turned = pl.pallas_call(
        assemble_kernel,
        out_shape=shape(own_rows, group),
        in_specs=[SMEM] + [VMEM] * len(MOVES),
        out_specs=VMEM,
        scratch_shapes=[pltpu.VMEM((group, (2 * WINDOW + 2) * UNIT), BF16)],
        compiler_params=params(16),
        cost_estimate=cost(10**7, 3 * 10**6),
        name="assemble",
    )(me_value, *moves)

    grad_tilde, term = solve_grad(damp_value, group_grad, left)
    devices = lax.axis_size("section") * groups
    terms = lax.all_to_all(
        jnp.broadcast_to(term, (devices, 128)), ("section", "dp"), 0, 0, tiled=True
    )

    parts, _ = lax.optimization_barrier((parts, term))
    out_f, out_b = pl.pallas_call(
        finish_kernel,
        out_shape=(shape(1, tokens, width),) * 2,
        in_specs=[VMEM] * 5,
        out_specs=(VMEM,) * 2,
        compiler_params=params(32),
        cost_estimate=cost(10**7, 8 * 10**6),
        name="finish",
    )(parts, fwd, bwd, grad, gain)
    next_fwd = from_behind(out_f, "section", 1)
    next_grad = from_behind(out_b, "section", -1)

    columns = 512
    entries = float(lax.axis_size("section") * width * out_width)
    update = pl.pallas_call(
        lambda *refs: update_kernel(entries, *refs),
        grid=(out_width // columns,),
        out_shape=shape(own_rows, out_width),
        in_specs=[
            pl.BlockSpec((devices, 128), lambda i: (0, 0)),
            pl.BlockSpec((own_rows, group), lambda i: (0, 0)),
            pl.BlockSpec((group, columns), lambda i: (0, i)),
        ],
        out_specs=pl.BlockSpec((own_rows, columns), lambda i: (0, i)),
        compiler_params=params(32),
        cost_estimate=cost(2 * 10**9, 8 * 10**6),
        name="update",
    )(terms, turned, grad_tilde)
    return (next_fwd, next_grad, update[None])


def solution(mesh):
    return jax.shard_map(
        per_device,
        mesh=mesh,
        in_specs=(
            P("section", "dp", None),
            P("section", "dp", None),
            P("section", "dp", None),
            P("section", None),
            P("section", "dp", None),
            P("section"),
        ),
        out_specs=(P("section", "dp", None), P("section", "dp", None), P("section", "dp", None)),
        check_vma=False,
    )
```

profile of v0, /device:TPU:40, one launch (start us, length us, event | category | flops | bytes accessed | tf_op | source)
XLA Modules:
  0.0 189.4 jit_solution(7255129731707059851)
XLA Ops:
  3.5 1.9 %normalize.1 = bf16[8,64,1664]{2,1,0:T(8,128)(2,1)} custom-call(bf16[64,5120]{1,0:T(8,128)(2,1)S(1)} %bitcast.12, bf16[64,5120]{1,0:T(8,128)(2,1)S(1)} %bitcast.14, f32[1,5120]{1,0:T(1,128)S(1)} %copy-done.11), custom_call_target="tpu_custom_call" | custom-call | flops 10000000 | bytes 3000000 | tf_op jit(solution)/shard_map/normalize/pallas_call | solution.py:441
  5.5 5.8 %all-to-all-start = ((bf16[8,64,1664]{2,1,0:T(8,128)(2,1)}), bf16[8,64,1664]{2,1,0:T(8,128)(2,1)S(1)}, u32[]{:S(2)}, u32[]{:S(2)}) async-start(bf16[8,64,1664]{2,1,0:T(8,128)(2,1)} %normalize.1), calls=%async_computation | async-start | bytes 3407872 | tf_op jit(solution)/shard_map/all_to_all | solution.py:450
  11.3 1.5 collective-permute-start.6
  12.9 2.1 %collective-permute-start.5 = (bf16[64,3072]{1,0:T(8,128)(2,1)S(1)}, bf16[64,3072]{1,0:T(8,128)(2,1)S(1)}, u32[]{:S(2)}, u32[]{:S(2)}) collective-permute-start(bf16[64,3072]{1,0:T(8,128)(2,1)S(1)} %slice.4.refs_0_), channel_id=1, source_target_pairs={{0,6},{1,7},{2,4},{3,5},{4,2},{5,3},{6,0},{7,1},{8,14},{9,15},{10,... | collective-permute-start | bytes 1179656 | tf_op jit(solution)/shard_map/ppermute | solution.py:354
  15.0 1.5 collective-permute-start.4
  16.4 1.5 collective-permute-start.3
  17.9 1.5 collective-permute-start.2
  20.0 21.9 %collective-permute-done.6.refs_7_ = bf16[64,3072]{1,0:T(8,128)(2,1)S(1)} collective-permute-done((bf16[64,3072]{1,0:T(8,128)(2,1)S(1)}, bf16[64,3072]{1,0:T(8,128)(2,1)S(1)}, u32[]{:S(2)}, u32[]{:S(2)}) %collective-permute-start.6) | collective-permute-done | bytes 393248 | tf_op jit(solution)/shard_map/ppermute | solution.py:354
  43.2 7.6 %collective-permute-done.5.refs_6_ = bf16[64,3072]{1,0:T(8,128)(2,1)S(1)} collective-permute-done((bf16[64,3072]{1,0:T(8,128)(2,1)S(1)}, bf16[64,3072]{1,0:T(8,128)(2,1)S(1)}, u32[]{:S(2)}, u32[]{:S(2)}) %collective-permute-start.5) | collective-permute-done | bytes 393248 | tf_op jit(solution)/shard_map/ppermute | solution.py:354
  50.8 1.6 collective-permute-start
  52.5 13.9 %solve_act.1 = (f32[512,512]{1,0:T(8,128)S(1)}, bf16[512,640]{1,0:T(8,128)(2,1)S(1)}, bf16[512,512]{1,0:T(8,128)(2,1)}, bf16[512,256]{1,0:T(8,128)(2,1)}, bf16[512,128]{1,0:T(8,128)(2,1)S(1)}) custom-call(f32[1,1]{1,0:T(1,128)} %bitcast.10.damping_ref, s32[1,1]{1,0:T(1,128)} %bitcast.me_ref, bf16[512,1664]{1,0:T(8,128)(2,1)S(1)} %bitcast.16), custom_call_target="tpu_custom_call" | custom-call | flops 16000000000 | bytes 4194304 | tf_op jit(solution)/shard_map/solve_act/pallas_call | solution.py:319
  69.0 4.7 %collective-permute-done.refs_1_ = bf16[64,3072]{1,0:T(8,128)(2,1)} collective-permute-done((bf16[64,3072]{1,0:T(8,128)(2,1)S(1)}, bf16[64,3072]{1,0:T(8,128)(2,1)}, u32[]{:S(2)}, u32[]{:S(2)}) %collective-permute-start) | collective-permute-done | bytes 393248 | tf_op jit(solution)/shard_map/ppermute | solution.py:354
  73.6 7.8 %products.1 = (bf16[512,3072]{1,0:T(8,128)(2,1)S(1)}, bf16[8,64,3712]{2,1,0:T(8,128)(2,1)S(1)}) custom-call(s32[1,1]{1,0:T(1,128)} %bitcast.me_ref, bf16[64,3072]{1,0:T(8,128)(2,1)S(1)} %slice.4.refs_0_, bf16[64,3072]{1,0:T(8,128)(2,1)} %collective-permute-done.refs_1_, bf16[64,3072]{1,0:T(8,128)(2,1)} %collective-permute-done.1.refs_2_, ...), custom_call_target="tpu_custom_call" | custom-call | flops 4000000000 | bytes 10000000 | tf_op jit(solution)/shard_map/products/pallas_call | solution.py:455
  81.4 1.9 copy-done
  83.3 1.7 copy-done.14
  85.0 6.0 %all-to-all-start.1 = ((bf16[8,64,3712]{2,1,0:T(8,128)(2,1)}), bf16[8,64,3712]{2,1,0:T(8,128)(2,1)}, u32[]{:S(2)}, u32[]{:S(2)}) async-start(bf16[8,64,3712]{2,1,0:T(8,128)(2,1)} %copy-done), calls=%async_computation.1 | async-start | bytes 7602176 | tf_op jit(solution)/shard_map/all_to_all | solution.py:464
  91.0 1.5 collective-permute-start.9
  92.5 1.9 copy-done.15
  95.6 35.6 %solve_grad.1 = (bf16[512,3072]{1,0:T(8,128)(2,1)S(1)}, f32[1,1]{1,0:T(1,128)}) custom-call(f32[1,1]{1,0:T(1,128)} %bitcast.11.damping_ref, bf16[512,3072]{1,0:T(8,128)(2,1)S(1)} %copy-done.15, f32[512,512]{1,0:T(8,128)S(1)} %copy-done.17), custom_call_target="tpu_custom_call" | custom-call | flops 44999999488 | bytes 8388608 | tf_op jit(solution)/shard_map/solve_grad/pallas_call | solution.py:336
  131.2 3.6 %all-to-all-done.1.parts_ref = bf16[8,64,3712]{2,1,0:T(8,128)(2,1)} async-done(((bf16[8,64,3712]{2,1,0:T(8,128)(2,1)}), bf16[8,64,3712]{2,1,0:T(8,128)(2,1)}, u32[]{:S(2)}, u32[]{:S(2)}) %all-to-all-start.1) | async-done | bytes 3801120 | tf_op jit(solution)/shard_map/all_to_all | solution.py:464
  138.0 4.6 %finish.1 = (bf16[1,64,5120]{2,1,0:T(8,128)(2,1)}, bf16[1,64,5120]{2,1,0:T(8,128)(2,1)}) custom-call(bf16[8,64,3712]{2,1,0:T(8,128)(2,1)} %all-to-all-done.1.parts_ref, bf16[64,5120]{1,0:T(8,128)(2,1)S(1)} %bitcast.13, bf16[64,5120]{1,0:T(8,128)(2,1)S(1)} %bitcast.15, bf16[64,5120]{1,0:T(8,128)(2,1)S(1)} %bitcast.19, f32[1,5120]{1,0:T(1,128)S(1)} %copy-done.12), custom_call_target="tpu_custom_call" | custom-call | flops 10000000 | bytes 8000000 | tf_op jit(solution)/shard_map/finish/pallas_call | solution.py:487
  142.6 2.7 %collective-permute-start.7 = (bf16[1,64,5120]{2,1,0:T(8,128)(2,1)}, bf16[1,64,5120]{2,1,0:T(8,128)(2,1)}, u32[]{:S(2)}, u32[]{:S(2)}) collective-permute-start(bf16[1,64,5120]{2,1,0:T(8,128)(2,1)} %get-tuple-element.40), channel_id=1, source_target_pairs={{0,8},{8,16},{16,24},{24,32},{32,40},{40,48},{48,56},{56,64},{64,7... | collective-permute-start | bytes 1966088 | tf_op jit(solution)/shard_map/ppermute | solution.py:28
  146.6 1.9 collective-permute-start.10
  148.5 1.3 broadcast_in_dim.11
  149.8 18.0 %all-to-all-start.2 = ((f32[256,1,128]{2,1,0:T(1,128)}), f32[256,1,128]{2,1,0:T(1,128)S(1)}, u32[]{:S(2)}, u32[]{:S(2)}) async-start(f32[256,1,128]{2,1,0:T(1,128)} %broadcast_in_dim.11), calls=%async_computation.2 | async-start | bytes 262144 | tf_op jit(solution)/shard_map/all_to_all | solution.py:482
  167.8 2.4 %collective-permute-start.11 = (bf16[512,128]{1,0:T(8,128)(2,1)}, bf16[512,128]{1,0:T(8,128)(2,1)S(1)}, u32[]{:S(2)}, u32[]{:S(2)}) collective-permute-start(bf16[512,128]{1,0:T(8,128)(2,1)} %copy-done.13), channel_id=1, source_target_pairs={{2,3},{5,4},{10,11},{13,12},{18,19},{21,20},{26,27},{29,28},{34,35... | collective-permute-start | bytes 393224 | tf_op jit(solution)/shard_map/ppermute | solution.py:467
  170.2 4.0 %collective-permute-done.11.refs_3_ = bf16[512,128]{1,0:T(8,128)(2,1)S(1)} collective-permute-done((bf16[512,128]{1,0:T(8,128)(2,1)}, bf16[512,128]{1,0:T(8,128)(2,1)S(1)}, u32[]{:S(2)}, u32[]{:S(2)}) %collective-permute-start.11) | collective-permute-done | bytes 131104 | tf_op jit(solution)/shard_map/ppermute | solution.py:467
  175.3 1.4 assemble.1.refs_1_
  177.6 2.1 %all-to-all-done.2 = f32[256,1,128]{2,1,0:T(1,128)S(1)} async-done(((f32[256,1,128]{2,1,0:T(1,128)}), f32[256,1,128]{2,1,0:T(1,128)S(1)}, u32[]{:S(2)}, u32[]{:S(2)}) %all-to-all-start.2) | async-done | bytes 131104 | tf_op jit(solution)/shard_map/all_to_all | solution.py:482
  180.7 4.7 %update.1 = bf16[640,3072]{1,0:T(8,128)(2,1)} custom-call(f32[256,128]{1,0:T(8,128)S(1)} %bitcast.20, bf16[640,512]{1,0:T(8,128)(2,1)S(1)} %copy-done.6, bf16[512,3072]{1,0:T(8,128)(2,1)S(1)} %get-tuple-element.46.refs_2_), custom_call_target="tpu_custom_call" | custom-call | flops 2000000000 | bytes 8000000 | tf_op jit(solution)/shard_map/update/pallas_call | solution.py:501
  185.4 2.0 %copy.12 = bf16[1,64,5120]{2,1,0:T(8,128)(2,1)} copy(bf16[1,64,5120]{2,1,0:T(8,128)(2,1)} %collective-permute-done.7) | data formatting | bytes 1310720
  187.4 2.0 %copy.13 = bf16[1,64,5120]{2,1,0:T(8,128)(2,1)} copy(bf16[1,64,5120]{2,1,0:T(8,128)(2,1)} %collective-permute-done.8) | data formatting | bytes 1310720
  (45 shorter events, 15.6 us)
Async XLA Ops:
  0.6 1.1 copy-start.1
  1.7 1.1 copy-start.3
  2.8 0.7 copy-start.11
  3.5 7.8 %copy-start.7 = (bf16[1,64,5120]{2,1,0:T(8,128)(2,1)S(1)}, bf16[1,64,5120]{2,1,0:T(8,128)(2,1)}, u32[]{:S(2)}) copy-start(bf16[1,64,5120]{2,1,0:T(8,128)(2,1)} %param.8) | copy-start | bytes 1966084
  5.5 47.0 %all-to-all-start = ((bf16[8,64,1664]{2,1,0:T(8,128)(2,1)}), bf16[8,64,1664]{2,1,0:T(8,128)(2,1)S(1)}, u32[]{:S(2)}, u32[]{:S(2)}) async-start(bf16[8,64,1664]{2,1,0:T(8,128)(2,1)} %normalize.1), calls=%async_computation | async-start | bytes 3407872 | tf_op jit(solution)/shard_map/all_to_all | solution.py:450
  11.3 30.6 %collective-permute-start.6 = (bf16[64,3072]{1,0:T(8,128)(2,1)S(1)}, bf16[64,3072]{1,0:T(8,128)(2,1)S(1)}, u32[]{:S(2)}, u32[]{:S(2)}) collective-permute-start(bf16[64,3072]{1,0:T(8,128)(2,1)S(1)} %slice.4.refs_0_), channel_id=1, source_target_pairs={{0,7},{1,6},{2,5},{3,4},{4,3},{5,2},{6,1},{7,0},{8,15},{9,14},{10,... | collective-permute-start | bytes 1179656 | tf_op jit(solution)/shard_map/ppermute | solution.py:354
  12.9 38.0 %collective-permute-start.5 = (bf16[64,3072]{1,0:T(8,128)(2,1)S(1)}, bf16[64,3072]{1,0:T(8,128)(2,1)S(1)}, u32[]{:S(2)}, u32[]{:S(2)}) collective-permute-start(bf16[64,3072]{1,0:T(8,128)(2,1)S(1)} %slice.4.refs_0_), channel_id=1, source_target_pairs={{0,6},{1,7},{2,4},{3,5},{4,2},{5,3},{6,0},{7,1},{8,14},{9,15},{10,... | collective-permute-start | bytes 1179656 | tf_op jit(solution)/shard_map/ppermute | solution.py:354
  15.0 54.0 %collective-permute-start.4 = (bf16[64,3072]{1,0:T(8,128)(2,1)S(1)}, bf16[64,3072]{1,0:T(8,128)(2,1)S(1)}, u32[]{:S(2)}, u32[]{:S(2)}) collective-permute-start(bf16[64,3072]{1,0:T(8,128)(2,1)S(1)} %slice.4.refs_0_), channel_id=1, source_target_pairs={{0,5},{1,4},{2,7},{3,6},{4,1},{5,0},{6,3},{7,2},{8,13},{9,12},{10,... | collective-permute-start | bytes 1179656 | tf_op jit(solution)/shard_map/ppermute | solution.py:354
  16.4 52.5 %collective-permute-start.3 = (bf16[64,3072]{1,0:T(8,128)(2,1)S(1)}, bf16[64,3072]{1,0:T(8,128)(2,1)}, u32[]{:S(2)}, u32[]{:S(2)}) collective-permute-start(bf16[64,3072]{1,0:T(8,128)(2,1)S(1)} %slice.4.refs_0_), channel_id=1, source_target_pairs={{0,4},{1,5},{2,6},{3,7},{4,0},{5,1},{6,2},{7,3},{8,12},{9,13},{10,... | collective-permute-start | bytes 1179656 | tf_op jit(solution)/shard_map/ppermute | solution.py:354
  17.9 51.1 %collective-permute-start.2 = (bf16[64,3072]{1,0:T(8,128)(2,1)S(1)}, bf16[64,3072]{1,0:T(8,128)(2,1)}, u32[]{:S(2)}, u32[]{:S(2)}) collective-permute-start(bf16[64,3072]{1,0:T(8,128)(2,1)S(1)} %slice.4.refs_0_), channel_id=1, source_target_pairs={{0,3},{1,2},{2,1},{3,0},{4,7},{5,6},{6,5},{7,4},{8,11},{9,10},{10,... | collective-permute-start | bytes 1179656 | tf_op jit(solution)/shard_map/ppermute | solution.py:354
  41.9 27.0 %collective-permute-start.1 = (bf16[64,3072]{1,0:T(8,128)(2,1)S(1)}, bf16[64,3072]{1,0:T(8,128)(2,1)}, u32[]{:S(2)}, u32[]{:S(2)}) collective-permute-start(bf16[64,3072]{1,0:T(8,128)(2,1)S(1)} %slice.4.refs_0_), channel_id=1, source_target_pairs={{0,2},{1,3},{2,0},{3,1},{4,6},{5,7},{6,4},{7,5},{8,10},{9,11},{10,... | collective-permute-start | bytes 1179656 | tf_op jit(solution)/shard_map/ppermute | solution.py:354
  50.8 22.8 %collective-permute-start = (bf16[64,3072]{1,0:T(8,128)(2,1)S(1)}, bf16[64,3072]{1,0:T(8,128)(2,1)}, u32[]{:S(2)}, u32[]{:S(2)}) collective-permute-start(bf16[64,3072]{1,0:T(8,128)(2,1)S(1)} %slice.4.refs_0_), channel_id=1, source_target_pairs={{0,1},{1,0},{2,3},{3,2},{4,5},{5,4},{6,7},{7,6},{8,9},{9,8},{10,11... | collective-permute-start | bytes 1179656 | tf_op jit(solution)/shard_map/ppermute | solution.py:354
  66.4 0.9 copy-start.9
  67.9 1.0 copy-start.16
  81.4 1.9 copy-start
  83.3 1.7 copy-start.14
  85.0 49.8 %all-to-all-start.1 = ((bf16[8,64,3712]{2,1,0:T(8,128)(2,1)}), bf16[8,64,3712]{2,1,0:T(8,128)(2,1)}, u32[]{:S(2)}, u32[]{:S(2)}) async-start(bf16[8,64,3712]{2,1,0:T(8,128)(2,1)} %copy-done), calls=%async_computation.1 | async-start | bytes 7602176 | tf_op jit(solution)/shard_map/all_to_all | solution.py:464
  91.0 83.2 %collective-permute-start.9 = (bf16[512,512]{1,0:T(8,128)(2,1)}, bf16[512,512]{1,0:T(8,128)(2,1)}, u32[]{:S(2)}, u32[]{:S(2)}) collective-permute-start(bf16[512,512]{1,0:T(8,128)(2,1)} %get-tuple-element.43), channel_id=1, source_target_pairs={{0,1},{4,3},{7,6},{8,9},{12,11},{15,14},{16,17},{20,19},{23,22},{2... | collective-permute-start | bytes 1572872 | tf_op jit(solution)/shard_map/ppermute | solution.py:467
  92.5 1.9 copy-start.15
  94.4 1.2 copy-start.17
  95.6 39.2 %copy-start.12 = (f32[1,5120]{1,0:T(1,128)S(1)}, f32[1,5120]{1,0:T(1,128)}, u32[]{:S(2)}) copy-start(f32[1,5120]{1,0:T(1,128)} %gain_ref.3) | copy-start | bytes 61444
  134.8 1.1 copy-start.2
  135.9 1.1 copy-start.4
  137.0 1.1 copy-start.8
  142.6 42.8 %collective-permute-start.7 = (bf16[1,64,5120]{2,1,0:T(8,128)(2,1)}, bf16[1,64,5120]{2,1,0:T(8,128)(2,1)}, u32[]{:S(2)}, u32[]{:S(2)}) collective-permute-start(bf16[1,64,5120]{2,1,0:T(8,128)(2,1)} %get-tuple-element.40), channel_id=1, source_target_pairs={{0,8},{8,16},{16,24},{24,32},{32,40},{40,48},{48,56},{56,64},{64,7... | collective-permute-start | bytes 1966088 | tf_op jit(solution)/shard_map/ppermute | solution.py:28
  145.3 40.1 %collective-permute-start.8 = (bf16[1,64,5120]{2,1,0:T(8,128)(2,1)}, bf16[1,64,5120]{2,1,0:T(8,128)(2,1)}, u32[]{:S(2)}, u32[]{:S(2)}) collective-permute-start(bf16[1,64,5120]{2,1,0:T(8,128)(2,1)} %get-tuple-element.41), channel_id=1, source_target_pairs={{8,0},{16,8},{24,16},{32,24},{40,32},{48,40},{56,48},{64,56},{72,6... | collective-permute-start | bytes 1966088 | tf_op jit(solution)/shard_map/ppermute | solution.py:28
  146.6 27.6 %collective-permute-start.10 = (bf16[512,256]{1,0:T(8,128)(2,1)}, bf16[512,256]{1,0:T(8,128)(2,1)S(1)}, u32[]{:S(2)}, u32[]{:S(2)}) collective-permute-start(bf16[512,256]{1,0:T(8,128)(2,1)} %get-tuple-element.44), channel_id=1, source_target_pairs={{2,1},{5,6},{10,9},{13,14},{18,17},{21,22},{26,25},{29,30},{34,33}... | collective-permute-start | bytes 786440 | tf_op jit(solution)/shard_map/ppermute | solution.py:467
  149.8 29.8 %all-to-all-start.2 = ((f32[256,1,128]{2,1,0:T(1,128)}), f32[256,1,128]{2,1,0:T(1,128)S(1)}, u32[]{:S(2)}, u32[]{:S(2)}) async-start(f32[256,1,128]{2,1,0:T(1,128)} %broadcast_in_dim.11), calls=%async_computation.2 | async-start | bytes 262144 | tf_op jit(solution)/shard_map/all_to_all | solution.py:482
  167.8 6.4 %collective-permute-start.11 = (bf16[512,128]{1,0:T(8,128)(2,1)}, bf16[512,128]{1,0:T(8,128)(2,1)S(1)}, u32[]{:S(2)}, u32[]{:S(2)}) collective-permute-start(bf16[512,128]{1,0:T(8,128)(2,1)} %copy-done.13), channel_id=1, source_target_pairs={{2,3},{5,4},{10,11},{13,12},{18,19},{21,20},{26,27},{29,28},{34,35... | collective-permute-start | bytes 393224 | tf_op jit(solution)/shard_map/ppermute | solution.py:467
  174.2 1.1 copy-start.10
  176.7 0.8 copy-start.5
  179.6 1.1 copy-start.6
  (1 other events, 0.7 us)
where the time goes:
time: 193 us; the launch traced here: 189 us
  Pallas kernels  69.9 us (36%)
  starting transfers between devices  50.5 us (26%)
  waiting for transfers between devices  43.9 us (23%)
  local copies, waits for them, and re-layouts  23.7 us (12%)
    pallas_call x1, Pallas kernels, solve_grad(): pl.pallas_call(grad_kernel, out_shape=(jax.ShapeDtypeStruct((count, width...  35.6 us
    ppermute x7, waiting for transfers between devices, swap(): return lax.ppermute(value, 'dp', [(i, i ^ offset) for i in range(8)])  34.2 us
    unnamed x38, local copies, waits for them, and re-layouts  22.3 us
    all_to_all x1, starting transfers between devices, per_device(): lax.all_to_all(jnp.broadcast_to(term, (devices, 128)), ('section', 'dp'),...  18 us
    pallas_call x1, Pallas kernels, solve_act(): pl.pallas_call(act_kernel, out_shape=(jax.ShapeDtypeStruct((count, count)...  13.9 us
    ppermute x7, starting transfers between devices, swap(): return lax.ppermute(value, 'dp', [(i, i ^ offset) for i in range(8)])  10.9 us
    pallas_call x1, Pallas kernels, per_device(): pl.pallas_call(product_kernel, out_shape=(shape(group, out_width), shape(...  7.79 us
    all_to_all x1, starting transfers between devices, per_device(): parts = lax.all_to_all(products, 'dp', 0, 0, tiled=True)  6.01 us
  transfers between devices with their start and end apart: 15, of which 6 were waited for; matrix products, arithmetic and copies ran while one was open for 1% of the time, Pallas kernels for 32%

commit v1 on v0

--- a/solution.py
+++ b/solution.py
@@ -230,8 +230,8 @@
 
 
 HARDEST = 2e4
-ACT_MIB = 18
-GRAD_MIB = 24
+ACT_MIB = 14
+GRAD_MIB = 16
 
 
 def solver_scratch(count):
@@ -368,18 +368,23 @@
         out_ref[device, :, BLOCK:] = normed_f[:, device * part : (device + 1) * part]
 
 
+def forward_kernel(rows_ref, weight_ref, out_ref):
+    for start in range(0, weight_ref.shape[1], 512):
+        columns = slice(start, start + 512)
+        forward = dot(rows_ref[:, BLOCK:], weight_ref[:, columns], precision=None)
+        out_ref[:, columns] = forward.astype(BF16)
+
+
 def product_kernel(me_ref, *refs):
     me = me_ref[0, 0]
-    pieces, (rows_ref, weight_ref, gathered, out_ref) = refs[:-4], refs[-4:]
+    pieces, (forward_ref, weight_ref, gathered, out_ref) = refs[:-4], refs[-4:]
     groups, tokens, _ = out_ref.shape
     part, width = weight_ref.shape
     for offset, piece in enumerate(pieces):
         start = pl.multiple_of((me ^ offset) * tokens, tokens)
         gathered[pl.ds(start, tokens), :] = piece[...]
-    for start in range(0, width, 512):
-        columns = slice(start, start + 512)
-        forward = dot(rows_ref[:, BLOCK:], weight_ref[:, columns], precision=None)
-        out_ref[:, :, columns] = forward.astype(BF16).reshape(groups, tokens, 512)
+    for device in range(groups):
+        out_ref[device, :, :width] = forward_ref[device * tokens : (device + 1) * tokens, :]
     backward = dot(gathered[...], weight_ref[...], (1, 1), None)
     out_ref[:, :, width:] = backward.astype(BF16).reshape(groups, tokens, part)
 
@@ -389,18 +394,32 @@
     width = fwd_ref.shape[1]
     part = width // groups
     out_width = parts_ref.shape[2] - part
-    layer = parts_ref[0, :, :out_width].astype(F32)
-    for group in range(1, groups):
-        layer += parts_ref[group, :, :out_width].astype(F32)
-    next_ref[0, :, :out_width] = (fwd_ref[:, :out_width].astype(F32) + layer).astype(BF16)
-    next_ref[0, :, out_width:] = fwd_ref[:, out_width:]
-    wide = bwd_ref[...].astype(F32)
-    scale = lax.rsqrt(jnp.mean(wide * wide, axis=-1, keepdims=True) + EPS)
-    back = jnp.concatenate([parts_ref[group, :, out_width:] for group in range(groups)], axis=1)
-    scaled = back.astype(F32) * gain_ref[...]
-    inner = jnp.mean(scaled * wide, axis=-1, keepdims=True)
-    out = grad_ref[...].astype(F32) + scale * scaled - wide * scale**3 * inner
-    back_ref[0] = out.astype(BF16)
+
+    def some(rows):
+        for start in range(0, out_width, 1024):
+            columns = slice(start, start + 1024)
+            layer = parts_ref[0, rows, columns].astype(F32)
+            for group in range(1, groups):
+                layer += parts_ref[group, rows, columns].astype(F32)
+            next_ref[0, rows, columns] = (fwd_ref[rows, columns].astype(F32) + layer).astype(BF16)
+        next_ref[0, rows, out_width:] = fwd_ref[rows, out_width:]
+        squares, inner = 0.0, 0.0
+        for group in range(groups):
+            columns = slice(group * part, (group + 1) * part)
+            wide = bwd_ref[rows, columns].astype(F32)
+            scaled = parts_ref[group, rows, out_width:].astype(F32) * gain_ref[:, columns]
+            squares += jnp.sum(wide * wide, axis=1, keepdims=True)
+            inner += jnp.sum(scaled * wide, axis=1, keepdims=True)
+        scale = lax.rsqrt(squares * (1.0 / width) + EPS)
+        pull = scale**3 * (inner * (1.0 / width))
+        for group in range(groups):
+            columns = slice(group * part, (group + 1) * part)
+            wide = bwd_ref[rows, columns].astype(F32)
+            scaled = parts_ref[group, rows, out_width:].astype(F32) * gain_ref[:, columns]
+            out = grad_ref[rows, columns].astype(F32) + scale * scaled - wide * pull
+            back_ref[0, rows, columns] = out.astype(BF16)
+
+    by_rows(fwd_ref.shape[0], 16, some)
 
 
 def update_kernel(entries, terms_ref, turned_ref, grad_ref, out_ref):
@@ -436,28 +455,41 @@
     damp_value = damping.reshape(1, 1)
 
     upstream = grad[:, :out_width]
-    pieces = [upstream] + [swap(upstream, offset) for offset in range(1, groups)]
+    other = swap(upstream, groups // 2)
+    pieces = [upstream] + [swap(upstream, offset) for offset in range(1, groups // 2)]
+    fwd_late, bwd_late, other = lax.optimization_barrier((fwd, bwd, other))
+    pieces += [other] + [swap(other, offset) for offset in range(1, groups // 2)]
 
     sent = pl.pallas_call(
         normalize_kernel,
         out_shape=shape(groups, tokens, BLOCK + own_rows),
         in_specs=[VMEM] * 3,
         out_specs=VMEM,
-        compiler_params=params(32),
+        compiler_params=params(8),
         cost_estimate=cost(10**7, 3 * 10**6),
         name="normalize",
-    )(fwd, bwd, gain)
+    )(fwd_late, bwd_late, gain)
     rows = lax.all_to_all(sent, "dp", 0, 0, tiled=True).reshape(group, BLOCK + own_rows)
 
     left, *moves = solve_act(damp_value, me_value, rows)
 
-    ready = lax.optimization_barrier((me_value, *pieces, rows, left))
+    forward = pl.pallas_call(
+        forward_kernel,
+        out_shape=shape(group, out_width),
+        in_specs=[VMEM] * 2,
+        out_specs=VMEM,
+        compiler_params=params(12),
+        cost_estimate=cost(2 * 10**9, 8 * 10**6),
+        name="forward",
+    )(rows, local_w)
+
+    ready = lax.optimization_barrier((me_value, *pieces, forward, left))
     group_grad, products = pl.pallas_call(
         product_kernel,
         out_shape=(shape(group, out_width), shape(groups, tokens, out_width + own_rows)),
         in_specs=[SMEM] + [VMEM] * (len(pieces) + 2),
         out_specs=(VMEM,) * 2,
-        compiler_params=params(40),
+        compiler_params=params(16),
         cost_estimate=cost(4 * 10**9, 10**7),
         name="products",
     )(*ready[:-1], local_w)
@@ -489,12 +521,13 @@
         out_shape=(shape(1, tokens, width),) * 2,
         in_specs=[VMEM] * 5,
         out_specs=(VMEM,) * 2,
-        compiler_params=params(32),
+        compiler_params=params(12),
         cost_estimate=cost(10**7, 8 * 10**6),
         name="finish",
     )(parts, fwd, bwd, grad, gain)
     next_fwd = from_behind(out_f, "section", 1)
     next_grad = from_behind(out_b, "section", -1)
+    terms, next_fwd, next_grad = lax.optimization_barrier((terms, next_fwd, next_grad))
 
     columns = 512
     entries = float(lax.axis_size("section") * width * out_width)
@@ -508,7 +541,7 @@
             pl.BlockSpec((group, columns), lambda i: (0, i)),
         ],
         out_specs=pl.BlockSpec((own_rows, columns), lambda i: (0, i)),
-        compiler_params=params(32),
+        compiler_params=params(12),
         cost_estimate=cost(2 * 10**9, 8 * 10**6),
         name="update",
     )(terms, turned, grad_tilde)

time: 193 us -> 203 us (1.052); the launches traced: 189 us -> 202 us
  starting transfers between devices: 50.5 us -> 59.3 us
  waiting for transfers between devices: 43.9 us -> 50.2 us
    ppermute x7, waiting for transfers between devices: 34.2 us -> 39.5 us  [swap(): return lax.ppermute(value, 'dp', [(i, i ^ offset) for i in range(8)])]
    all_to_all x1, waiting for transfers between devices: 2.06 us -> 6.74 us  [per_device(): lax.all_to_all(jnp.broadcast_to(term, (devices, 128)), ('section', 'dp'),...]
    ppermute x7, starting transfers between devices: 10.9 us -> 15.2 us  [swap(): return lax.ppermute(value, 'dp', [(i, i ^ offset) for i in range(8)])]
    all_to_all x1, waiting for transfers between devices: 3.62 us -> 0.01 us  [per_device(): parts = lax.all_to_all(products, 'dp', 0, 0, tiled=True)]
    pallas_call x1, Pallas kernels: 7.79 us -> 4.34 us  [per_device(): pl.pallas_call(product_kernel, out_shape=(shape(group, out_width), shape(...]
    all_to_all x1, starting transfers between devices: 18 us -> 20.9 us  [per_device(): lax.all_to_all(jnp.broadcast_to(term, (devices, 128)), ('section', 'dp'),...]
    pallas_call x0 -> x1, Pallas kernels: none -> 2.61 us  [per_device(): pl.pallas_call(forward_kernel, out_shape=shape(group, out_width), in_spec...]
    unnamed x38, local copies, waits for them, and re-layouts: 22.3 us -> 19.8 us
  transfers between devices with their start and end apart: 15 -> 15, of which waited for: 6 -> 4; matrix products, arithmetic and copies ran while one was open for 1% -> 1% of each run, Pallas kernels for 32% -> 27%
where the time goes in v1:
time: 203 us; the launch traced here: 202 us
  Pallas kernels  69.2 us (34%)
  starting transfers between devices  59.3 us (29%)
  waiting for transfers between devices  50.2 us (25%)
  local copies, waits for them, and re-layouts  22.1 us (11%)
    ppermute x7, waiting for transfers between devices, swap(): return lax.ppermute(value, 'dp', [(i, i ^ offset) for i in range(8)])  39.5 us
    pallas_call x1, Pallas kernels, solve_grad(): pl.pallas_call(grad_kernel, out_shape=(jax.ShapeDtypeStruct((count, width...  35.6 us
    all_to_all x1, starting transfers between devices, per_device(): lax.all_to_all(jnp.broadcast_to(term, (devices, 128)), ('section', 'dp'),...  20.9 us
    unnamed x38, local copies, waits for them, and re-layouts  19.8 us
    ppermute x7, starting transfers between devices, swap(): return lax.ppermute(value, 'dp', [(i, i ^ offset) for i in range(8)])  15.2 us
    pallas_call x1, Pallas kernels, solve_act(): pl.pallas_call(act_kernel, out_shape=(jax.ShapeDtypeStruct((count, count)...  14.3 us
    ppermute x3, starting transfers between devices, per_device(): lax.ppermute(piece, 'dp', pairs)  7.09 us
    all_to_all x1, starting transfers between devices, per_device(): parts = lax.all_to_all(products, 'dp', 0, 0, tiled=True)  6.85 us
  transfers between devices with their start and end apart: 15, of which 4 were waited for; matrix products, arithmetic and copies ran while one was open for 1% of the time, Pallas kernels for 27%

profile of v1, /device:TPU:40, one launch (start us, length us, event | category | flops | bytes accessed | tf_op | source)
XLA Modules:
  0.0 202.3 jit_solution(1637767334349807837)
XLA Ops:
  1.9 10.7 %collective-permute-done.3.refs_4_ = bf16[64,3072]{1,0:T(8,128)(2,1)S(1)} collective-permute-done((bf16[64,3072]{1,0:T(8,128)(2,1)S(1)}, bf16[64,3072]{1,0:T(8,128)(2,1)S(1)}, u32[]{:S(2)}, u32[]{:S(2)}) %collective-permute-start.3) | collective-permute-done | bytes 393248 | tf_op jit(solution)/shard_map/ppermute | solution.py:354
  15.5 1.9 normalize.1
  17.4 5.8 %all-to-all-start = ((bf16[8,64,1664]{2,1,0:T(8,128)(2,1)}), bf16[8,64,1664]{2,1,0:T(8,128)(2,1)S(1)}, u32[]{:S(2)}, u32[]{:S(2)}) async-start(bf16[8,64,1664]{2,1,0:T(8,128)(2,1)} %normalize.1), calls=%async_computation | async-start | bytes 3407872 | tf_op jit(solution)/shard_map/all_to_all | solution.py:472
  23.3 1.5 collective-permute-start.2
  24.7 1.2 collective-permute-start.1
  25.9 1.5 collective-permute-start
  28.0 1.6 collective-permute-start.6
  30.7 28.8 %collective-permute-done.2.refs_3_ = bf16[64,3072]{1,0:T(8,128)(2,1)S(1)} collective-permute-done((bf16[64,3072]{1,0:T(8,128)(2,1)S(1)}, bf16[64,3072]{1,0:T(8,128)(2,1)S(1)}, u32[]{:S(2)}, u32[]{:S(2)}) %collective-permute-start.2) | collective-permute-done | bytes 393248 | tf_op jit(solution)/shard_map/ppermute | solution.py:354
  59.5 8.2 %collective-permute-start.4 = (bf16[64,3072]{1,0:T(8,128)(2,1)S(1)}, bf16[64,3072]{1,0:T(8,128)(2,1)}, u32[]{:S(2)}, u32[]{:S(2)}) collective-permute-start(bf16[64,3072]{1,0:T(8,128)(2,1)S(1)} %collective-permute-done.3.refs_4_), channel_id=1, source_target_pairs={{0,1},{1,0},{2,3},{3,2},{4,5},{5,4},{6,7},{7,6},{8,9},{9,8},{10,11... | collective-permute-start | bytes 1179656 | tf_op jit(solution)/shard_map/ppermute | solution.py:354
  67.7 14.3 %solve_act.1 = (f32[512,512]{1,0:T(8,128)S(1)}, bf16[512,640]{1,0:T(8,128)(2,1)S(1)}, bf16[512,512]{1,0:T(8,128)(2,1)}, bf16[512,256]{1,0:T(8,128)(2,1)}, bf16[512,128]{1,0:T(8,128)(2,1)S(1)}) custom-call(f32[1,1]{1,0:T(1,128)} %bitcast.10.damping_ref, s32[1,1]{1,0:T(1,128)} %bitcast.1.me_ref, bf16[512,1664]{1,0:T(8,128)(2,1)S(1)} %bitcast.12), custom_call_target="tpu_custom_call" | custom-call | flops 16000000000 | bytes 4194304 | tf_op jit(solution)/shard_map/solve_act/pallas_call | solution.py:319
  82.0 2.6 %forward.1.refs_8_ = bf16[512,3072]{1,0:T(8,128)(2,1)S(1)} custom-call(bf16[512,1664]{1,0:T(8,128)(2,1)S(1)} %bitcast.13, bf16[640,3072]{1,0:T(8,128)(2,1)S(1)} %bitcast.14), custom_call_target="tpu_custom_call" | custom-call | flops 2000000000 | bytes 8000000 | tf_op jit(solution)/shard_map/forward/pallas_call | solution.py:476
  84.7 4.3 %products.1 = (bf16[512,3072]{1,0:T(8,128)(2,1)S(1)}, bf16[8,64,3712]{2,1,0:T(8,128)(2,1)S(1)}) custom-call(s32[1,1]{1,0:T(1,128)} %bitcast.1.me_ref, bf16[64,3072]{1,0:T(8,128)(2,1)S(1)} %slice.4.refs_0_, bf16[64,3072]{1,0:T(8,128)(2,1)} %collective-permute-done.refs_1_, bf16[64,3072]{1,0:T(8,128)(2,1)S(1)} %collective-permute-done.1.refs_2_, ...), custom_call_target="tpu_custom_call" | custom-call | flops 4000000000 | bytes 10000000 | tf_op jit(solution)/shard_map/products/pallas_call | solution.py:487
  89.1 1.9 copy-done.1
  90.9 1.7 copy-done.14
  92.6 6.8 %all-to-all-start.2 = ((bf16[8,64,3712]{2,1,0:T(8,128)(2,1)}), bf16[8,64,3712]{2,1,0:T(8,128)(2,1)}, u32[]{:S(2)}, u32[]{:S(2)}) async-start(bf16[8,64,3712]{2,1,0:T(8,128)(2,1)} %copy-done.1), calls=%async_computation.2 | async-start | bytes 7602176 | tf_op jit(solution)/shard_map/all_to_all | solution.py:496
  99.5 1.9 copy-done.15
  101.4 1.2 copy-done.17
  102.6 35.6 %solve_grad.1 = (bf16[512,3072]{1,0:T(8,128)(2,1)S(1)}, f32[1,1]{1,0:T(1,128)}) custom-call(f32[1,1]{1,0:T(1,128)} %bitcast.11.damping_ref, bf16[512,3072]{1,0:T(8,128)(2,1)S(1)} %copy-done.15, f32[512,512]{1,0:T(8,128)S(1)} %copy-done.17), custom_call_target="tpu_custom_call" | custom-call | flops 44999999488 | bytes 8388608 | tf_op jit(solution)/shard_map/solve_grad/pallas_call | solution.py:336
  141.4 4.3 %finish.1 = (bf16[1,64,5120]{2,1,0:T(8,128)(2,1)}, bf16[1,64,5120]{2,1,0:T(8,128)(2,1)}) custom-call(bf16[8,64,3712]{2,1,0:T(8,128)(2,1)} %all-to-all-done.2.parts_ref, bf16[64,5120]{1,0:T(8,128)(2,1)S(1)} %bitcast.17, bf16[64,5120]{1,0:T(8,128)(2,1)S(1)} %bitcast.19, bf16[64,5120]{1,0:T(8,128)(2,1)S(1)} %bitcast.21, f32[1,5120]{1,0:T(1,128)S(1)} %copy-done.12), custom_call_target="tpu_custom_call" | custom-call | flops 10000000 | bytes 8000000 | tf_op jit(solution)/shard_map/finish/pallas_call | solution.py:519
  145.7 2.1 %collective-permute-start.7 = (bf16[1,64,5120]{2,1,0:T(8,128)(2,1)}, bf16[1,64,5120]{2,1,0:T(8,128)(2,1)}, u32[]{:S(2)}, u32[]{:S(2)}) collective-permute-start(bf16[1,64,5120]{2,1,0:T(8,128)(2,1)} %get-tuple-element.49), channel_id=1, source_target_pairs={{0,8},{8,16},{16,24},{24,32},{32,40},{40,48},{48,56},{56,64},{64,7... | collective-permute-start | bytes 1966088 | tf_op jit(solution)/shard_map/ppermute | solution.py:28
  147.9 1.3 collective-permute-start.8
  149.2 1.5 collective-permute-start.9
  150.6 3.2 %collective-permute-start.10 = (bf16[512,256]{1,0:T(8,128)(2,1)}, bf16[512,256]{1,0:T(8,128)(2,1)S(1)}, u32[]{:S(2)}, u32[]{:S(2)}) collective-permute-start(bf16[512,256]{1,0:T(8,128)(2,1)} %get-tuple-element.56), channel_id=1, source_target_pairs={{2,1},{5,6},{10,9},{13,14},{18,17},{21,22},{26,25},{29,30},{34,33}... | collective-permute-start | bytes 786440 | tf_op jit(solution)/shard_map/ppermute | solution.py:499
  153.8 1.3 broadcast_in_dim.11
  155.1 20.9 %all-to-all-start.1 = ((f32[256,1,128]{2,1,0:T(1,128)}), f32[256,1,128]{2,1,0:T(1,128)S(1)}, u32[]{:S(2)}, u32[]{:S(2)}) async-start(f32[256,1,128]{2,1,0:T(1,128)} %broadcast_in_dim.11), calls=%async_computation.1 | async-start | bytes 262144 | tf_op jit(solution)/shard_map/all_to_all | solution.py:514
  176.1 2.4 %collective-permute-start.11 = (bf16[512,128]{1,0:T(8,128)(2,1)}, bf16[512,128]{1,0:T(8,128)(2,1)S(1)}, u32[]{:S(2)}, u32[]{:S(2)}) collective-permute-start(bf16[512,128]{1,0:T(8,128)(2,1)} %copy-done.13), channel_id=1, source_target_pairs={{2,3},{5,4},{10,11},{13,12},{18,19},{21,20},{26,27},{29,28},{34,35... | collective-permute-start | bytes 393224 | tf_op jit(solution)/shard_map/ppermute | solution.py:499
  178.5 4.0 %collective-permute-done.11.refs_3_ = bf16[512,128]{1,0:T(8,128)(2,1)S(1)} collective-permute-done((bf16[512,128]{1,0:T(8,128)(2,1)}, bf16[512,128]{1,0:T(8,128)(2,1)S(1)}, u32[]{:S(2)}, u32[]{:S(2)}) %collective-permute-start.11) | collective-permute-done | bytes 131104 | tf_op jit(solution)/shard_map/ppermute | solution.py:499
  183.6 1.4 assemble.1.refs_1_
  185.8 6.7 %all-to-all-done.1 = f32[256,1,128]{2,1,0:T(1,128)S(1)} async-done(((f32[256,1,128]{2,1,0:T(1,128)}), f32[256,1,128]{2,1,0:T(1,128)S(1)}, u32[]{:S(2)}, u32[]{:S(2)}) %all-to-all-start.1) | async-done | bytes 131104 | tf_op jit(solution)/shard_map/all_to_all | solution.py:514
  193.7 4.7 %update.1 = bf16[640,3072]{1,0:T(8,128)(2,1)} custom-call(f32[256,128]{1,0:T(8,128)S(1)} %bitcast.22, bf16[640,512]{1,0:T(8,128)(2,1)S(1)} %copy-done.7, bf16[512,3072]{1,0:T(8,128)(2,1)S(1)} %get-tuple-element.58.refs_2_), custom_call_target="tpu_custom_call" | custom-call | flops 2000000000 | bytes 8000000 | tf_op jit(solution)/shard_map/update/pallas_call | solution.py:534
  198.4 2.0 copy.12
  200.3 2.0 copy.13
  (46 shorter events, 11.6 us)
Async XLA Ops:
  1.7 10.9 %collective-permute-start.3 = (bf16[64,3072]{1,0:T(8,128)(2,1)S(1)}, bf16[64,3072]{1,0:T(8,128)(2,1)S(1)}, u32[]{:S(2)}, u32[]{:S(2)}) collective-permute-start(bf16[64,3072]{1,0:T(8,128)(2,1)S(1)} %slice.4.refs_0_), channel_id=1, source_target_pairs={{0,4},{1,5},{2,6},{3,7},{4,0},{5,1},{6,2},{7,3},{8,12},{9,13},{10,... | collective-permute-start | bytes 1179656 | tf_op jit(solution)/shard_map/ppermute | solution.py:354
  12.6 1.1 copy-start.2
  13.7 1.1 copy-start.4
  17.4 50.3 %all-to-all-start = ((bf16[8,64,1664]{2,1,0:T(8,128)(2,1)}), bf16[8,64,1664]{2,1,0:T(8,128)(2,1)S(1)}, u32[]{:S(2)}, u32[]{:S(2)}) async-start(bf16[8,64,1664]{2,1,0:T(8,128)(2,1)} %normalize.1), calls=%async_computation | async-start | bytes 3407872 | tf_op jit(solution)/shard_map/all_to_all | solution.py:472
  23.3 36.2 %collective-permute-start.2 = (bf16[64,3072]{1,0:T(8,128)(2,1)S(1)}, bf16[64,3072]{1,0:T(8,128)(2,1)S(1)}, u32[]{:S(2)}, u32[]{:S(2)}) collective-permute-start(bf16[64,3072]{1,0:T(8,128)(2,1)S(1)} %slice.4.refs_0_), channel_id=1, source_target_pairs={{0,3},{1,2},{2,1},{3,0},{4,7},{5,6},{6,5},{7,4},{8,11},{9,10},{10,... | collective-permute-start | bytes 1179656 | tf_op jit(solution)/shard_map/ppermute | solution.py:354
  24.7 59.9 %collective-permute-start.1 = (bf16[64,3072]{1,0:T(8,128)(2,1)S(1)}, bf16[64,3072]{1,0:T(8,128)(2,1)S(1)}, u32[]{:S(2)}, u32[]{:S(2)}) collective-permute-start(bf16[64,3072]{1,0:T(8,128)(2,1)S(1)} %slice.4.refs_0_), channel_id=1, source_target_pairs={{0,2},{1,3},{2,0},{3,1},{4,6},{5,7},{6,4},{7,5},{8,10},{9,11},{10,... | collective-permute-start | bytes 1179656 | tf_op jit(solution)/shard_map/ppermute | solution.py:354
  25.9 58.8 %collective-permute-start = (bf16[64,3072]{1,0:T(8,128)(2,1)S(1)}, bf16[64,3072]{1,0:T(8,128)(2,1)}, u32[]{:S(2)}, u32[]{:S(2)}) collective-permute-start(bf16[64,3072]{1,0:T(8,128)(2,1)S(1)} %slice.4.refs_0_), channel_id=1, source_target_pairs={{0,1},{1,0},{2,3},{3,2},{4,5},{5,4},{6,7},{7,6},{8,9},{9,8},{10,11... | collective-permute-start | bytes 1179656 | tf_op jit(solution)/shard_map/ppermute | solution.py:354
  28.0 56.7 %collective-permute-start.6 = (bf16[64,3072]{1,0:T(8,128)(2,1)S(1)}, bf16[64,3072]{1,0:T(8,128)(2,1)}, u32[]{:S(2)}, u32[]{:S(2)}) collective-permute-start(bf16[64,3072]{1,0:T(8,128)(2,1)S(1)} %collective-permute-done.3.refs_4_), channel_id=1, source_target_pairs={{0,3},{1,2},{2,1},{3,0},{4,7},{5,6},{6,5},{7,4},{8,11},{9,10},{10,... | collective-permute-start | bytes 1179656 | tf_op jit(solution)/shard_map/ppermute | solution.py:354
  29.6 55.1 %collective-permute-start.5 = (bf16[64,3072]{1,0:T(8,128)(2,1)S(1)}, bf16[64,3072]{1,0:T(8,128)(2,1)}, u32[]{:S(2)}, u32[]{:S(2)}) collective-permute-start(bf16[64,3072]{1,0:T(8,128)(2,1)S(1)} %collective-permute-done.3.refs_4_), channel_id=1, source_target_pairs={{0,2},{1,3},{2,0},{3,1},{4,6},{5,7},{6,4},{7,5},{8,10},{9,11},{10,... | collective-permute-start | bytes 1179656 | tf_op jit(solution)/shard_map/ppermute | solution.py:354
  59.5 25.2 %collective-permute-start.4 = (bf16[64,3072]{1,0:T(8,128)(2,1)S(1)}, bf16[64,3072]{1,0:T(8,128)(2,1)}, u32[]{:S(2)}, u32[]{:S(2)}) collective-permute-start(bf16[64,3072]{1,0:T(8,128)(2,1)S(1)} %collective-permute-done.3.refs_4_), channel_id=1, source_target_pairs={{0,1},{1,0},{2,3},{3,2},{4,5},{5,4},{6,7},{7,6},{8,9},{9,8},{10,11... | collective-permute-start | bytes 1179656 | tf_op jit(solution)/shard_map/ppermute | solution.py:354
  67.7 14.3 %copy-start = (bf16[1,640,3072]{2,1,0:T(8,128)(2,1)S(1)}, bf16[1,640,3072]{2,1,0:T(8,128)(2,1)}, u32[]{:S(2)}) copy-start(bf16[1,640,3072]{2,1,0:T(8,128)(2,1)} %param.10) | copy-start | bytes 11796484
  82.0 2.6 %copy-start.9 = (bf16[512,640]{1,0:T(8,128)(2,1)}, bf16[512,640]{1,0:T(8,128)(2,1)S(1)}, u32[]{:S(2)}) copy-start(bf16[512,640]{1,0:T(8,128)(2,1)S(1)} %get-tuple-element.54.refs_0_) | copy-start | bytes 1966084
  82.0 2.6 %copy-start.13 = (bf16[512,128]{1,0:T(8,128)(2,1)}, bf16[512,128]{1,0:T(8,128)(2,1)S(1)}, u32[]{:S(2)}) copy-start(bf16[512,128]{1,0:T(8,128)(2,1)S(1)} %get-tuple-element.57) | copy-start | bytes 393220
  82.0 2.6 %copy-start.16 = (f32[512,512]{1,0:T(8,128)}, f32[512,512]{1,0:T(8,128)S(1)}, u32[]{:S(2)}) copy-start(f32[512,512]{1,0:T(8,128)S(1)} %get-tuple-element.34.left_ref) | copy-start | bytes 3145732
  89.1 1.9 copy-start.1
  90.9 1.7 copy-start.14
  92.6 45.5 %all-to-all-start.2 = ((bf16[8,64,3712]{2,1,0:T(8,128)(2,1)}), bf16[8,64,3712]{2,1,0:T(8,128)(2,1)}, u32[]{:S(2)}, u32[]{:S(2)}) async-start(bf16[8,64,3712]{2,1,0:T(8,128)(2,1)} %copy-done.1), calls=%async_computation.2 | async-start | bytes 7602176 | tf_op jit(solution)/shard_map/all_to_all | solution.py:496
  99.5 1.9 copy-start.15
  101.4 1.2 copy-start.17
  102.6 35.6 %copy-start.12 = (f32[1,5120]{1,0:T(1,128)S(1)}, f32[1,5120]{1,0:T(1,128)}, u32[]{:S(2)}) copy-start(f32[1,5120]{1,0:T(1,128)} %gain_ref.3) | copy-start | bytes 61444
  138.2 1.1 copy-start.3
  139.3 1.1 copy-start.5
  140.4 1.1 copy-start.8
  145.7 46.9 %collective-permute-start.7 = (bf16[1,64,5120]{2,1,0:T(8,128)(2,1)}, bf16[1,64,5120]{2,1,0:T(8,128)(2,1)}, u32[]{:S(2)}, u32[]{:S(2)}) collective-permute-start(bf16[1,64,5120]{2,1,0:T(8,128)(2,1)} %get-tuple-element.49), channel_id=1, source_target_pairs={{0,8},{8,16},{16,24},{24,32},{32,40},{40,48},{48,56},{56,64},{64,7... | collective-permute-start | bytes 1966088 | tf_op jit(solution)/shard_map/ppermute | solution.py:28
  147.9 44.7 %collective-permute-start.8 = (bf16[1,64,5120]{2,1,0:T(8,128)(2,1)}, bf16[1,64,5120]{2,1,0:T(8,128)(2,1)}, u32[]{:S(2)}, u32[]{:S(2)}) collective-permute-start(bf16[1,64,5120]{2,1,0:T(8,128)(2,1)} %get-tuple-element.50), channel_id=1, source_target_pairs={{8,0},{16,8},{24,16},{32,24},{40,32},{48,40},{56,48},{64,56},{72,6... | collective-permute-start | bytes 1966088 | tf_op jit(solution)/shard_map/ppermute | solution.py:28
  149.2 33.3 %collective-permute-start.9 = (bf16[512,512]{1,0:T(8,128)(2,1)}, bf16[512,512]{1,0:T(8,128)(2,1)}, u32[]{:S(2)}, u32[]{:S(2)}) collective-permute-start(bf16[512,512]{1,0:T(8,128)(2,1)} %get-tuple-element.55), channel_id=1, source_target_pairs={{0,1},{4,3},{7,6},{8,9},{12,11},{15,14},{16,17},{20,19},{23,22},{2... | collective-permute-start | bytes 1572872 | tf_op jit(solution)/shard_map/ppermute | solution.py:499
  150.6 31.8 %collective-permute-start.10 = (bf16[512,256]{1,0:T(8,128)(2,1)}, bf16[512,256]{1,0:T(8,128)(2,1)S(1)}, u32[]{:S(2)}, u32[]{:S(2)}) collective-permute-start(bf16[512,256]{1,0:T(8,128)(2,1)} %get-tuple-element.56), channel_id=1, source_target_pairs={{2,1},{5,6},{10,9},{13,14},{18,17},{21,22},{26,25},{29,30},{34,33}... | collective-permute-start | bytes 786440 | tf_op jit(solution)/shard_map/ppermute | solution.py:499
  155.1 37.4 %all-to-all-start.1 = ((f32[256,1,128]{2,1,0:T(1,128)}), f32[256,1,128]{2,1,0:T(1,128)S(1)}, u32[]{:S(2)}, u32[]{:S(2)}) async-start(f32[256,1,128]{2,1,0:T(1,128)} %broadcast_in_dim.11), calls=%async_computation.1 | async-start | bytes 262144 | tf_op jit(solution)/shard_map/all_to_all | solution.py:514
  176.1 6.4 %collective-permute-start.11 = (bf16[512,128]{1,0:T(8,128)(2,1)}, bf16[512,128]{1,0:T(8,128)(2,1)S(1)}, u32[]{:S(2)}, u32[]{:S(2)}) collective-permute-start(bf16[512,128]{1,0:T(8,128)(2,1)} %copy-done.13), channel_id=1, source_target_pairs={{2,3},{5,4},{10,11},{13,12},{18,19},{21,20},{26,27},{29,28},{34,35... | collective-permute-start | bytes 393224 | tf_op jit(solution)/shard_map/ppermute | solution.py:499
  182.5 1.1 copy-start.10
  185.0 0.8 copy-start.6
  192.6 1.1 copy-start.7
  (1 other events, 0.7 us)

commit v2 on v1

--- a/solution.py
+++ b/solution.py
@@ -230,8 +230,6 @@
 
 
 HARDEST = 2e4
-ACT_MIB = 14
-GRAD_MIB = 16
 
 
 def solver_scratch(count):
@@ -310,44 +308,53 @@
     term_ref[...] = jnp.sum(product, axis=1, keepdims=True)
 
 
-VMEM = pl.BlockSpec(memory_space=pltpu.VMEM)
 SMEM = pl.BlockSpec(memory_space=pltpu.SMEM)
+
+
+def shape(*dims, dtype=BF16):
+    return jax.ShapeDtypeStruct(dims, dtype)
+
+
+def whole_block(value):
+    return pl.BlockSpec(value.shape, lambda i: (0,) * len(value.shape))
+
+
+def cost(flops, moved):
+    return pl.CostEstimate(flops=flops, bytes_accessed=moved, transcendentals=0)
+
+
+def params():
+    return pltpu.CompilerParams(vmem_limit_bytes=56 * 2**20)
+
+
+def run(kernel, name, outs, scalars, arrays, flops, scratch=()):
+    moved = sum(value.size * value.dtype.itemsize for value in (*arrays, *outs))
+    return pl.pallas_call(
+        kernel,
+        grid=(1,),
+        out_shape=tuple(outs),
+        in_specs=[SMEM] * len(scalars) + [whole_block(value) for value in arrays],
+        out_specs=tuple(whole_block(value) for value in outs),
+        scratch_shapes=list(scratch),
+        compiler_params=params(),
+        cost_estimate=cost(flops, moved),
+        name=name,
+    )(*scalars, *arrays)
 
 
 def solve_act(damping, me, rows):
     count = rows.shape[0]
-    return pl.pallas_call(
-        act_kernel,
-        out_shape=(jax.ShapeDtypeStruct((count, count), F32),)
-        + tuple(jax.ShapeDtypeStruct((count, units * UNIT), BF16) for units, _, _ in MOVES),
-        in_specs=[SMEM, SMEM, VMEM],
-        out_specs=(VMEM,) * (len(MOVES) + 1),
-        scratch_shapes=[pltpu.VMEM((count, BLOCK), BF16)] + solver_scratch(count),
-        compiler_params=pltpu.CompilerParams(vmem_limit_bytes=ACT_MIB * 2**20),
-        cost_estimate=pl.CostEstimate(
-            flops=16 * 10**9, bytes_accessed=4 * 2**20, transcendentals=0
-        ),
-        name="solve_act",
-    )(damping, me, rows)
+    outs = [shape(count, count, dtype=F32)]
+    outs += [shape(count, units * UNIT) for units, _, _ in MOVES]
+    scratch = [pltpu.VMEM((count, BLOCK), BF16)] + solver_scratch(count)
+    return run(act_kernel, "solve_act", outs, (damping, me), (rows,), 16 * 10**9, scratch)
 
 
 def solve_grad(damping, rows, left):
     count, width = rows.shape
-    return pl.pallas_call(
-        grad_kernel,
-        out_shape=(
-            jax.ShapeDtypeStruct((count, width), BF16),
-            jax.ShapeDtypeStruct((1, 1), F32),
-        ),
-        in_specs=[SMEM, VMEM, VMEM],
-        out_specs=(VMEM, VMEM),
-        scratch_shapes=[pltpu.VMEM((count, count), F32)] + solver_scratch(count),
-        compiler_params=pltpu.CompilerParams(vmem_limit_bytes=GRAD_MIB * 2**20),
-        cost_estimate=pl.CostEstimate(
-            flops=45 * 10**9, bytes_accessed=8 * 2**20, transcendentals=0
-        ),
-        name="solve_grad",
-    )(damping, rows, left)
+    outs = [shape(count, width), shape(1, 1, dtype=F32)]
+    scratch = [pltpu.VMEM((count, count), F32)] + solver_scratch(count)
+    return run(grad_kernel, "solve_grad", outs, (damping,), (rows, left), 45 * 10**9, scratch)
 
 
 def swap(value, offset):
@@ -381,8 +388,9 @@
     groups, tokens, _ = out_ref.shape
     part, width = weight_ref.shape
     for offset, piece in enumerate(pieces):
-        start = pl.multiple_of((me ^ offset) * tokens, tokens)
-        gathered[pl.ds(start, tokens), :] = piece[...]
+        for half in range(2):
+            start = pl.multiple_of((me ^ offset ^ (half * groups // 2)) * tokens, tokens)
+            gathered[pl.ds(start, tokens), :] = piece[half * tokens : (half + 1) * tokens, :]
     for device in range(groups):
         out_ref[device, :, :width] = forward_ref[device * tokens : (device + 1) * tokens, :]
     backward = dot(gathered[...], weight_ref[...], (1, 1), None)
@@ -422,23 +430,28 @@
     by_rows(fwd_ref.shape[0], 16, some)
 
 
-def update_kernel(entries, terms_ref, turned_ref, grad_ref, out_ref):
+def update_kernel(
+    entries, terms_ref, turned_ref, grad_ref, fwd_ref, back_ref, out_ref, next_ref, last_ref, sems
+):
+    copies = (
+        pltpu.make_async_copy(fwd_ref, next_ref, sems.at[0]),
+        pltpu.make_async_copy(back_ref, last_ref, sems.at[1]),
+    )
+
+    @pl.when(pl.program_id(0) == 0)
+    def _():
+        for copy in copies:
+            copy.start()
+
     terms = terms_ref[...]
     total = jnp.sum(jnp.sum(terms, axis=0, keepdims=True)[:, :1], axis=1, keepdims=True)
     ratio = jnp.sqrt(entries / total)
     out_ref[...] = (ratio * dot(turned_ref[...], grad_ref[...], precision=None)).astype(BF16)
 
-
-def shape(*dims, dtype=BF16):
-    return jax.ShapeDtypeStruct(dims, dtype)
-
-
-def cost(flops, moved):
-    return pl.CostEstimate(flops=flops, bytes_accessed=moved, transcendentals=0)
-
-
-def params(mib):
-    return pltpu.CompilerParams(vmem_limit_bytes=mib * 2**20)
+    @pl.when(pl.program_id(0) == pl.num_programs(0) - 1)
+    def _():
+        for copy in copies:
+            copy.wait()
 
 
 def per_device(x_fwd, x_bwd, grad_in, gain, weight, damping):
@@ -455,59 +468,48 @@
     damp_value = damping.reshape(1, 1)
 
     upstream = grad[:, :out_width]
-    other = swap(upstream, groups // 2)
-    pieces = [upstream] + [swap(upstream, offset) for offset in range(1, groups // 2)]
-    fwd_late, bwd_late, other = lax.optimization_barrier((fwd, bwd, other))
-    pieces += [other] + [swap(other, offset) for offset in range(1, groups // 2)]
-
-    sent = pl.pallas_call(
+    half = groups // 2
+    other = swap(upstream, half)
+    (sent,) = run(
         normalize_kernel,
-        out_shape=shape(groups, tokens, BLOCK + own_rows),
-        in_specs=[VMEM] * 3,
-        out_specs=VMEM,
-        compiler_params=params(8),
-        cost_estimate=cost(10**7, 3 * 10**6),
-        name="normalize",
-    )(fwd_late, bwd_late, gain)
+        "normalize",
+        [shape(groups, tokens, BLOCK + own_rows)],
+        (),
+        (fwd, bwd, gain),
+        10**7,
+    )
+    sent, other = lax.optimization_barrier((sent, other))
+    pair = jnp.concatenate([upstream, other], axis=0)
+    pieces = [pair] + [swap(pair, offset) for offset in range(1, half)]
     rows = lax.all_to_all(sent, "dp", 0, 0, tiled=True).reshape(group, BLOCK + own_rows)
 
     left, *moves = solve_act(damp_value, me_value, rows)
-
-    forward = pl.pallas_call(
-        forward_kernel,
-        out_shape=shape(group, out_width),
-        in_specs=[VMEM] * 2,
-        out_specs=VMEM,
-        compiler_params=params(12),
-        cost_estimate=cost(2 * 10**9, 8 * 10**6),
-        name="forward",
-    )(rows, local_w)
-
+    (forward,) = run(
+        forward_kernel, "forward", [shape(group, out_width)], (), (rows, local_w), 2 * 10**9
+    )
     ready = lax.optimization_barrier((me_value, *pieces, forward, left))
-    group_grad, products = pl.pallas_call(
+    group_grad, products = run(
         product_kernel,
-        out_shape=(shape(group, out_width), shape(groups, tokens, out_width + own_rows)),
-        in_specs=[SMEM] + [VMEM] * (len(pieces) + 2),
-        out_specs=(VMEM,) * 2,
-        compiler_params=params(16),
-        cost_estimate=cost(4 * 10**9, 10**7),
-        name="products",
-    )(*ready[:-1], local_w)
+        "products",
+        [shape(group, out_width), shape(groups, tokens, out_width + own_rows)],
+        ready[:1],
+        (*ready[1:-1], local_w),
+        2 * 10**9,
+    )
     parts = lax.all_to_all(products, "dp", 0, 0, tiled=True)
 
     moves = moves[:1] + [
         lax.ppermute(piece, "dp", pairs) for piece, pairs in zip(moves[1:], PAIRS[1:])
     ]
-    turned = pl.pallas_call(
+    (turned,) = run(
         assemble_kernel,
-        out_shape=shape(own_rows, group),
-        in_specs=[SMEM] + [VMEM] * len(MOVES),
-        out_specs=VMEM,
-        scratch_shapes=[pltpu.VMEM((group, (2 * WINDOW + 2) * UNIT), BF16)],
-        compiler_params=params(16),
-        cost_estimate=cost(10**7, 3 * 10**6),
-        name="assemble",
-    )(me_value, *moves)
+        "assemble",
+        [shape(own_rows, group)],
+        (me_value,),
+        moves,
+        10**7,
+        [pltpu.VMEM((group, (2 * WINDOW + 2) * UNIT), BF16)],
+    )
 
     grad_tilde, term = solve_grad(damp_value, group_grad, left)
     devices = lax.axis_size("section") * groups
@@ -516,35 +518,38 @@
     )
 
     parts, _ = lax.optimization_barrier((parts, term))
-    out_f, out_b = pl.pallas_call(
+    out_f, out_b = run(
         finish_kernel,
-        out_shape=(shape(1, tokens, width),) * 2,
-        in_specs=[VMEM] * 5,
-        out_specs=(VMEM,) * 2,
-        compiler_params=params(12),
-        cost_estimate=cost(10**7, 8 * 10**6),
-        name="finish",
-    )(parts, fwd, bwd, grad, gain)
+        "finish",
+        [shape(1, tokens, width)] * 2,
+        (),
+        (parts, fwd, bwd, grad, gain),
+        10**7,
+    )
     next_fwd = from_behind(out_f, "section", 1)
     next_grad = from_behind(out_b, "section", -1)
     terms, next_fwd, next_grad = lax.optimization_barrier((terms, next_fwd, next_grad))
 
     columns = 512
     entries = float(lax.axis_size("section") * width * out_width)
-    update = pl.pallas_call(
+    keep = pl.BlockSpec(memory_space=pl.ANY)
+    update, next_fwd, next_grad = pl.pallas_call(
         lambda *refs: update_kernel(entries, *refs),
         grid=(out_width // columns,),
-        out_shape=shape(own_rows, out_width),
+        out_shape=(shape(own_rows, out_width),) + (shape(1, tokens, width),) * 2,
         in_specs=[
             pl.BlockSpec((devices, 128), lambda i: (0, 0)),
             pl.BlockSpec((own_rows, group), lambda i: (0, 0)),
             pl.BlockSpec((group, columns), lambda i: (0, i)),
+            keep,
+            keep,
         ],
-        out_specs=pl.BlockSpec((own_rows, columns), lambda i: (0, i)),
-        compiler_params=params(12),
+        out_specs=(pl.BlockSpec((own_rows, columns), lambda i: (0, i)), keep, keep),
+        scratch_shapes=[pltpu.SemaphoreType.DMA((2,))],
+        compiler_params=params(),
         cost_estimate=cost(2 * 10**9, 8 * 10**6),
         name="update",
-    )(terms, turned, grad_tilde)
+    )(terms, turned, grad_tilde, next_fwd, next_grad)
     return (next_fwd, next_grad, update[None])
 
 

time: 203 us -> 227 us (1.12)
  Pallas kernels: 69.2 us -> 123 us
  local copies, waits for them, and re-layouts: 22.1 us -> 6.57 us
  waiting for transfers between devices: 50.2 us -> 43 us
  starting transfers between devices: 59.3 us -> 52.1 us
    pallas_call x1, Pallas kernels: 4.7 us -> 43 us  [per_device(): pl.pallas_call(lambda *refs: update_kernel(entries, *refs), grid=(out_wid...]
    ppermute x7 -> x4, waiting for transfers between devices: 39.5 us -> 15.7 us  [swap(): return lax.ppermute(value, 'dp', [(i, i ^ offset) for i in range(8)])]
    all_to_all x1, waiting for transfers between devices: 0.01 us -> 15.7 us  [per_device(): lax.all_to_all(sent, 'dp', 0, 0, tiled=True)]
    unnamed x38 -> x24, local copies, waits for them, and re-layouts: 19.8 us -> 4.14 us
    pallas_call x7, Pallas kernels: 64.4 us -> 80 us  [run(): pl.pallas_call(kernel, grid=(1,), out_shape=tuple(outs), in_specs=[SMEM]...]
    ppermute x7 -> x4, starting transfers between devices: 15.2 us -> 4.38 us  [swap(): return lax.ppermute(value, 'dp', [(i, i ^ offset) for i in range(8)])]
    all_to_all x1, starting transfers between devices: 6.85 us -> 11.6 us  [per_device(): parts = lax.all_to_all(products, 'dp', 0, 0, tiled=True)]
  transfers between devices with their start and end apart: 15 -> 12, of which waited for: 4 -> 5; matrix products, arithmetic and copies ran while one was open for 1% -> 1% of each run, Pallas kernels for 27% -> 29%
where the time goes in v2:
time: 227 us; the launch traced here: 226 us
  Pallas kernels  123 us (54%)
  starting transfers between devices  52.1 us (23%)
  waiting for transfers between devices  43 us (19%)
  local copies, waits for them, and re-layouts  6.57 us (3%)
    pallas_call x7, Pallas kernels, run(): pl.pallas_call(kernel, grid=(1,), out_shape=tuple(outs), in_specs=[SMEM]...  80 us
    pallas_call x1, Pallas kernels, per_device(): pl.pallas_call(lambda *refs: update_kernel(entries, *refs), grid=(out_wid...  43 us
    all_to_all x1, starting transfers between devices, per_device(): lax.all_to_all(jnp.broadcast_to(term, (devices, 128)), ('section', 'dp'),...  20.6 us
    ppermute x4, waiting for transfers between devices, swap(): return lax.ppermute(value, 'dp', [(i, i ^ offset) for i in range(8)])  15.7 us
    all_to_all x1, waiting for transfers between devices, per_device(): lax.all_to_all(sent, 'dp', 0, 0, tiled=True)  15.7 us
    all_to_all x1, starting transfers between devices, per_device(): parts = lax.all_to_all(products, 'dp', 0, 0, tiled=True)  11.6 us
    all_to_all x1, waiting for transfers between devices, per_device(): lax.all_to_all(jnp.broadcast_to(term, (devices, 128)), ('section', 'dp'),...  7.85 us
    ppermute x3, starting transfers between devices, per_device(): lax.ppermute(piece, 'dp', pairs)  6.55 us
  transfers between devices with their start and end apart: 12, of which 5 were waited for; matrix products, arithmetic and copies ran while one was open for 1% of the time, Pallas kernels for 29%

profile of v2, /device:TPU:40, one launch (start us, length us, event | category | flops | bytes accessed | tf_op | source)
XLA Modules:
  0.0 226.3 jit_solution(496323569717037382)
XLA Ops:
  0.6 1.0 slice.4
  1.9 3.2 %normalize.1 = bf16[8,64,1664]{2,1,0:T(8,128)(2,1)} custom-call(bf16[64,5120]{1,0:T(8,128)(2,1)} %bitcast.16, bf16[64,5120]{1,0:T(8,128)(2,1)} %bitcast.18, f32[1,5120]{1,0:T(1,128)} %gain_ref.3), custom_call_target="tpu_custom_call" | custom-call | flops 10000000 | bytes 3035136 | tf_op jit(solution)/shard_map/normalize/pallas_call | solution.py:332
  5.1 7.5 %collective-permute-done = bf16[64,3072]{1,0:T(8,128)(2,1)S(1)} collective-permute-done((bf16[64,3072]{1,0:T(8,128)(2,1)S(1)}, bf16[64,3072]{1,0:T(8,128)(2,1)S(1)}, u32[]{:S(2)}, u32[]{:S(2)}) %collective-permute-start) | collective-permute-done | bytes 393248 | tf_op jit(solution)/shard_map/ppermute | solution.py:361
  12.6 5.8 %all-to-all-start = ((bf16[8,64,1664]{2,1,0:T(8,128)(2,1)}), bf16[8,64,1664]{2,1,0:T(8,128)(2,1)S(1)}, u32[]{:S(2)}, u32[]{:S(2)}) async-start(bf16[8,64,1664]{2,1,0:T(8,128)(2,1)} %normalize.1), calls=%async_computation | async-start | bytes 3407872 | tf_op jit(solution)/shard_map/all_to_all | solution.py:484
  19.1 1.6 collective-permute-start.3
  20.7 1.2 collective-permute-start.2
  21.9 1.5 collective-permute-start.1
  23.3 15.7 %all-to-all-done = bf16[8,64,1664]{2,1,0:T(8,128)(2,1)S(1)} async-done(((bf16[8,64,1664]{2,1,0:T(8,128)(2,1)}), bf16[8,64,1664]{2,1,0:T(8,128)(2,1)S(1)}, u32[]{:S(2)}, u32[]{:S(2)}) %all-to-all-start) | async-done | bytes 1703968 | tf_op jit(solution)/shard_map/all_to_all | solution.py:484
  39.0 1.2 copy-done
  40.2 16.0 %solve_act.1 = (f32[512,512]{1,0:T(8,128)}, bf16[512,640]{1,0:T(8,128)(2,1)}, bf16[512,512]{1,0:T(8,128)(2,1)}, bf16[512,256]{1,0:T(8,128)(2,1)}, bf16[512,128]{1,0:T(8,128)(2,1)}) custom-call(f32[1,1]{1,0:T(1,128)} %bitcast.10.damping_ref, s32[1,1]{1,0:T(1,128)} %bitcast.1.me_ref, bf16[512,1664]{1,0:T(8,128)(2,1)} %bitcast.14), custom_call_target="tpu_custom_call" | custom-call | flops 16000000000 | bytes 4325376 | tf_op jit(solution)/shard_map/solve_act/pallas_call | solution.py:332
  56.2 6.9 %forward.1.refs_4_ = bf16[512,3072]{1,0:T(8,128)(2,1)} custom-call(bf16[512,1664]{1,0:T(8,128)(2,1)} %bitcast.15, bf16[640,3072]{1,0:T(8,128)(2,1)} %bitcast.12), custom_call_target="tpu_custom_call" | custom-call | flops 2000000000 | bytes 8781824 | tf_op jit(solution)/shard_map/forward/pallas_call | solution.py:332
  63.1 8.2 %collective-permute-done.3.refs_3_ = bf16[128,3072]{1,0:T(8,128)(2,1)S(1)} collective-permute-done((bf16[128,3072]{1,0:T(8,128)(2,1)S(1)}, bf16[128,3072]{1,0:T(8,128)(2,1)S(1)}, u32[]{:S(2)}, u32[]{:S(2)}) %collective-permute-start.3) | collective-permute-done | bytes 786464 | tf_op jit(solution)/shard_map/ppermute | solution.py:361
  71.3 0.9 copy-done.2
  72.2 8.8 %products.1 = (bf16[512,3072]{1,0:T(8,128)(2,1)}, bf16[8,64,3712]{2,1,0:T(8,128)(2,1)}) custom-call(s32[1,1]{1,0:T(1,128)} %bitcast.1.me_ref, bf16[128,3072]{1,0:T(8,128)(2,1)} %copy-done.1, bf16[128,3072]{1,0:T(8,128)(2,1)} %collective-permute-done.1.refs_1_, bf16[128,3072]{1,0:T(8,128)(2,1)} %collective-permute-done.2.refs_2_, ...), custom_call_target="tpu_custom_call" | custom-call | flops 2000000000 | bytes 17170432 | tf_op jit(solution)/shard_map/products/pallas_call | solution.py:332
  81.0 11.6 %all-to-all-start.2 = ((bf16[8,64,3712]{2,1,0:T(8,128)(2,1)}), bf16[8,64,3712]{2,1,0:T(8,128)(2,1)}, u32[]{:S(2)}, u32[]{:S(2)}) async-start(bf16[8,64,3712]{2,1,0:T(8,128)(2,1)} %get-tuple-element.40), calls=%async_computation.2 | async-start | bytes 7602176 | tf_op jit(solution)/shard_map/all_to_all | solution.py:499
  92.6 37.8 %solve_grad.1 = (bf16[512,3072]{1,0:T(8,128)(2,1)}, f32[1,1]{1,0:T(1,128)}) custom-call(f32[1,1]{1,0:T(1,128)} %bitcast.11.damping_ref, bf16[512,3072]{1,0:T(8,128)(2,1)} %get-tuple-element.38.rows_ref, f32[512,512]{1,0:T(8,128)} %get-tuple-element.31.left_ref), custom_call_target="tpu_custom_call" | custom-call | flops 44999999488 | bytes 7340036 | tf_op jit(solution)/shard_map/solve_grad/pallas_call | solution.py:332
  130.5 4.8 %finish.1 = (bf16[1,64,5120]{2,1,0:T(8,128)(2,1)}, bf16[1,64,5120]{2,1,0:T(8,128)(2,1)}) custom-call(bf16[8,64,3712]{2,1,0:T(8,128)(2,1)} %all-to-all-done.2.parts_ref, bf16[64,5120]{1,0:T(8,128)(2,1)} %bitcast.17, bf16[64,5120]{1,0:T(8,128)(2,1)} %bitcast.19, bf16[64,5120]{1,0:T(8,128)(2,1)} %bitcast.21, f32[1,5120]{1,0:T(1,128)} %gain_ref.3), custom_call_target="tpu_custom_call" | custom-call | flops 10000000 | bytes 7098368 | tf_op jit(solution)/shard_map/finish/pallas_call | solution.py:332
  135.3 1.8 collective-permute-start.4
  137.1 1.3 collective-permute-start.5
  138.4 0.7 collective-permute-start.6
  139.1 3.5 %collective-permute-start.7 = (bf16[512,256]{1,0:T(8,128)(2,1)S(1)}, bf16[512,256]{1,0:T(8,128)(2,1)S(1)}, u32[]{:S(2)}, u32[]{:S(2)}) collective-permute-start(bf16[512,256]{1,0:T(8,128)(2,1)S(1)} %copy-done.10), channel_id=1, source_target_pairs={{2,1},{5,6},{10,9},{13,14},{18,17},{21,22},{26,25},{29,30},{34,33}... | collective-permute-start | bytes 786440 | tf_op jit(solution)/shard_map/ppermute | solution.py:502
  142.6 1.4 broadcast_in_dim.11
  144.0 20.6 %all-to-all-start.1 = ((f32[256,1,128]{2,1,0:T(1,128)}), f32[256,1,128]{2,1,0:T(1,128)S(1)}, u32[]{:S(2)}, u32[]{:S(2)}) async-start(f32[256,1,128]{2,1,0:T(1,128)} %broadcast_in_dim.11), calls=%async_computation.1 | async-start | bytes 262144 | tf_op jit(solution)/shard_map/all_to_all | solution.py:516
  164.6 2.4 %collective-permute-start.8 = (bf16[512,128]{1,0:T(8,128)(2,1)S(1)}, bf16[512,128]{1,0:T(8,128)(2,1)S(1)}, u32[]{:S(2)}, u32[]{:S(2)}) collective-permute-start(bf16[512,128]{1,0:T(8,128)(2,1)S(1)} %copy-done.11), channel_id=1, source_target_pairs={{2,3},{5,4},{10,11},{13,12},{18,19},{21,20},{26,27},{29,28},{34,35... | collective-permute-start | bytes 393224 | tf_op jit(solution)/shard_map/ppermute | solution.py:502
  167.0 3.6 %collective-permute-done.8.refs_3_ = bf16[512,128]{1,0:T(8,128)(2,1)S(1)} collective-permute-done((bf16[512,128]{1,0:T(8,128)(2,1)S(1)}, bf16[512,128]{1,0:T(8,128)(2,1)S(1)}, u32[]{:S(2)}, u32[]{:S(2)}) %collective-permute-start.8) | collective-permute-done | bytes 131104 | tf_op jit(solution)/shard_map/ppermute | solution.py:502
  170.7 0.6 copy-done.5
  171.4 0.2 copy-done.3
  171.6 2.6 %assemble.1.refs_1_ = bf16[640,512]{1,0:T(8,128)(2,1)} custom-call(s32[1,1]{1,0:T(1,128)} %bitcast.1.me_ref, bf16[512,640]{1,0:T(8,128)(2,1)} %get-tuple-element.45.refs_0_, bf16[512,512]{1,0:T(8,128)(2,1)} %copy-done.3, bf16[512,256]{1,0:T(8,128)(2,1)} %copy-done.4, bf16[512,128]{1,0:T(8,128)(2,1)} %copy-done.5), custom_call_target="tpu_custom_call" | custom-call | flops 10000000 | bytes 2228224 | tf_op jit(solution)/shard_map/assemble/pallas_call | solution.py:332
  174.2 7.9 %all-to-all-done.1 = f32[256,1,128]{2,1,0:T(1,128)S(1)} async-done(((f32[256,1,128]{2,1,0:T(1,128)}), f32[256,1,128]{2,1,0:T(1,128)S(1)}, u32[]{:S(2)}, u32[]{:S(2)}) %all-to-all-start.1) | async-done | bytes 131104 | tf_op jit(solution)/shard_map/all_to_all | solution.py:516
  182.1 0.6 copy-done.6
  182.7 0.3 copy-done.7
  183.2 43.0 %update.1 = (bf16[640,3072]{1,0:T(8,128)(2,1)}, bf16[1,64,5120]{2,1,0:T(8,128)(2,1)}, bf16[1,64,5120]{2,1,0:T(8,128)(2,1)}) custom-call(f32[256,128]{1,0:T(8,128)} %bitcast.22, bf16[640,512]{1,0:T(8,128)(2,1)} %assemble.1.refs_1_, bf16[512,3072]{1,0:T(8,128)(2,1)} %get-tuple-element.49.refs_2_, bf16[1,64,5120]{2,1,0:T(8,128)(2,1)} %copy-done.7, ...), custom_call_target="tpu_custom_call" | custom-call | flops 2000000000 | bytes 8000000 | tf_op jit(solution)/shard_map/update/pallas_call | solution.py:536
  (27 shorter events, 0.6 us)
Async XLA Ops:
  1.7 10.9 %collective-permute-start = (bf16[64,3072]{1,0:T(8,128)(2,1)S(1)}, bf16[64,3072]{1,0:T(8,128)(2,1)S(1)}, u32[]{:S(2)}, u32[]{:S(2)}) collective-permute-start(bf16[64,3072]{1,0:T(8,128)(2,1)S(1)} %slice.4), channel_id=1, source_target_pairs={{0,4},{1,5},{2,6},{3,7},{4,0},{5,1},{6,2},{7,3},{8,12},{9,13},{10,... | collective-permute-start | bytes 1179656 | tf_op jit(solution)/shard_map/ppermute | solution.py:361
  12.6 26.4 %all-to-all-start = ((bf16[8,64,1664]{2,1,0:T(8,128)(2,1)}), bf16[8,64,1664]{2,1,0:T(8,128)(2,1)S(1)}, u32[]{:S(2)}, u32[]{:S(2)}) async-start(bf16[8,64,1664]{2,1,0:T(8,128)(2,1)} %normalize.1), calls=%async_computation | async-start | bytes 3407872 | tf_op jit(solution)/shard_map/all_to_all | solution.py:484
  19.1 37.1 %copy-start.1 = (bf16[128,3072]{1,0:T(8,128)(2,1)}, bf16[128,3072]{1,0:T(8,128)(2,1)S(1)}, u32[]{:S(2)}) copy-start(bf16[128,3072]{1,0:T(8,128)(2,1)S(1)} %pad_maximum_fusion.refs_0_) | copy-start | bytes 2359300
  19.1 52.2 %collective-permute-start.3 = (bf16[128,3072]{1,0:T(8,128)(2,1)S(1)}, bf16[128,3072]{1,0:T(8,128)(2,1)S(1)}, u32[]{:S(2)}, u32[]{:S(2)}) collective-permute-start(bf16[128,3072]{1,0:T(8,128)(2,1)S(1)} %pad_maximum_fusion.refs_0_), channel_id=1, source_target_pairs={{0,3},{1,2},{2,1},{3,0},{4,7},{5,6},{6,5},{7,4},{8,11},{9,10},{10,... | collective-permute-start | bytes 2359304 | tf_op jit(solution)/shard_map/ppermute | solution.py:361
  20.7 50.6 %collective-permute-start.2 = (bf16[128,3072]{1,0:T(8,128)(2,1)S(1)}, bf16[128,3072]{1,0:T(8,128)(2,1)}, u32[]{:S(2)}, u32[]{:S(2)}) collective-permute-start(bf16[128,3072]{1,0:T(8,128)(2,1)S(1)} %pad_maximum_fusion.refs_0_), channel_id=1, source_target_pairs={{0,2},{1,3},{2,0},{3,1},{4,6},{5,7},{6,4},{7,5},{8,10},{9,11},{10,... | collective-permute-start | bytes 2359304 | tf_op jit(solution)/shard_map/ppermute | solution.py:361
  21.9 49.5 %collective-permute-start.1 = (bf16[128,3072]{1,0:T(8,128)(2,1)S(1)}, bf16[128,3072]{1,0:T(8,128)(2,1)}, u32[]{:S(2)}, u32[]{:S(2)}) collective-permute-start(bf16[128,3072]{1,0:T(8,128)(2,1)S(1)} %pad_maximum_fusion.refs_0_), channel_id=1, source_target_pairs={{0,1},{1,0},{2,3},{3,2},{4,5},{5,4},{6,7},{7,6},{8,9},{9,8},{10,11... | collective-permute-start | bytes 2359304 | tf_op jit(solution)/shard_map/ppermute | solution.py:361
  39.0 1.2 copy-start
  71.3 0.9 copy-start.2
  81.0 49.5 %all-to-all-start.2 = ((bf16[8,64,3712]{2,1,0:T(8,128)(2,1)}), bf16[8,64,3712]{2,1,0:T(8,128)(2,1)}, u32[]{:S(2)}, u32[]{:S(2)}) async-start(bf16[8,64,3712]{2,1,0:T(8,128)(2,1)} %get-tuple-element.40), calls=%async_computation.2 | async-start | bytes 7602176 | tf_op jit(solution)/shard_map/all_to_all | solution.py:499
  130.4 8.0 %copy-start.9 = (bf16[512,512]{1,0:T(8,128)(2,1)S(1)}, bf16[512,512]{1,0:T(8,128)(2,1)}, u32[]{:S(2)}) copy-start(bf16[512,512]{1,0:T(8,128)(2,1)} %get-tuple-element.46) | copy-start | bytes 1572868
  130.5 8.7 %copy-start.10 = (bf16[512,256]{1,0:T(8,128)(2,1)S(1)}, bf16[512,256]{1,0:T(8,128)(2,1)}, u32[]{:S(2)}) copy-start(bf16[512,256]{1,0:T(8,128)(2,1)} %get-tuple-element.47) | copy-start | bytes 786436
  130.5 34.1 %copy-start.11 = (bf16[512,128]{1,0:T(8,128)(2,1)S(1)}, bf16[512,128]{1,0:T(8,128)(2,1)}, u32[]{:S(2)}) copy-start(bf16[512,128]{1,0:T(8,128)(2,1)} %get-tuple-element.48) | copy-start | bytes 393220
  135.3 46.8 %collective-permute-start.4 = (bf16[1,64,5120]{2,1,0:T(8,128)(2,1)}, bf16[1,64,5120]{2,1,0:T(8,128)(2,1)S(1)}, u32[]{:S(2)}, u32[]{:S(2)}) collective-permute-start(bf16[1,64,5120]{2,1,0:T(8,128)(2,1)} %get-tuple-element.42), channel_id=1, source_target_pairs={{0,8},{8,16},{16,24},{24,32},{32,40},{40,48},{48,56},{56,64},{64,7... | collective-permute-start | bytes 1966088 | tf_op jit(solution)/shard_map/ppermute | solution.py:28
  137.1 44.9 %collective-permute-start.5 = (bf16[1,64,5120]{2,1,0:T(8,128)(2,1)}, bf16[1,64,5120]{2,1,0:T(8,128)(2,1)S(1)}, u32[]{:S(2)}, u32[]{:S(2)}) collective-permute-start(bf16[1,64,5120]{2,1,0:T(8,128)(2,1)} %get-tuple-element.43), channel_id=1, source_target_pairs={{8,0},{16,8},{24,16},{32,24},{40,32},{48,40},{56,48},{64,56},{72,6... | collective-permute-start | bytes 1966088 | tf_op jit(solution)/shard_map/ppermute | solution.py:28
  138.4 32.2 %collective-permute-start.6 = (bf16[512,512]{1,0:T(8,128)(2,1)S(1)}, bf16[512,512]{1,0:T(8,128)(2,1)S(1)}, u32[]{:S(2)}, u32[]{:S(2)}) collective-permute-start(bf16[512,512]{1,0:T(8,128)(2,1)S(1)} %copy-done.9), channel_id=1, source_target_pairs={{0,1},{4,3},{7,6},{8,9},{12,11},{15,14},{16,17},{20,19},{23,22},{2... | collective-permute-start | bytes 1572872 | tf_op jit(solution)/shard_map/ppermute | solution.py:502
  139.1 31.5 %collective-permute-start.7 = (bf16[512,256]{1,0:T(8,128)(2,1)S(1)}, bf16[512,256]{1,0:T(8,128)(2,1)S(1)}, u32[]{:S(2)}, u32[]{:S(2)}) collective-permute-start(bf16[512,256]{1,0:T(8,128)(2,1)S(1)} %copy-done.10), channel_id=1, source_target_pairs={{2,1},{5,6},{10,9},{13,14},{18,17},{21,22},{26,25},{29,30},{34,33}... | collective-permute-start | bytes 786440 | tf_op jit(solution)/shard_map/ppermute | solution.py:502
  144.0 38.0 %all-to-all-start.1 = ((f32[256,1,128]{2,1,0:T(1,128)}), f32[256,1,128]{2,1,0:T(1,128)S(1)}, u32[]{:S(2)}, u32[]{:S(2)}) async-start(f32[256,1,128]{2,1,0:T(1,128)} %broadcast_in_dim.11), calls=%async_computation.1 | async-start | bytes 262144 | tf_op jit(solution)/shard_map/all_to_all | solution.py:516
  164.6 6.1 %collective-permute-start.8 = (bf16[512,128]{1,0:T(8,128)(2,1)S(1)}, bf16[512,128]{1,0:T(8,128)(2,1)S(1)}, u32[]{:S(2)}, u32[]{:S(2)}) collective-permute-start(bf16[512,128]{1,0:T(8,128)(2,1)S(1)} %copy-done.11), channel_id=1, source_target_pairs={{2,3},{5,4},{10,11},{13,12},{18,19},{21,20},{26,27},{29,28},{34,35... | collective-permute-start | bytes 393224 | tf_op jit(solution)/shard_map/ppermute | solution.py:502
  170.7 0.7 copy-start.5
  170.7 0.7 copy-start.4
  170.7 1.0 copy-start.3
  182.0 0.7 copy-start.6
  182.1 0.9 copy-start.7
  182.1 1.1 copy-start.8

commit v3 on v2

--- a/solution.py
+++ b/solution.py
@@ -376,25 +376,26 @@
 
 
 def forward_kernel(rows_ref, weight_ref, out_ref):
-    for start in range(0, weight_ref.shape[1], 512):
-        columns = slice(start, start + 512)
-        forward = dot(rows_ref[:, BLOCK:], weight_ref[:, columns], precision=None)
-        out_ref[:, columns] = forward.astype(BF16)
+    forward = dot(rows_ref[:, BLOCK:], weight_ref[...], precision=None)
+    out_ref[...] = forward.astype(BF16).reshape(out_ref.shape)
+
+
+HELD = ((0, 4), (1, 5), (3, 7), (2,), (6,))
 
 
 def product_kernel(me_ref, *refs):
     me = me_ref[0, 0]
-    pieces, (forward_ref, weight_ref, gathered, out_ref) = refs[:-4], refs[-4:]
-    groups, tokens, _ = out_ref.shape
-    part, width = weight_ref.shape
-    for offset, piece in enumerate(pieces):
-        for half in range(2):
-            start = pl.multiple_of((me ^ offset ^ (half * groups // 2)) * tokens, tokens)
-            gathered[pl.ds(start, tokens), :] = piece[half * tokens : (half + 1) * tokens, :]
-    for device in range(groups):
-        out_ref[device, :, :width] = forward_ref[device * tokens : (device + 1) * tokens, :]
+    pieces, (weight_ref, _, gathered, out_ref, back, sem) = refs[: len(HELD)], refs[len(HELD) :]
+    groups, tokens, part = back.shape
+    for held, piece in zip(HELD, pieces):
+        for index, offset in enumerate(held):
+            start = pl.multiple_of((me ^ offset) * tokens, tokens)
+            gathered[pl.ds(start, tokens), :] = piece[index * tokens : (index + 1) * tokens, :]
     backward = dot(gathered[...], weight_ref[...], (1, 1), None)
-    out_ref[:, :, width:] = backward.astype(BF16).reshape(groups, tokens, part)
+    back[...] = backward.astype(BF16).reshape(groups, tokens, part)
+    copy = pltpu.make_async_copy(back, out_ref.at[:, :, pl.ds(weight_ref.shape[1], part)], sem)
+    copy.start()
+    copy.wait()
 
 
 def finish_kernel(parts_ref, fwd_ref, bwd_ref, grad_ref, gain_ref, next_ref, back_ref):
@@ -403,55 +404,40 @@
     part = width // groups
     out_width = parts_ref.shape[2] - part
 
-    def some(rows):
-        for start in range(0, out_width, 1024):
-            columns = slice(start, start + 1024)
-            layer = parts_ref[0, rows, columns].astype(F32)
-            for group in range(1, groups):
-                layer += parts_ref[group, rows, columns].astype(F32)
-            next_ref[0, rows, columns] = (fwd_ref[rows, columns].astype(F32) + layer).astype(BF16)
-        next_ref[0, rows, out_width:] = fwd_ref[rows, out_width:]
-        squares, inner = 0.0, 0.0
-        for group in range(groups):
-            columns = slice(group * part, (group + 1) * part)
-            wide = bwd_ref[rows, columns].astype(F32)
-            scaled = parts_ref[group, rows, out_width:].astype(F32) * gain_ref[:, columns]
-            squares += jnp.sum(wide * wide, axis=1, keepdims=True)
-            inner += jnp.sum(scaled * wide, axis=1, keepdims=True)
-        scale = lax.rsqrt(squares * (1.0 / width) + EPS)
-        pull = scale**3 * (inner * (1.0 / width))
-        for group in range(groups):
-            columns = slice(group * part, (group + 1) * part)
-            wide = bwd_ref[rows, columns].astype(F32)
-            scaled = parts_ref[group, rows, out_width:].astype(F32) * gain_ref[:, columns]
-            out = grad_ref[rows, columns].astype(F32) + scale * scaled - wide * pull
-            back_ref[0, rows, columns] = out.astype(BF16)
-
-    by_rows(fwd_ref.shape[0], 16, some)
+    rows = slice(None)
+    for start in range(0, out_width, 1024):
+        columns = slice(start, start + 1024)
+        layer = parts_ref[0, rows, columns].astype(F32)
+        for group in range(1, groups):
+            layer += parts_ref[group, rows, columns].astype(F32)
+        next_ref[0, rows, columns] = (fwd_ref[rows, columns].astype(F32) + layer).astype(BF16)
+    next_ref[0, rows, out_width:] = fwd_ref[rows, out_width:]
+    squares, inner = 0.0, 0.0
+    for group in range(groups):
+        columns = slice(group * part, (group + 1) * part)
+        wide = bwd_ref[rows, columns].astype(F32)
+        scaled = parts_ref[group, rows, out_width:].astype(F32) * gain_ref[:, columns]
+        squares += jnp.sum(wide * wide, axis=1, keepdims=True)
+        inner += jnp.sum(scaled * wide, axis=1, keepdims=True)
+    scale = lax.rsqrt(squares * (1.0 / width) + EPS)
+    pull = scale**3 * (inner * (1.0 / width))
+    for group in range(groups):
+        columns = slice(group * part, (group + 1) * part)
+        wide = bwd_ref[rows, columns].astype(F32)
+        scaled = parts_ref[group, rows, out_width:].astype(F32) * gain_ref[:, columns]
+        out = grad_ref[rows, columns].astype(F32) + scale * scaled - wide * pull
+        back_ref[0, rows, columns] = out.astype(BF16)
 
 
 def update_kernel(
-    entries, terms_ref, turned_ref, grad_ref, fwd_ref, back_ref, out_ref, next_ref, last_ref, sems
+    entries, terms_ref, turned_ref, grad_ref, fwd_ref, back_ref, out_ref, next_ref, last_ref
 ):
-    copies = (
-        pltpu.make_async_copy(fwd_ref, next_ref, sems.at[0]),
-        pltpu.make_async_copy(back_ref, last_ref, sems.at[1]),
-    )
-
-    @pl.when(pl.program_id(0) == 0)
-    def _():
-        for copy in copies:
-            copy.start()
-
     terms = terms_ref[...]
     total = jnp.sum(jnp.sum(terms, axis=0, keepdims=True)[:, :1], axis=1, keepdims=True)
     ratio = jnp.sqrt(entries / total)
     out_ref[...] = (ratio * dot(turned_ref[...], grad_ref[...], precision=None)).astype(BF16)
-
-    @pl.when(pl.program_id(0) == pl.num_programs(0) - 1)
-    def _():
-        for copy in copies:
-            copy.wait()
+    next_ref[...] = fwd_ref[...]
+    last_ref[...] = back_ref[...]
 
 
 def per_device(x_fwd, x_bwd, grad_in, gain, weight, damping):
@@ -480,22 +466,45 @@
     )
     sent, other = lax.optimization_barrier((sent, other))
     pair = jnp.concatenate([upstream, other], axis=0)
-    pieces = [pair] + [swap(pair, offset) for offset in range(1, half)]
+    near, far = swap(pair, 1), swap(pair, half - 1)
     rows = lax.all_to_all(sent, "dp", 0, 0, tiled=True).reshape(group, BLOCK + own_rows)
 
     left, *moves = solve_act(damp_value, me_value, rows)
-    (forward,) = run(
-        forward_kernel, "forward", [shape(group, out_width)], (), (rows, local_w), 2 * 10**9
-    )
-    ready = lax.optimization_barrier((me_value, *pieces, forward, left))
-    group_grad, products = run(
+    near, far, _ = lax.optimization_barrier((near, far, left))
+    pieces = [pair, near, far, swap(far[:tokens], 1), swap(near[tokens:], half - 1)]
+    columns = 512
+    forward = pl.pallas_call(
+        forward_kernel,
+        grid=(out_width // columns,),
+        out_shape=shape(groups, tokens, out_width + own_rows),
+        in_specs=[
+            pl.BlockSpec((group, BLOCK + own_rows), lambda i: (0, 0)),
+            pl.BlockSpec((own_rows, columns), lambda i: (0, i)),
+        ],
+        out_specs=pl.BlockSpec((groups, tokens, columns), lambda i: (0, 0, i)),
+        compiler_params=params(),
+        cost_estimate=cost(2 * 10**9, 8 * 10**6),
+        name="forward",
+    )(rows, local_w)
+    scalar, *arrays = lax.optimization_barrier((me_value, *pieces, forward, left))[:-1]
+    arrays = arrays[:-1] + [local_w, arrays[-1]]
+    keep = pl.BlockSpec(memory_space=pl.ANY)
+    outs = (shape(group, out_width), shape(groups, tokens, out_width + own_rows))
+    group_grad, products = pl.pallas_call(
         product_kernel,
-        "products",
-        [shape(group, out_width), shape(groups, tokens, out_width + own_rows)],
-        ready[:1],
-        (*ready[1:-1], local_w),
-        2 * 10**9,
-    )
+        grid=(1,),
+        out_shape=outs,
+        in_specs=[SMEM] + [whole_block(value) for value in arrays[:-1]] + [keep],
+        out_specs=(whole_block(outs[0]), keep),
+        scratch_shapes=[
+            pltpu.VMEM((groups, tokens, own_rows), BF16),
+            pltpu.SemaphoreType.DMA,
+        ],
+        input_output_aliases={len(arrays): 1},
+        compiler_params=params(),
+        cost_estimate=cost(2 * 10**9, 10**7),
+        name="products",
+    )(scalar, *arrays)
     parts = lax.all_to_all(products, "dp", 0, 0, tiled=True)
 
     moves = moves[:1] + [
@@ -518,34 +527,45 @@
     )
 
     parts, _ = lax.optimization_barrier((parts, term))
-    out_f, out_b = run(
+    step = 16
+    wide_block = pl.BlockSpec((step, width), lambda i: (i, 0))
+    out_block = pl.BlockSpec((1, step, width), lambda i: (0, i, 0))
+    out_f, out_b = pl.pallas_call(
         finish_kernel,
-        "finish",
-        [shape(1, tokens, width)] * 2,
-        (),
-        (parts, fwd, bwd, grad, gain),
-        10**7,
-    )
+        grid=(tokens // step,),
+        out_shape=(shape(1, tokens, width),) * 2,
+        in_specs=[
+            pl.BlockSpec((groups, step, out_width + own_rows), lambda i: (0, i, 0)),
+            wide_block,
+            wide_block,
+            wide_block,
+            pl.BlockSpec((1, width), lambda i: (0, 0)),
+        ],
+        out_specs=(out_block, out_block),
+        compiler_params=params(),
+        cost_estimate=cost(10**7, 8 * 10**6),
+        name="finish",
+    )(parts, fwd, bwd, grad, gain)
     next_fwd = from_behind(out_f, "section", 1)
     next_grad = from_behind(out_b, "section", -1)
     terms, next_fwd, next_grad = lax.optimization_barrier((terms, next_fwd, next_grad))
 
-    columns = 512
     entries = float(lax.axis_size("section") * width * out_width)
-    keep = pl.BlockSpec(memory_space=pl.ANY)
+    steps = 4
+    columns = out_width // steps
+    same = pl.BlockSpec((1, tokens, width // steps), lambda i: (0, 0, i))
     update, next_fwd, next_grad = pl.pallas_call(
         lambda *refs: update_kernel(entries, *refs),
-        grid=(out_width // columns,),
+        grid=(steps,),
         out_shape=(shape(own_rows, out_width),) + (shape(1, tokens, width),) * 2,
         in_specs=[
             pl.BlockSpec((devices, 128), lambda i: (0, 0)),
             pl.BlockSpec((own_rows, group), lambda i: (0, 0)),
             pl.BlockSpec((group, columns), lambda i: (0, i)),
-            keep,
-            keep,
+            same,
+            same,
         ],
-        out_specs=(pl.BlockSpec((own_rows, columns), lambda i: (0, i)), keep, keep),
-        scratch_shapes=[pltpu.SemaphoreType.DMA((2,))],
+        out_specs=(pl.BlockSpec((own_rows, columns), lambda i: (0, i)), same, same),
         compiler_params=params(),
         cost_estimate=cost(2 * 10**9, 8 * 10**6),
         name="update",

time: 227 us -> 184 us (0.81)
  Pallas kernels: 123 us -> 86.6 us
  starting transfers between devices: 52.1 us -> 47.6 us
  waiting for transfers between devices: 43 us -> 39.5 us
    pallas_call x7 -> x4, Pallas kernels: 80 us -> 59.5 us  [run(): pl.pallas_call(kernel, grid=(1,), out_shape=tuple(outs), in_specs=[SMEM]...]
    pallas_call x1 -> x4, Pallas kernels: 43 us -> 27 us  [the longest x1 8.42 us: per_device(): pl.pallas_call(product_kernel, grid=(1,), out_shape=outs, in_specs=[SMEM]...]
    ppermute x4 -> x5, waiting for transfers between devices: 15.7 us -> 7.85 us  [swap(): return lax.ppermute(value, 'dp', [(i, i ^ offset) for i in range(8)])]
    all_to_all x1, starting transfers between devices: 11.6 us -> 5.61 us  [per_device(): parts = lax.all_to_all(products, 'dp', 0, 0, tiled=True)]
    all_to_all x1, waiting for transfers between devices: 0.05 us -> 3.59 us  [per_device(): parts = lax.all_to_all(products, 'dp', 0, 0, tiled=True)]
    ppermute x4 -> x5, starting transfers between devices: 4.38 us -> 6.54 us  [swap(): return lax.ppermute(value, 'dp', [(i, i ^ offset) for i in range(8)])]
  transfers between devices with their start and end apart: 12 -> 13, of which waited for: 5 -> 6; matrix products, arithmetic and copies ran while one was open for 1% -> 1% of each run, Pallas kernels for 29% -> 37%
where the time goes in v3:
time: 184 us; the launch traced here: 183 us
  Pallas kernels  86.6 us (47%)
  starting transfers between devices  47.6 us (26%)
  waiting for transfers between devices  39.5 us (21%)
  local copies, waits for them, and re-layouts  8.15 us (4%)
    pallas_call x4, Pallas kernels, run(): pl.pallas_call(kernel, grid=(1,), out_shape=tuple(outs), in_specs=[SMEM]...  59.5 us
    all_to_all x1, starting transfers between devices, per_device(): lax.all_to_all(jnp.broadcast_to(term, (devices, 128)), ('section', 'dp'),...  21.4 us
    all_to_all x1, waiting for transfers between devices, per_device(): lax.all_to_all(sent, 'dp', 0, 0, tiled=True)  16.6 us
    pallas_call x1, Pallas kernels, per_device(): pl.pallas_call(product_kernel, grid=(1,), out_shape=outs, in_specs=[SMEM]...  8.42 us
    ppermute x5, waiting for transfers between devices, swap(): return lax.ppermute(value, 'dp', [(i, i ^ offset) for i in range(8)])  7.85 us
    all_to_all x1, waiting for transfers between devices, per_device(): lax.all_to_all(jnp.broadcast_to(term, (devices, 128)), ('section', 'dp'),...  7.82 us
    pallas_call x1, Pallas kernels, per_device(): pl.pallas_call(forward_kernel, grid=(out_width // columns,), out_shape=sh...  7.44 us
    pallas_call x1, Pallas kernels, per_device(): pl.pallas_call(lambda *refs: update_kernel(entries, *refs), grid=(steps,)...  6.57 us
  transfers between devices with their start and end apart: 13, of which 6 were waited for; matrix products, arithmetic and copies ran while one was open for 1% of the time, Pallas kernels for 37%

profile of v3, /device:TPU:40, one launch (start us, length us, event | category | flops | bytes accessed | tf_op | source)
XLA Modules:
  0.0 183.3 jit_solution(1702850513852731403)
XLA Ops:
  0.6 1.0 slice.12
  1.9 3.2 %normalize.1 = bf16[8,64,1664]{2,1,0:T(8,128)(2,1)} custom-call(bf16[64,5120]{1,0:T(8,128)(2,1)} %bitcast.16, bf16[64,5120]{1,0:T(8,128)(2,1)} %bitcast.18, f32[1,5120]{1,0:T(1,128)} %gain_ref.3), custom_call_target="tpu_custom_call" | custom-call | flops 10000000 | bytes 3035136 | tf_op jit(solution)/shard_map/normalize/pallas_call | solution.py:332
  5.1 7.5 %collective-permute-done = bf16[64,3072]{1,0:T(8,128)(2,1)S(1)} collective-permute-done((bf16[64,3072]{1,0:T(8,128)(2,1)S(1)}, bf16[64,3072]{1,0:T(8,128)(2,1)S(1)}, u32[]{:S(2)}, u32[]{:S(2)}) %collective-permute-start) | collective-permute-done | bytes 393248 | tf_op jit(solution)/shard_map/ppermute | solution.py:361
  12.6 5.8 %all-to-all-start = ((bf16[8,64,1664]{2,1,0:T(8,128)(2,1)}), bf16[8,64,1664]{2,1,0:T(8,128)(2,1)S(1)}, u32[]{:S(2)}, u32[]{:S(2)}) async-start(bf16[8,64,1664]{2,1,0:T(8,128)(2,1)} %normalize.1), calls=%async_computation | async-start | bytes 3407872 | tf_op jit(solution)/shard_map/all_to_all | solution.py:470
  19.1 1.6 collective-permute-start.2
  20.7 1.8 collective-permute-start.1
  22.5 16.6 %all-to-all-done = bf16[8,64,1664]{2,1,0:T(8,128)(2,1)S(1)} async-done(((bf16[8,64,1664]{2,1,0:T(8,128)(2,1)}), bf16[8,64,1664]{2,1,0:T(8,128)(2,1)S(1)}, u32[]{:S(2)}, u32[]{:S(2)}) %all-to-all-start) | async-done | bytes 1703968 | tf_op jit(solution)/shard_map/all_to_all | solution.py:470
  39.0 1.2 copy-done
  40.3 16.0 %solve_act.1 = (f32[512,512]{1,0:T(8,128)}, bf16[512,640]{1,0:T(8,128)(2,1)}, bf16[512,512]{1,0:T(8,128)(2,1)}, bf16[512,256]{1,0:T(8,128)(2,1)}, bf16[512,128]{1,0:T(8,128)(2,1)}) custom-call(f32[1,1]{1,0:T(1,128)} %bitcast.10.damping_ref, s32[1,1]{1,0:T(1,128)} %bitcast.1.me_ref, bf16[512,1664]{1,0:T(8,128)(2,1)} %bitcast.14), custom_call_target="tpu_custom_call" | custom-call | flops 16000000000 | bytes 4325376 | tf_op jit(solution)/shard_map/solve_act/pallas_call | solution.py:332
  56.2 1.3 slice.11
  57.6 0.9 collective-permute-start.3
  58.5 2.1 %collective-permute-start.4 = (bf16[64,3072]{1,0:T(8,128)(2,1)S(1)}, bf16[64,3072]{1,0:T(8,128)(2,1)S(1)}, u32[]{:S(2)}, u32[]{:S(2)}) collective-permute-start(bf16[64,3072]{1,0:T(8,128)(2,1)S(1)} %slice.11), channel_id=1, source_target_pairs={{0,3},{1,2},{2,1},{3,0},{4,7},{5,6},{6,5},{7,4},{8,11},{9,10},{10,... | collective-permute-start | bytes 1179656 | tf_op jit(solution)/shard_map/ppermute | solution.py:361
  60.6 7.4 %forward.1.refs_6_ = bf16[8,64,3712]{2,1,0:T(8,128)(2,1)} custom-call(bf16[512,1664]{1,0:T(8,128)(2,1)} %bitcast.15, bf16[640,3072]{1,0:T(8,128)(2,1)} %bitcast.12), custom_call_target="tpu_custom_call" | custom-call | flops 2000000000 | bytes 8000000 | tf_op jit(solution)/shard_map/forward/pallas_call | solution.py:476
  68.8 0.7 copy-done.5
  69.5 8.4 %products.1 = (bf16[512,3072]{1,0:T(8,128)(2,1)}, bf16[8,64,3712]{2,1,0:T(8,128)(2,1)}) custom-call(s32[1,1]{1,0:T(1,128)} %bitcast.1.me_ref, bf16[128,3072]{1,0:T(8,128)(2,1)} %copy-done.1, bf16[128,3072]{1,0:T(8,128)(2,1)} %collective-permute-done.1.refs_1_, bf16[128,3072]{1,0:T(8,128)(2,1)} %copy-done.2, ...), custom_call_target="tpu_custom_call", output_to_operand_aliasing={{1}: (7, {})} | custom-call | flops 2000000000 | bytes 10000000 | tf_op jit(solution)/shard_map/products/pallas_call | solution.py:493
  78.0 5.6 %all-to-all-start.2 = ((bf16[8,64,3712]{2,1,0:T(8,128)(2,1)}), bf16[8,64,3712]{2,1,0:T(8,128)(2,1)}, u32[]{:S(2)}, u32[]{:S(2)}) async-start(bf16[8,64,3712]{2,1,0:T(8,128)(2,1)} %get-tuple-element.46), calls=%async_computation.2 | async-start | bytes 7602176 | tf_op jit(solution)/shard_map/all_to_all | solution.py:508
  83.6 37.8 %solve_grad.1 = (bf16[512,3072]{1,0:T(8,128)(2,1)}, f32[1,1]{1,0:T(1,128)}) custom-call(f32[1,1]{1,0:T(1,128)} %bitcast.11.damping_ref, bf16[512,3072]{1,0:T(8,128)(2,1)} %get-tuple-element.44.rows_ref, f32[512,512]{1,0:T(8,128)} %get-tuple-element.34.left_ref), custom_call_target="tpu_custom_call" | custom-call | flops 44999999488 | bytes 7340036 | tf_op jit(solution)/shard_map/solve_grad/pallas_call | solution.py:332
  121.3 3.6 %all-to-all-done.2.parts_ref = bf16[8,64,3712]{2,1,0:T(8,128)(2,1)} async-done(((bf16[8,64,3712]{2,1,0:T(8,128)(2,1)}), bf16[8,64,3712]{2,1,0:T(8,128)(2,1)}, u32[]{:S(2)}, u32[]{:S(2)}) %all-to-all-start.2) | async-done | bytes 3801120 | tf_op jit(solution)/shard_map/all_to_all | solution.py:508
  124.9 4.6 %finish.1 = (bf16[1,64,5120]{2,1,0:T(8,128)(2,1)}, bf16[1,64,5120]{2,1,0:T(8,128)(2,1)}) custom-call(bf16[8,64,3712]{2,1,0:T(8,128)(2,1)} %all-to-all-done.2.parts_ref, bf16[64,5120]{1,0:T(8,128)(2,1)} %bitcast.17, bf16[64,5120]{1,0:T(8,128)(2,1)} %bitcast.19, bf16[64,5120]{1,0:T(8,128)(2,1)} %bitcast.21, f32[1,5120]{1,0:T(1,128)} %gain_ref.3), custom_call_target="tpu_custom_call" | custom-call | flops 10000000 | bytes 8000000 | tf_op jit(solution)/shard_map/finish/pallas_call | solution.py:533
  129.6 1.9 %collective-permute-start.5 = (bf16[1,64,5120]{2,1,0:T(8,128)(2,1)}, bf16[1,64,5120]{2,1,0:T(8,128)(2,1)S(1)}, u32[]{:S(2)}, u32[]{:S(2)}) collective-permute-start(bf16[1,64,5120]{2,1,0:T(8,128)(2,1)} %get-tuple-element.48), channel_id=1, source_target_pairs={{0,8},{8,16},{16,24},{24,32},{32,40},{40,48},{48,56},{56,64},{64,7... | collective-permute-start | bytes 1966088 | tf_op jit(solution)/shard_map/ppermute | solution.py:28
  131.5 1.3 collective-permute-start.6
  132.8 0.7 collective-permute-start.7
  133.5 1.9 %collective-permute-start.8 = (bf16[512,256]{1,0:T(8,128)(2,1)S(1)}, bf16[512,256]{1,0:T(8,128)(2,1)S(1)}, u32[]{:S(2)}, u32[]{:S(2)}) collective-permute-start(bf16[512,256]{1,0:T(8,128)(2,1)S(1)} %copy-done.12), channel_id=1, source_target_pairs={{2,1},{5,6},{10,9},{13,14},{18,17},{21,22},{26,25},{29,30},{34,33}... | collective-permute-start | bytes 786440 | tf_op jit(solution)/shard_map/ppermute | solution.py:511
  135.5 1.3 broadcast_in_dim.11
  136.8 21.4 %all-to-all-start.1 = ((f32[256,1,128]{2,1,0:T(1,128)}), f32[256,1,128]{2,1,0:T(1,128)S(1)}, u32[]{:S(2)}, u32[]{:S(2)}) async-start(f32[256,1,128]{2,1,0:T(1,128)} %broadcast_in_dim.11), calls=%async_computation.1 | async-start | bytes 262144 | tf_op jit(solution)/shard_map/all_to_all | solution.py:525
  158.2 2.4 %collective-permute-start.9 = (bf16[512,128]{1,0:T(8,128)(2,1)S(1)}, bf16[512,128]{1,0:T(8,128)(2,1)S(1)}, u32[]{:S(2)}, u32[]{:S(2)}) collective-permute-start(bf16[512,128]{1,0:T(8,128)(2,1)S(1)} %copy-done.13), channel_id=1, source_target_pairs={{2,3},{5,4},{10,11},{13,12},{18,19},{21,20},{26,27},{29,28},{34,35... | collective-permute-start | bytes 393224 | tf_op jit(solution)/shard_map/ppermute | solution.py:511
  160.6 3.6 %collective-permute-done.9.refs_3_ = bf16[512,128]{1,0:T(8,128)(2,1)S(1)} collective-permute-done((bf16[512,128]{1,0:T(8,128)(2,1)S(1)}, bf16[512,128]{1,0:T(8,128)(2,1)S(1)}, u32[]{:S(2)}, u32[]{:S(2)}) %collective-permute-start.9) | collective-permute-done | bytes 131104 | tf_op jit(solution)/shard_map/ppermute | solution.py:511
  164.3 0.6 copy-done.7
  165.3 2.6 %assemble.1.refs_1_ = bf16[640,512]{1,0:T(8,128)(2,1)} custom-call(s32[1,1]{1,0:T(1,128)} %bitcast.1.me_ref, bf16[512,640]{1,0:T(8,128)(2,1)} %get-tuple-element.51.refs_0_, bf16[512,512]{1,0:T(8,128)(2,1)} %copy-done.3, bf16[512,256]{1,0:T(8,128)(2,1)} %copy-done.6, bf16[512,128]{1,0:T(8,128)(2,1)} %copy-done.7), custom_call_target="tpu_custom_call" | custom-call | flops 10000000 | bytes 2228224 | tf_op jit(solution)/shard_map/assemble/pallas_call | solution.py:332
  167.8 7.8 %all-to-all-done.1 = f32[256,1,128]{2,1,0:T(1,128)S(1)} async-done(((f32[256,1,128]{2,1,0:T(1,128)}), f32[256,1,128]{2,1,0:T(1,128)S(1)}, u32[]{:S(2)}, u32[]{:S(2)}) %all-to-all-start.1) | async-done | bytes 131104 | tf_op jit(solution)/shard_map/all_to_all | solution.py:525
  175.7 0.6 copy-done.8
  176.8 6.6 %update.1 = (bf16[640,3072]{1,0:T(8,128)(2,1)}, bf16[1,64,5120]{2,1,0:T(8,128)(2,1)}, bf16[1,64,5120]{2,1,0:T(8,128)(2,1)}) custom-call(f32[256,128]{1,0:T(8,128)} %bitcast.22, bf16[640,512]{1,0:T(8,128)(2,1)} %assemble.1.refs_1_, bf16[512,3072]{1,0:T(8,128)(2,1)} %get-tuple-element.55.refs_2_, bf16[1,64,5120]{2,1,0:T(8,128)(2,1)} %copy-done.9, ...), custom_call_target="tpu_custom_call" | custom-call | flops 2000000000 | bytes 8000000 | tf_op jit(solution)/shard_map/update/pallas_call | solution.py:557
  (35 shorter events, 1.9 us)
Async XLA Ops:
  1.7 10.9 %collective-permute-start = (bf16[64,3072]{1,0:T(8,128)(2,1)S(1)}, bf16[64,3072]{1,0:T(8,128)(2,1)S(1)}, u32[]{:S(2)}, u32[]{:S(2)}) collective-permute-start(bf16[64,3072]{1,0:T(8,128)(2,1)S(1)} %slice.12), channel_id=1, source_target_pairs={{0,4},{1,5},{2,6},{3,7},{4,0},{5,1},{6,2},{7,3},{8,12},{9,13},{10,... | collective-permute-start | bytes 1179656 | tf_op jit(solution)/shard_map/ppermute | solution.py:361
  12.6 26.4 %all-to-all-start = ((bf16[8,64,1664]{2,1,0:T(8,128)(2,1)}), bf16[8,64,1664]{2,1,0:T(8,128)(2,1)S(1)}, u32[]{:S(2)}, u32[]{:S(2)}) async-start(bf16[8,64,1664]{2,1,0:T(8,128)(2,1)} %normalize.1), calls=%async_computation | async-start | bytes 3407872 | tf_op jit(solution)/shard_map/all_to_all | solution.py:470
  19.1 37.1 %copy-start.1 = (bf16[128,3072]{1,0:T(8,128)(2,1)}, bf16[128,3072]{1,0:T(8,128)(2,1)S(1)}, u32[]{:S(2)}) copy-start(bf16[128,3072]{1,0:T(8,128)(2,1)S(1)} %pad_maximum_fusion.refs_0_) | copy-start | bytes 2359300
  19.1 37.1 %collective-permute-start.2 = (bf16[128,3072]{1,0:T(8,128)(2,1)S(1)}, bf16[128,3072]{1,0:T(8,128)(2,1)S(1)}, u32[]{:S(2)}, u32[]{:S(2)}) collective-permute-start(bf16[128,3072]{1,0:T(8,128)(2,1)S(1)} %pad_maximum_fusion.refs_0_), channel_id=1, source_target_pairs={{0,3},{1,2},{2,1},{3,0},{4,7},{5,6},{6,5},{7,4},{8,11},{9,10},{10,... | collective-permute-start | bytes 2359304 | tf_op jit(solution)/shard_map/ppermute | solution.py:361
  20.7 35.5 %collective-permute-start.1 = (bf16[128,3072]{1,0:T(8,128)(2,1)S(1)}, bf16[128,3072]{1,0:T(8,128)(2,1)}, u32[]{:S(2)}, u32[]{:S(2)}) collective-permute-start(bf16[128,3072]{1,0:T(8,128)(2,1)S(1)} %pad_maximum_fusion.refs_0_), channel_id=1, source_target_pairs={{0,1},{1,0},{2,3},{3,2},{4,5},{5,4},{6,7},{7,6},{8,9},{9,8},{10,11... | collective-permute-start | bytes 2359304 | tf_op jit(solution)/shard_map/ppermute | solution.py:361
  39.0 1.2 copy-start
  56.2 11.8 %copy-start.2 = (bf16[128,3072]{1,0:T(8,128)(2,1)}, bf16[128,3072]{1,0:T(8,128)(2,1)S(1)}, u32[]{:S(2)}) copy-start(bf16[128,3072]{1,0:T(8,128)(2,1)S(1)} %collective-permute-done.2.refs_2_) | copy-start | bytes 2359300
  57.6 10.5 %collective-permute-start.3 = (bf16[64,3072]{1,0:T(8,128)(2,1)S(1)}, bf16[64,3072]{1,0:T(8,128)(2,1)S(1)}, u32[]{:S(2)}, u32[]{:S(2)}) collective-permute-start(bf16[64,3072]{1,0:T(8,128)(2,1)S(1)} %slice.10), channel_id=1, source_target_pairs={{0,1},{1,0},{2,3},{3,2},{4,5},{5,4},{6,7},{7,6},{8,9},{9,8},{10,11... | collective-permute-start | bytes 1179656 | tf_op jit(solution)/shard_map/ppermute | solution.py:361
  58.5 9.9 %collective-permute-start.4 = (bf16[64,3072]{1,0:T(8,128)(2,1)S(1)}, bf16[64,3072]{1,0:T(8,128)(2,1)S(1)}, u32[]{:S(2)}, u32[]{:S(2)}) collective-permute-start(bf16[64,3072]{1,0:T(8,128)(2,1)S(1)} %slice.11), channel_id=1, source_target_pairs={{0,3},{1,2},{2,1},{3,0},{4,7},{5,6},{6,5},{7,4},{8,11},{9,10},{10,... | collective-permute-start | bytes 1179656 | tf_op jit(solution)/shard_map/ppermute | solution.py:361
  68.1 0.7 copy-start.4
  68.8 0.7 copy-start.5
  78.0 47.0 %all-to-all-start.2 = ((bf16[8,64,3712]{2,1,0:T(8,128)(2,1)}), bf16[8,64,3712]{2,1,0:T(8,128)(2,1)}, u32[]{:S(2)}, u32[]{:S(2)}) async-start(bf16[8,64,3712]{2,1,0:T(8,128)(2,1)} %get-tuple-element.46), calls=%async_computation.2 | async-start | bytes 7602176 | tf_op jit(solution)/shard_map/all_to_all | solution.py:508
  121.3 11.5 %copy-start.11 = (bf16[512,512]{1,0:T(8,128)(2,1)S(1)}, bf16[512,512]{1,0:T(8,128)(2,1)}, u32[]{:S(2)}) copy-start(bf16[512,512]{1,0:T(8,128)(2,1)} %get-tuple-element.52) | copy-start | bytes 1572868
  121.3 12.2 %copy-start.12 = (bf16[512,256]{1,0:T(8,128)(2,1)S(1)}, bf16[512,256]{1,0:T(8,128)(2,1)}, u32[]{:S(2)}) copy-start(bf16[512,256]{1,0:T(8,128)(2,1)} %get-tuple-element.53) | copy-start | bytes 786436
  121.3 36.9 %copy-start.13 = (bf16[512,128]{1,0:T(8,128)(2,1)S(1)}, bf16[512,128]{1,0:T(8,128)(2,1)}, u32[]{:S(2)}) copy-start(bf16[512,128]{1,0:T(8,128)(2,1)} %get-tuple-element.54) | copy-start | bytes 393220
  129.6 46.1 %collective-permute-start.5 = (bf16[1,64,5120]{2,1,0:T(8,128)(2,1)}, bf16[1,64,5120]{2,1,0:T(8,128)(2,1)S(1)}, u32[]{:S(2)}, u32[]{:S(2)}) collective-permute-start(bf16[1,64,5120]{2,1,0:T(8,128)(2,1)} %get-tuple-element.48), channel_id=1, source_target_pairs={{0,8},{8,16},{16,24},{24,32},{32,40},{40,48},{48,56},{56,64},{64,7... | collective-permute-start | bytes 1966088 | tf_op jit(solution)/shard_map/ppermute | solution.py:28
  131.5 44.1 %collective-permute-start.6 = (bf16[1,64,5120]{2,1,0:T(8,128)(2,1)}, bf16[1,64,5120]{2,1,0:T(8,128)(2,1)S(1)}, u32[]{:S(2)}, u32[]{:S(2)}) collective-permute-start(bf16[1,64,5120]{2,1,0:T(8,128)(2,1)} %get-tuple-element.49), channel_id=1, source_target_pairs={{8,0},{16,8},{24,16},{32,24},{40,32},{48,40},{56,48},{64,56},{72,6... | collective-permute-start | bytes 1966088 | tf_op jit(solution)/shard_map/ppermute | solution.py:28
  132.8 31.5 %collective-permute-start.7 = (bf16[512,512]{1,0:T(8,128)(2,1)S(1)}, bf16[512,512]{1,0:T(8,128)(2,1)S(1)}, u32[]{:S(2)}, u32[]{:S(2)}) collective-permute-start(bf16[512,512]{1,0:T(8,128)(2,1)S(1)} %copy-done.11), channel_id=1, source_target_pairs={{0,1},{4,3},{7,6},{8,9},{12,11},{15,14},{16,17},{20,19},{23,22},{2... | collective-permute-start | bytes 1572872 | tf_op jit(solution)/shard_map/ppermute | solution.py:511
  133.5 30.7 %collective-permute-start.8 = (bf16[512,256]{1,0:T(8,128)(2,1)S(1)}, bf16[512,256]{1,0:T(8,128)(2,1)S(1)}, u32[]{:S(2)}, u32[]{:S(2)}) collective-permute-start(bf16[512,256]{1,0:T(8,128)(2,1)S(1)} %copy-done.12), channel_id=1, source_target_pairs={{2,1},{5,6},{10,9},{13,14},{18,17},{21,22},{26,25},{29,30},{34,33}... | collective-permute-start | bytes 786440 | tf_op jit(solution)/shard_map/ppermute | solution.py:511
  136.8 38.8 %all-to-all-start.1 = ((f32[256,1,128]{2,1,0:T(1,128)}), f32[256,1,128]{2,1,0:T(1,128)S(1)}, u32[]{:S(2)}, u32[]{:S(2)}) async-start(f32[256,1,128]{2,1,0:T(1,128)} %broadcast_in_dim.11), calls=%async_computation.1 | async-start | bytes 262144 | tf_op jit(solution)/shard_map/all_to_all | solution.py:525
  158.2 6.0 %collective-permute-start.9 = (bf16[512,128]{1,0:T(8,128)(2,1)S(1)}, bf16[512,128]{1,0:T(8,128)(2,1)S(1)}, u32[]{:S(2)}, u32[]{:S(2)}) collective-permute-start(bf16[512,128]{1,0:T(8,128)(2,1)S(1)} %copy-done.13), channel_id=1, source_target_pairs={{2,3},{5,4},{10,11},{13,12},{18,19},{21,20},{26,27},{29,28},{34,35... | collective-permute-start | bytes 393224 | tf_op jit(solution)/shard_map/ppermute | solution.py:511
  164.3 0.7 copy-start.7
  164.3 0.7 copy-start.6
  164.3 1.0 copy-start.3
  175.6 0.7 copy-start.8
  175.6 0.9 copy-start.9
  175.6 1.1 copy-start.10

commit v4 on v3

--- a/solution.py
+++ b/solution.py
@@ -309,6 +309,7 @@
 
 
 SMEM = pl.BlockSpec(memory_space=pltpu.SMEM)
+VMEM = pl.BlockSpec(memory_space=pltpu.VMEM)
 
 
 def shape(*dims, dtype=BF16):
@@ -323,11 +324,11 @@
     return pl.CostEstimate(flops=flops, bytes_accessed=moved, transcendentals=0)
 
 
-def params():
-    return pltpu.CompilerParams(vmem_limit_bytes=56 * 2**20)
-
-
-def run(kernel, name, outs, scalars, arrays, flops, scratch=()):
+def params(mib=56):
+    return pltpu.CompilerParams(vmem_limit_bytes=mib * 2**20)
+
+
+def run(kernel, name, outs, scalars, arrays, flops, scratch=(), mib=56):
     moved = sum(value.size * value.dtype.itemsize for value in (*arrays, *outs))
     return pl.pallas_call(
         kernel,
@@ -336,7 +337,7 @@
         in_specs=[SMEM] * len(scalars) + [whole_block(value) for value in arrays],
         out_specs=tuple(whole_block(value) for value in outs),
         scratch_shapes=list(scratch),
-        compiler_params=params(),
+        compiler_params=params(mib),
         cost_estimate=cost(flops, moved),
         name=name,
     )(*scalars, *arrays)
@@ -347,7 +348,7 @@
     outs = [shape(count, count, dtype=F32)]
     outs += [shape(count, units * UNIT) for units, _, _ in MOVES]
     scratch = [pltpu.VMEM((count, BLOCK), BF16)] + solver_scratch(count)
-    return run(act_kernel, "solve_act", outs, (damping, me), (rows,), 16 * 10**9, scratch)
+    return run(act_kernel, "solve_act", outs, (damping, me), (rows,), 16 * 10**9, scratch, 28)
 
 
 def solve_grad(damping, rows, left):
@@ -376,7 +377,9 @@
 
 
 def forward_kernel(rows_ref, weight_ref, out_ref):
-    forward = dot(rows_ref[:, BLOCK:], weight_ref[...], precision=None)
+    width = out_ref.shape[2]
+    columns = pl.ds(pl.multiple_of(pl.program_id(0) * width, width), width)
+    forward = dot(rows_ref[:, BLOCK:], weight_ref[:, columns], precision=None)
     out_ref[...] = forward.astype(BF16).reshape(out_ref.shape)
 
 
@@ -479,10 +482,10 @@
         out_shape=shape(groups, tokens, out_width + own_rows),
         in_specs=[
             pl.BlockSpec((group, BLOCK + own_rows), lambda i: (0, 0)),
-            pl.BlockSpec((own_rows, columns), lambda i: (0, i)),
+            VMEM,
         ],
         out_specs=pl.BlockSpec((groups, tokens, columns), lambda i: (0, 0, i)),
-        compiler_params=params(),
+        compiler_params=params(20),
         cost_estimate=cost(2 * 10**9, 8 * 10**6),
         name="forward",
     )(rows, local_w)
@@ -494,14 +497,14 @@
         product_kernel,
         grid=(1,),
         out_shape=outs,
-        in_specs=[SMEM] + [whole_block(value) for value in arrays[:-1]] + [keep],
+        in_specs=[SMEM] + [VMEM] * (len(arrays) - 1) + [keep],
         out_specs=(whole_block(outs[0]), keep),
         scratch_shapes=[
             pltpu.VMEM((groups, tokens, own_rows), BF16),
             pltpu.SemaphoreType.DMA,
         ],
         input_output_aliases={len(arrays): 1},
-        compiler_params=params(),
+        compiler_params=params(20),
         cost_estimate=cost(2 * 10**9, 10**7),
         name="products",
     )(scalar, *arrays)

time: 184 us -> 182 us (0.989)
  Pallas kernels: 86.6 us -> 75.9 us
  waiting for transfers between devices: 39.5 us -> 48.5 us
  starting transfers between devices: 47.6 us -> 45.5 us
    ppermute x5, waiting for transfers between devices: 7.85 us -> 14.4 us  [swap(): return lax.ppermute(value, 'dp', [(i, i ^ offset) for i in range(8)])]
    pallas_call x1, Pallas kernels: 8.42 us -> 3.99 us  [per_device(): pl.pallas_call(product_kernel, grid=(1,), out_shape=outs, in_specs=[SMEM]...]
    pallas_call x1, Pallas kernels: 7.44 us -> 3.79 us  [per_device(): pl.pallas_call(forward_kernel, grid=(out_width // columns,), out_shape=sh...]
    pallas_call x4, Pallas kernels: 59.5 us -> 57 us  [run(): pl.pallas_call(kernel, grid=(1,), out_shape=tuple(outs), in_specs=[SMEM]...]
    unnamed x28 -> x30, local copies, waits for them, and re-layouts: 4.46 us -> 6.63 us
    all_to_all x1, starting transfers between devices: 21.4 us -> 19.3 us  [per_device(): lax.all_to_all(jnp.broadcast_to(term, (devices, 128)), ('section', 'dp'),...]
  transfers between devices with their start and end apart: 13 -> 13, of which waited for: 6 -> 8; matrix products, arithmetic and copies ran while one was open for 1% -> 1% of each run, Pallas kernels for 37% -> 33%
where the time goes in v4:
time: 182 us; the launch traced here: 181 us
  Pallas kernels  75.9 us (42%)
  waiting for transfers between devices  48.5 us (27%)
  starting transfers between devices  45.5 us (25%)
  local copies, waits for them, and re-layouts  9.99 us (5%)
    pallas_call x4, Pallas kernels, run(): pl.pallas_call(kernel, grid=(1,), out_shape=tuple(outs), in_specs=[SMEM]...  57 us
    all_to_all x1, starting transfers between devices, per_device(): lax.all_to_all(jnp.broadcast_to(term, (devices, 128)), ('section', 'dp'),...  19.3 us
    all_to_all x1, waiting for transfers between devices, per_device(): lax.all_to_all(sent, 'dp', 0, 0, tiled=True)  16.6 us
    ppermute x5, waiting for transfers between devices, swap(): return lax.ppermute(value, 'dp', [(i, i ^ offset) for i in range(8)])  14.4 us
    all_to_all x1, waiting for transfers between devices, per_device(): lax.all_to_all(jnp.broadcast_to(term, (devices, 128)), ('section', 'dp'),...  9.34 us
    unnamed x30, local copies, waits for them, and re-layouts  6.63 us
    pallas_call x1, Pallas kernels, per_device(): pl.pallas_call(lambda *refs: update_kernel(entries, *refs), grid=(steps,)...  6.57 us
    ppermute x5, starting transfers between devices, swap(): return lax.ppermute(value, 'dp', [(i, i ^ offset) for i in range(8)])  6.02 us
  transfers between devices with their start and end apart: 13, of which 8 were waited for; matrix products, arithmetic and copies ran while one was open for 1% of the time, Pallas kernels for 33%

profile of v4, /device:TPU:40, one launch (start us, length us, event | category | flops | bytes accessed | tf_op | source)
XLA Modules:
  0.0 181.4 jit_solution(14994674152161139221)
XLA Ops:
  0.6 1.0 slice.12
  1.9 3.2 %normalize.1 = bf16[8,64,1664]{2,1,0:T(8,128)(2,1)} custom-call(bf16[64,5120]{1,0:T(8,128)(2,1)} %bitcast.16, bf16[64,5120]{1,0:T(8,128)(2,1)} %bitcast.18, f32[1,5120]{1,0:T(1,128)} %gain_ref.3), custom_call_target="tpu_custom_call" | custom-call | flops 10000000 | bytes 3035136 | tf_op jit(solution)/shard_map/normalize/pallas_call | solution.py:333
  5.1 7.5 %collective-permute-done = bf16[64,3072]{1,0:T(8,128)(2,1)S(1)} collective-permute-done((bf16[64,3072]{1,0:T(8,128)(2,1)S(1)}, bf16[64,3072]{1,0:T(8,128)(2,1)S(1)}, u32[]{:S(2)}, u32[]{:S(2)}) %collective-permute-start) | collective-permute-done | bytes 393248 | tf_op jit(solution)/shard_map/ppermute | solution.py:362
  12.6 5.8 %all-to-all-start = ((bf16[8,64,1664]{2,1,0:T(8,128)(2,1)}), bf16[8,64,1664]{2,1,0:T(8,128)(2,1)S(1)}, u32[]{:S(2)}, u32[]{:S(2)}) async-start(bf16[8,64,1664]{2,1,0:T(8,128)(2,1)} %normalize.1), calls=%async_computation | async-start | bytes 3407872 | tf_op jit(solution)/shard_map/all_to_all | solution.py:473
  19.1 1.6 collective-permute-start.2
  20.7 1.8 collective-permute-start.1
  22.5 16.6 %all-to-all-done = bf16[8,64,1664]{2,1,0:T(8,128)(2,1)S(1)} async-done(((bf16[8,64,1664]{2,1,0:T(8,128)(2,1)}), bf16[8,64,1664]{2,1,0:T(8,128)(2,1)S(1)}, u32[]{:S(2)}, u32[]{:S(2)}) %all-to-all-start) | async-done | bytes 1703968 | tf_op jit(solution)/shard_map/all_to_all | solution.py:473
  39.0 13.4 %solve_act.1 = (f32[512,512]{1,0:T(8,128)S(1)}, bf16[512,640]{1,0:T(8,128)(2,1)S(1)}, bf16[512,512]{1,0:T(8,128)(2,1)S(1)}, bf16[512,256]{1,0:T(8,128)(2,1)S(1)}, bf16[512,128]{1,0:T(8,128)(2,1)S(1)}) custom-call(f32[1,1]{1,0:T(1,128)} %bitcast.10.damping_ref, s32[1,1]{1,0:T(1,128)} %bitcast.1.me_ref, bf16[512,1664]{1,0:T(8,128)(2,1)S(1)} %bitcast.14), custom_call_target="tpu_custom_call" | custom-call | flops 16000000000 | bytes 4325376 | tf_op jit(solution)/shard_map/solve_act/pallas_call | solution.py:333
  52.5 1.0 copy-done.8
  53.5 1.0 collective-permute-done.2.refs_2_
  54.4 1.0 slice.11
  55.5 1.9 %collective-permute-start.3 = (bf16[64,3072]{1,0:T(8,128)(2,1)S(1)}, bf16[64,3072]{1,0:T(8,128)(2,1)S(1)}, u32[]{:S(2)}, u32[]{:S(2)}) collective-permute-start(bf16[64,3072]{1,0:T(8,128)(2,1)S(1)} %slice.10), channel_id=1, source_target_pairs={{0,1},{1,0},{2,3},{3,2},{4,5},{5,4},{6,7},{7,6},{8,9},{9,8},{10,11... | collective-permute-start | bytes 1179656 | tf_op jit(solution)/shard_map/ppermute | solution.py:362
  58.0 3.8 %forward.1.refs_6_ = bf16[8,64,3712]{2,1,0:T(8,128)(2,1)S(1)} custom-call(bf16[512,1664]{1,0:T(8,128)(2,1)S(1)} %bitcast.15, bf16[640,3072]{1,0:T(8,128)(2,1)S(1)} %bitcast.12), custom_call_target="tpu_custom_call" | custom-call | flops 2000000000 | bytes 8000000 | tf_op jit(solution)/shard_map/forward/pallas_call | solution.py:479
  61.8 4.8 %collective-permute-done.3.refs_3_ = bf16[64,3072]{1,0:T(8,128)(2,1)S(1)} collective-permute-done((bf16[64,3072]{1,0:T(8,128)(2,1)S(1)}, bf16[64,3072]{1,0:T(8,128)(2,1)S(1)}, u32[]{:S(2)}, u32[]{:S(2)}) %collective-permute-start.3) | collective-permute-done | bytes 393248 | tf_op jit(solution)/shard_map/ppermute | solution.py:362
  66.6 1.1 collective-permute-done.4.refs_4_
  67.8 4.0 %products.1 = (bf16[512,3072]{1,0:T(8,128)(2,1)S(1)}, bf16[8,64,3712]{2,1,0:T(8,128)(2,1)S(1)}) custom-call(s32[1,1]{1,0:T(1,128)} %bitcast.1.me_ref, bf16[128,3072]{1,0:T(8,128)(2,1)S(1)} %pad_maximum_fusion.refs_0_, bf16[128,3072]{1,0:T(8,128)(2,1)} %collective-permute-done.1.refs_1_, ...), custom_call_target="tpu_custom_call", output_to_operand_aliasing={{1}: (7, {})} | custom-call | flops 2000000000 | bytes 10000000 | tf_op jit(solution)/shard_map/products/pallas_call | solution.py:496
  71.8 1.9 %copy-done = bf16[8,64,3712]{2,1,0:T(8,128)(2,1)} copy-done((bf16[8,64,3712]{2,1,0:T(8,128)(2,1)}, bf16[8,64,3712]{2,1,0:T(8,128)(2,1)S(1)}, u32[]{:S(2)}) %copy-start) | copy-done | bytes 3801112
  73.6 1.7 copy-done.3
  75.4 6.0 %all-to-all-start.2 = ((bf16[8,64,3712]{2,1,0:T(8,128)(2,1)}), bf16[8,64,3712]{2,1,0:T(8,128)(2,1)}, u32[]{:S(2)}, u32[]{:S(2)}) async-start(bf16[8,64,3712]{2,1,0:T(8,128)(2,1)} %copy-done), calls=%async_computation.2 | async-start | bytes 7602176 | tf_op jit(solution)/shard_map/all_to_all | solution.py:511
  81.4 37.7 %solve_grad.1 = (bf16[512,3072]{1,0:T(8,128)(2,1)}, f32[1,1]{1,0:T(1,128)}) custom-call(f32[1,1]{1,0:T(1,128)} %bitcast.11.damping_ref, bf16[512,3072]{1,0:T(8,128)(2,1)} %copy-done.3, f32[512,512]{1,0:T(8,128)} %copy-done.8), custom_call_target="tpu_custom_call" | custom-call | flops 44999999488 | bytes 7340036 | tf_op jit(solution)/shard_map/solve_grad/pallas_call | solution.py:333
  119.1 4.5 %all-to-all-done.2.parts_ref = bf16[8,64,3712]{2,1,0:T(8,128)(2,1)} async-done(((bf16[8,64,3712]{2,1,0:T(8,128)(2,1)}), bf16[8,64,3712]{2,1,0:T(8,128)(2,1)}, u32[]{:S(2)}, u32[]{:S(2)}) %all-to-all-start.2) | async-done | bytes 3801120 | tf_op jit(solution)/shard_map/all_to_all | solution.py:511
  123.6 4.6 %finish.1 = (bf16[1,64,5120]{2,1,0:T(8,128)(2,1)}, bf16[1,64,5120]{2,1,0:T(8,128)(2,1)}) custom-call(bf16[8,64,3712]{2,1,0:T(8,128)(2,1)} %all-to-all-done.2.parts_ref, bf16[64,5120]{1,0:T(8,128)(2,1)} %bitcast.17, bf16[64,5120]{1,0:T(8,128)(2,1)} %bitcast.19, bf16[64,5120]{1,0:T(8,128)(2,1)} %bitcast.21, f32[1,5120]{1,0:T(1,128)} %gain_ref.3), custom_call_target="tpu_custom_call" | custom-call | flops 10000000 | bytes 8000000 | tf_op jit(solution)/shard_map/finish/pallas_call | solution.py:536
  128.2 1.9 %collective-permute-start.5 = (bf16[1,64,5120]{2,1,0:T(8,128)(2,1)}, bf16[1,64,5120]{2,1,0:T(8,128)(2,1)S(1)}, u32[]{:S(2)}, u32[]{:S(2)}) collective-permute-start(bf16[1,64,5120]{2,1,0:T(8,128)(2,1)} %get-tuple-element.48), channel_id=1, source_target_pairs={{0,8},{8,16},{16,24},{24,32},{32,40},{40,48},{48,56},{56,64},{64,7... | collective-permute-start | bytes 1966088 | tf_op jit(solution)/shard_map/ppermute | solution.py:28
  130.2 1.3 collective-permute-start.6
  132.2 1.9 %collective-permute-start.8 = (bf16[512,256]{1,0:T(8,128)(2,1)S(1)}, bf16[512,256]{1,0:T(8,128)(2,1)S(1)}, u32[]{:S(2)}, u32[]{:S(2)}) collective-permute-start(bf16[512,256]{1,0:T(8,128)(2,1)S(1)} %get-tuple-element.53), channel_id=1, source_target_pairs={{2,1},{5,6},{10,9},{13,14},{18,17},{21,22},{26,25},{29,30},{34,33}... | collective-permute-start | bytes 786440 | tf_op jit(solution)/shard_map/ppermute | solution.py:514
  134.1 1.3 broadcast_in_dim.11
  135.4 19.3 %all-to-all-start.1 = ((f32[256,1,128]{2,1,0:T(1,128)}), f32[256,1,128]{2,1,0:T(1,128)S(1)}, u32[]{:S(2)}, u32[]{:S(2)}) async-start(f32[256,1,128]{2,1,0:T(1,128)} %broadcast_in_dim.11), calls=%async_computation.1 | async-start | bytes 262144 | tf_op jit(solution)/shard_map/all_to_all | solution.py:528
  154.8 2.4 %collective-permute-start.9 = (bf16[512,128]{1,0:T(8,128)(2,1)S(1)}, bf16[512,128]{1,0:T(8,128)(2,1)S(1)}, u32[]{:S(2)}, u32[]{:S(2)}) collective-permute-start(bf16[512,128]{1,0:T(8,128)(2,1)S(1)} %copy-done.7), channel_id=1, source_target_pairs={{2,3},{5,4},{10,11},{13,12},{18,19},{21,20},{26,27},{29,28},{34,35... | collective-permute-start | bytes 393224 | tf_op jit(solution)/shard_map/ppermute | solution.py:514
  157.2 3.6 %collective-permute-done.9.refs_3_ = bf16[512,128]{1,0:T(8,128)(2,1)S(1)} collective-permute-done((bf16[512,128]{1,0:T(8,128)(2,1)S(1)}, bf16[512,128]{1,0:T(8,128)(2,1)S(1)}, u32[]{:S(2)}, u32[]{:S(2)}) %collective-permute-start.9) | collective-permute-done | bytes 131104 | tf_op jit(solution)/shard_map/ppermute | solution.py:514
  161.8 2.6 %assemble.1.refs_1_ = bf16[640,512]{1,0:T(8,128)(2,1)} custom-call(s32[1,1]{1,0:T(1,128)} %bitcast.1.me_ref, bf16[512,640]{1,0:T(8,128)(2,1)} %copy-done.2, bf16[512,512]{1,0:T(8,128)(2,1)} %copy-done.9, bf16[512,256]{1,0:T(8,128)(2,1)} %copy-done.10, bf16[512,128]{1,0:T(8,128)(2,1)} %copy-done.11), custom_call_target="tpu_custom_call" | custom-call | flops 10000000 | bytes 2228224 | tf_op jit(solution)/shard_map/assemble/pallas_call | solution.py:333
  164.4 9.3 %all-to-all-done.1 = f32[256,1,128]{2,1,0:T(1,128)S(1)} async-done(((f32[256,1,128]{2,1,0:T(1,128)}), f32[256,1,128]{2,1,0:T(1,128)S(1)}, u32[]{:S(2)}, u32[]{:S(2)}) %all-to-all-start.1) | async-done | bytes 131104 | tf_op jit(solution)/shard_map/all_to_all | solution.py:528
  174.8 6.6 %update.1 = (bf16[640,3072]{1,0:T(8,128)(2,1)}, bf16[1,64,5120]{2,1,0:T(8,128)(2,1)}, bf16[1,64,5120]{2,1,0:T(8,128)(2,1)}) custom-call(f32[256,128]{1,0:T(8,128)} %bitcast.22, bf16[640,512]{1,0:T(8,128)(2,1)} %assemble.1.refs_1_, bf16[512,3072]{1,0:T(8,128)(2,1)} %get-tuple-element.55.refs_2_, bf16[1,64,5120]{2,1,0:T(8,128)(2,1)} %copy-done.13, ...), custom_call_target="tpu_custom_call" | custom-call | flops 2000000000 | bytes 8000000 | tf_op jit(solution)/shard_map/update/pallas_call | solution.py:560
  (37 shorter events, 3.7 us)
Async XLA Ops:
  1.7 10.9 %collective-permute-start = (bf16[64,3072]{1,0:T(8,128)(2,1)S(1)}, bf16[64,3072]{1,0:T(8,128)(2,1)S(1)}, u32[]{:S(2)}, u32[]{:S(2)}) collective-permute-start(bf16[64,3072]{1,0:T(8,128)(2,1)S(1)} %slice.12), channel_id=1, source_target_pairs={{0,4},{1,5},{2,6},{3,7},{4,0},{5,1},{6,2},{7,3},{8,12},{9,13},{10,... | collective-permute-start | bytes 1179656 | tf_op jit(solution)/shard_map/ppermute | solution.py:362
  12.6 26.4 %all-to-all-start = ((bf16[8,64,1664]{2,1,0:T(8,128)(2,1)}), bf16[8,64,1664]{2,1,0:T(8,128)(2,1)S(1)}, u32[]{:S(2)}, u32[]{:S(2)}) async-start(bf16[8,64,1664]{2,1,0:T(8,128)(2,1)} %normalize.1), calls=%async_computation | async-start | bytes 3407872 | tf_op jit(solution)/shard_map/all_to_all | solution.py:473
  19.1 35.3 %collective-permute-start.2 = (bf16[128,3072]{1,0:T(8,128)(2,1)S(1)}, bf16[128,3072]{1,0:T(8,128)(2,1)S(1)}, u32[]{:S(2)}, u32[]{:S(2)}) collective-permute-start(bf16[128,3072]{1,0:T(8,128)(2,1)S(1)} %pad_maximum_fusion.refs_0_), channel_id=1, source_target_pairs={{0,3},{1,2},{2,1},{3,0},{4,7},{5,6},{6,5},{7,4},{8,11},{9,10},{10,... | collective-permute-start | bytes 2359304 | tf_op jit(solution)/shard_map/ppermute | solution.py:362
  20.7 33.8 %collective-permute-start.1 = (bf16[128,3072]{1,0:T(8,128)(2,1)S(1)}, bf16[128,3072]{1,0:T(8,128)(2,1)}, u32[]{:S(2)}, u32[]{:S(2)}) collective-permute-start(bf16[128,3072]{1,0:T(8,128)(2,1)S(1)} %pad_maximum_fusion.refs_0_), channel_id=1, source_target_pairs={{0,1},{1,0},{2,3},{3,2},{4,5},{5,4},{6,7},{7,6},{8,9},{9,8},{10,11... | collective-permute-start | bytes 2359304 | tf_op jit(solution)/shard_map/ppermute | solution.py:362
  39.0 19.0 %copy-start.1 = (bf16[1,640,3072]{2,1,0:T(8,128)(2,1)S(1)}, bf16[1,640,3072]{2,1,0:T(8,128)(2,1)}, u32[]{:S(2)}) copy-start(bf16[1,640,3072]{2,1,0:T(8,128)(2,1)} %param.10) | copy-start | bytes 11796484
  52.5 1.0 copy-start.8
  53.5 8.4 %copy-start.2 = (bf16[512,640]{1,0:T(8,128)(2,1)}, bf16[512,640]{1,0:T(8,128)(2,1)S(1)}, u32[]{:S(2)}) copy-start(bf16[512,640]{1,0:T(8,128)(2,1)S(1)} %get-tuple-element.51.refs_0_) | copy-start | bytes 1966084
  53.5 8.4 %copy-start.4 = (bf16[512,512]{1,0:T(8,128)(2,1)}, bf16[512,512]{1,0:T(8,128)(2,1)S(1)}, u32[]{:S(2)}) copy-start(bf16[512,512]{1,0:T(8,128)(2,1)S(1)} %get-tuple-element.52) | copy-start | bytes 1572868
  53.5 8.4 %copy-start.6 = (bf16[512,128]{1,0:T(8,128)(2,1)}, bf16[512,128]{1,0:T(8,128)(2,1)S(1)}, u32[]{:S(2)}) copy-start(bf16[512,128]{1,0:T(8,128)(2,1)S(1)} %get-tuple-element.54) | copy-start | bytes 393220
  55.5 11.1 %collective-permute-start.3 = (bf16[64,3072]{1,0:T(8,128)(2,1)S(1)}, bf16[64,3072]{1,0:T(8,128)(2,1)S(1)}, u32[]{:S(2)}, u32[]{:S(2)}) collective-permute-start(bf16[64,3072]{1,0:T(8,128)(2,1)S(1)} %slice.10), channel_id=1, source_target_pairs={{0,1},{1,0},{2,3},{3,2},{4,5},{5,4},{6,7},{7,6},{8,9},{9,8},{10,11... | collective-permute-start | bytes 1179656 | tf_op jit(solution)/shard_map/ppermute | solution.py:362
  57.4 10.4 %collective-permute-start.4 = (bf16[64,3072]{1,0:T(8,128)(2,1)S(1)}, bf16[64,3072]{1,0:T(8,128)(2,1)S(1)}, u32[]{:S(2)}, u32[]{:S(2)}) collective-permute-start(bf16[64,3072]{1,0:T(8,128)(2,1)S(1)} %slice.11), channel_id=1, source_target_pairs={{0,3},{1,2},{2,1},{3,0},{4,7},{5,6},{6,5},{7,4},{8,11},{9,10},{10,... | collective-permute-start | bytes 1179656 | tf_op jit(solution)/shard_map/ppermute | solution.py:362
  71.8 1.9 %copy-start = (bf16[8,64,3712]{2,1,0:T(8,128)(2,1)}, bf16[8,64,3712]{2,1,0:T(8,128)(2,1)S(1)}, u32[]{:S(2)}) copy-start(bf16[8,64,3712]{2,1,0:T(8,128)(2,1)S(1)} %get-tuple-element.46) | copy-start | bytes 11403268
  73.6 1.7 copy-start.3
  75.4 48.3 %all-to-all-start.2 = ((bf16[8,64,3712]{2,1,0:T(8,128)(2,1)}), bf16[8,64,3712]{2,1,0:T(8,128)(2,1)}, u32[]{:S(2)}, u32[]{:S(2)}) async-start(bf16[8,64,3712]{2,1,0:T(8,128)(2,1)} %copy-done), calls=%async_computation.2 | async-start | bytes 7602176 | tf_op jit(solution)/shard_map/all_to_all | solution.py:511
  119.1 12.4 %copy-start.5 = (bf16[512,512]{1,0:T(8,128)(2,1)S(1)}, bf16[512,512]{1,0:T(8,128)(2,1)}, u32[]{:S(2)}) copy-start(bf16[512,512]{1,0:T(8,128)(2,1)} %copy-done.4) | copy-start | bytes 1572868
  119.1 35.7 %copy-start.7 = (bf16[512,128]{1,0:T(8,128)(2,1)S(1)}, bf16[512,128]{1,0:T(8,128)(2,1)}, u32[]{:S(2)}) copy-start(bf16[512,128]{1,0:T(8,128)(2,1)} %copy-done.6) | copy-start | bytes 393220
  128.2 45.5 %collective-permute-start.5 = (bf16[1,64,5120]{2,1,0:T(8,128)(2,1)}, bf16[1,64,5120]{2,1,0:T(8,128)(2,1)S(1)}, u32[]{:S(2)}, u32[]{:S(2)}) collective-permute-start(bf16[1,64,5120]{2,1,0:T(8,128)(2,1)} %get-tuple-element.48), channel_id=1, source_target_pairs={{0,8},{8,16},{16,24},{24,32},{32,40},{40,48},{48,56},{56,64},{64,7... | collective-permute-start | bytes 1966088 | tf_op jit(solution)/shard_map/ppermute | solution.py:28
  130.2 43.5 %collective-permute-start.6 = (bf16[1,64,5120]{2,1,0:T(8,128)(2,1)}, bf16[1,64,5120]{2,1,0:T(8,128)(2,1)S(1)}, u32[]{:S(2)}, u32[]{:S(2)}) collective-permute-start(bf16[1,64,5120]{2,1,0:T(8,128)(2,1)} %get-tuple-element.49), channel_id=1, source_target_pairs={{8,0},{16,8},{24,16},{32,24},{40,32},{48,40},{56,48},{64,56},{72,6... | collective-permute-start | bytes 1966088 | tf_op jit(solution)/shard_map/ppermute | solution.py:28
  131.5 29.4 %collective-permute-start.7 = (bf16[512,512]{1,0:T(8,128)(2,1)S(1)}, bf16[512,512]{1,0:T(8,128)(2,1)S(1)}, u32[]{:S(2)}, u32[]{:S(2)}) collective-permute-start(bf16[512,512]{1,0:T(8,128)(2,1)S(1)} %copy-done.5), channel_id=1, source_target_pairs={{0,1},{4,3},{7,6},{8,9},{12,11},{15,14},{16,17},{20,19},{23,22},{2... | collective-permute-start | bytes 1572872 | tf_op jit(solution)/shard_map/ppermute | solution.py:514
  132.2 28.6 %collective-permute-start.8 = (bf16[512,256]{1,0:T(8,128)(2,1)S(1)}, bf16[512,256]{1,0:T(8,128)(2,1)S(1)}, u32[]{:S(2)}, u32[]{:S(2)}) collective-permute-start(bf16[512,256]{1,0:T(8,128)(2,1)S(1)} %get-tuple-element.53), channel_id=1, source_target_pairs={{2,1},{5,6},{10,9},{13,14},{18,17},{21,22},{26,25},{29,30},{34,33}... | collective-permute-start | bytes 786440 | tf_op jit(solution)/shard_map/ppermute | solution.py:514
  135.4 38.3 %all-to-all-start.1 = ((f32[256,1,128]{2,1,0:T(1,128)}), f32[256,1,128]{2,1,0:T(1,128)S(1)}, u32[]{:S(2)}, u32[]{:S(2)}) async-start(f32[256,1,128]{2,1,0:T(1,128)} %broadcast_in_dim.11), calls=%async_computation.1 | async-start | bytes 262144 | tf_op jit(solution)/shard_map/all_to_all | solution.py:528
  154.8 6.0 %collective-permute-start.9 = (bf16[512,128]{1,0:T(8,128)(2,1)S(1)}, bf16[512,128]{1,0:T(8,128)(2,1)S(1)}, u32[]{:S(2)}, u32[]{:S(2)}) collective-permute-start(bf16[512,128]{1,0:T(8,128)(2,1)S(1)} %copy-done.7), channel_id=1, source_target_pairs={{2,3},{5,4},{10,11},{13,12},{18,19},{21,20},{26,27},{29,28},{34,35... | collective-permute-start | bytes 393224 | tf_op jit(solution)/shard_map/ppermute | solution.py:514
  160.8 0.6 copy-start.11
  160.8 0.7 copy-start.10
  160.9 0.9 copy-start.9
  173.7 0.6 copy-start.12
  173.7 0.9 copy-start.13
  173.7 1.1 copy-start.14

commit v5 on v4

--- a/solution.py
+++ b/solution.py
@@ -305,7 +305,7 @@
 
     by_rows(count, 256, compare)
     product = jnp.sum(right[...], axis=0, keepdims=True)
-    term_ref[...] = jnp.sum(product, axis=1, keepdims=True)
+    term_ref[...] = jnp.broadcast_to(jnp.sum(product, axis=1, keepdims=True), term_ref.shape)
 
 
 SMEM = pl.BlockSpec(memory_space=pltpu.SMEM)
@@ -351,9 +351,9 @@
     return run(act_kernel, "solve_act", outs, (damping, me), (rows,), 16 * 10**9, scratch, 28)
 
 
-def solve_grad(damping, rows, left):
+def solve_grad(damping, rows, left, devices):
     count, width = rows.shape
-    outs = [shape(count, width), shape(1, 1, dtype=F32)]
+    outs = [shape(count, width), shape(devices, UNIT, dtype=F32)]
     scratch = [pltpu.VMEM((count, count), F32)] + solver_scratch(count)
     return run(grad_kernel, "solve_grad", outs, (damping,), (rows, left), 45 * 10**9, scratch)
 
@@ -433,14 +433,24 @@
 
 
 def update_kernel(
-    entries, terms_ref, turned_ref, grad_ref, fwd_ref, back_ref, out_ref, next_ref, last_ref
+    entries, terms_ref, turned_ref, grad_ref, fwd_ref, back_ref, out_ref, next_ref, last_ref, held
 ):
-    terms = terms_ref[...]
-    total = jnp.sum(jnp.sum(terms, axis=0, keepdims=True)[:, :1], axis=1, keepdims=True)
-    ratio = jnp.sqrt(entries / total)
-    out_ref[...] = (ratio * dot(turned_ref[...], grad_ref[...], precision=None)).astype(BF16)
-    next_ref[...] = fwd_ref[...]
-    last_ref[...] = back_ref[...]
+    step = pl.program_id(0)
+
+    def columns(width):
+        return pl.ds(pl.multiple_of(step * width, width), width)
+
+    @pl.when(step == 0)
+    def _():
+        terms = jnp.sum(terms_ref[...], axis=0, keepdims=True)[:, :1]
+        held[...] = jnp.broadcast_to(jnp.sqrt(entries / terms), held.shape)
+
+    ratio = held[:1, :1]
+    precond = dot(turned_ref[...], grad_ref[:, columns(out_ref.shape[1])], precision=None)
+    out_ref[...] = (ratio * precond).astype(BF16)
+    width = next_ref.shape[2]
+    next_ref[...] = fwd_ref[:, :, columns(width)]
+    last_ref[...] = back_ref[:, :, columns(width)]
 
 
 def per_device(x_fwd, x_bwd, grad_in, gain, weight, damping):
@@ -523,11 +533,9 @@
         [pltpu.VMEM((group, (2 * WINDOW + 2) * UNIT), BF16)],
     )
 
-    grad_tilde, term = solve_grad(damp_value, group_grad, left)
     devices = lax.axis_size("section") * groups
-    terms = lax.all_to_all(
-        jnp.broadcast_to(term, (devices, 128)), ("section", "dp"), 0, 0, tiled=True
-    )
+    grad_tilde, term = solve_grad(damp_value, group_grad, left, devices)
+    terms = lax.all_to_all(term, ("section", "dp"), 0, 0, tiled=True)
 
     parts, _ = lax.optimization_barrier((parts, term))
     step = 16
@@ -561,15 +569,10 @@
         lambda *refs: update_kernel(entries, *refs),
         grid=(steps,),
         out_shape=(shape(own_rows, out_width),) + (shape(1, tokens, width),) * 2,
-        in_specs=[
-            pl.BlockSpec((devices, 128), lambda i: (0, 0)),
-            pl.BlockSpec((own_rows, group), lambda i: (0, 0)),
-            pl.BlockSpec((group, columns), lambda i: (0, i)),
-            same,
-            same,
-        ],
+        in_specs=[pl.BlockSpec((devices, 128), lambda i: (0, 0))] + [VMEM] * 4,
         out_specs=(pl.BlockSpec((own_rows, columns), lambda i: (0, i)), same, same),
-        compiler_params=params(),
+        scratch_shapes=[pltpu.VMEM((8, 128), F32)],
+        compiler_params=params(20),
         cost_estimate=cost(2 * 10**9, 8 * 10**6),
         name="update",
     )(terms, turned, grad_tilde, next_fwd, next_grad)

time: 182 us -> 182 us (level)
  Pallas kernels: 75.9 us -> 73.7 us
    pallas_call x1, Pallas kernels: 6.57 us -> 4.17 us  [per_device(): pl.pallas_call(lambda *refs: update_kernel(entries, *refs), grid=(steps,)...]
    unnamed x30 -> x28, local copies, waits for them, and re-layouts: 6.63 us -> 8.49 us
  transfers between devices with their start and end apart: 13 -> 13, of which waited for: 8 -> 8; matrix products, arithmetic and copies ran while one was open for 1% -> 0% of each run, Pallas kernels for 33% -> 34%
where the time goes in v5:
time: 182 us; the launch traced here: 181 us
  Pallas kernels  73.7 us (40%)
  waiting for transfers between devices  49.6 us (27%)
  starting transfers between devices  45.6 us (25%)
  local copies, waits for them, and re-layouts  10.6 us (6%)
    pallas_call x4, Pallas kernels, run(): pl.pallas_call(kernel, grid=(1,), out_shape=tuple(outs), in_specs=[SMEM]...  57.1 us
    all_to_all x1, starting transfers between devices, per_device(): terms = lax.all_to_all(term, ('section', 'dp'), 0, 0, tiled=True)  19.4 us
    all_to_all x1, waiting for transfers between devices, per_device(): lax.all_to_all(sent, 'dp', 0, 0, tiled=True)  16.6 us
    ppermute x5, waiting for transfers between devices, swap(): return lax.ppermute(value, 'dp', [(i, i ^ offset) for i in range(8)])  14.4 us
    all_to_all x1, waiting for transfers between devices, per_device(): terms = lax.all_to_all(term, ('section', 'dp'), 0, 0, tiled=True)  10.5 us
    unnamed x28, local copies, waits for them, and re-layouts  8.49 us
    ppermute x5, starting transfers between devices, swap(): return lax.ppermute(value, 'dp', [(i, i ^ offset) for i in range(8)])  6.03 us
    all_to_all x1, starting transfers between devices, per_device(): parts = lax.all_to_all(products, 'dp', 0, 0, tiled=True)  6.01 us
  transfers between devices with their start and end apart: 13, of which 8 were waited for; matrix products, arithmetic and copies ran while one was open for 0% of the time, Pallas kernels for 34%

profile of v5, /device:TPU:40, one launch (start us, length us, event | category | flops | bytes accessed | tf_op | source)
XLA Modules:
  0.0 180.9 jit_solution(9491640106830588273)
XLA Ops:
  0.6 1.0 slice.12
  1.9 3.2 %normalize.1 = bf16[8,64,1664]{2,1,0:T(8,128)(2,1)} custom-call(bf16[64,5120]{1,0:T(8,128)(2,1)} %bitcast.19, bf16[64,5120]{1,0:T(8,128)(2,1)} %bitcast.21, f32[1,5120]{1,0:T(1,128)} %gain_ref.3), custom_call_target="tpu_custom_call" | custom-call | flops 10000000 | bytes 3035136 | tf_op jit(solution)/shard_map/normalize/pallas_call | solution.py:333
  5.1 7.5 %collective-permute-done = bf16[64,3072]{1,0:T(8,128)(2,1)S(1)} collective-permute-done((bf16[64,3072]{1,0:T(8,128)(2,1)S(1)}, bf16[64,3072]{1,0:T(8,128)(2,1)S(1)}, u32[]{:S(2)}, u32[]{:S(2)}) %collective-permute-start) | collective-permute-done | bytes 393248 | tf_op jit(solution)/shard_map/ppermute | solution.py:362
  12.6 5.8 %all-to-all-start = ((bf16[8,64,1664]{2,1,0:T(8,128)(2,1)}), bf16[8,64,1664]{2,1,0:T(8,128)(2,1)S(1)}, u32[]{:S(2)}, u32[]{:S(2)}) async-start(bf16[8,64,1664]{2,1,0:T(8,128)(2,1)} %normalize.1), calls=%async_computation | async-start | bytes 3407872 | tf_op jit(solution)/shard_map/all_to_all | solution.py:483
  19.1 1.6 collective-permute-start.2
  20.7 1.8 collective-permute-start.1
  22.5 16.6 %all-to-all-done = bf16[8,64,1664]{2,1,0:T(8,128)(2,1)S(1)} async-done(((bf16[8,64,1664]{2,1,0:T(8,128)(2,1)}), bf16[8,64,1664]{2,1,0:T(8,128)(2,1)S(1)}, u32[]{:S(2)}, u32[]{:S(2)}) %all-to-all-start) | async-done | bytes 1703968 | tf_op jit(solution)/shard_map/all_to_all | solution.py:483
  39.0 13.4 %solve_act.1 = (f32[512,512]{1,0:T(8,128)S(1)}, bf16[512,640]{1,0:T(8,128)(2,1)S(1)}, bf16[512,512]{1,0:T(8,128)(2,1)S(1)}, bf16[512,256]{1,0:T(8,128)(2,1)S(1)}, bf16[512,128]{1,0:T(8,128)(2,1)S(1)}) custom-call(f32[1,1]{1,0:T(1,128)} %bitcast.12.damping_ref, s32[1,1]{1,0:T(1,128)} %bitcast.1.me_ref, bf16[512,1664]{1,0:T(8,128)(2,1)S(1)} %bitcast.16), custom_call_target="tpu_custom_call" | custom-call | flops 16000000000 | bytes 4325376 | tf_op jit(solution)/shard_map/solve_act/pallas_call | solution.py:333
  53.5 1.0 collective-permute-done.2.refs_2_
  54.4 1.0 slice.11
  55.5 1.9 %collective-permute-start.3 = (bf16[64,3072]{1,0:T(8,128)(2,1)S(1)}, bf16[64,3072]{1,0:T(8,128)(2,1)S(1)}, u32[]{:S(2)}, u32[]{:S(2)}) collective-permute-start(bf16[64,3072]{1,0:T(8,128)(2,1)S(1)} %slice.10), channel_id=1, source_target_pairs={{0,1},{1,0},{2,3},{3,2},{4,5},{5,4},{6,7},{7,6},{8,9},{9,8},{10,11... | collective-permute-start | bytes 1179656 | tf_op jit(solution)/shard_map/ppermute | solution.py:362
  58.0 3.8 %forward.1.refs_6_ = bf16[8,64,3712]{2,1,0:T(8,128)(2,1)S(1)} custom-call(bf16[512,1664]{1,0:T(8,128)(2,1)S(1)} %bitcast.17, bf16[640,3072]{1,0:T(8,128)(2,1)S(1)} %bitcast.14), custom_call_target="tpu_custom_call" | custom-call | flops 2000000000 | bytes 8000000 | tf_op jit(solution)/shard_map/forward/pallas_call | solution.py:489
  61.9 4.8 %collective-permute-done.3.refs_3_ = bf16[64,3072]{1,0:T(8,128)(2,1)S(1)} collective-permute-done((bf16[64,3072]{1,0:T(8,128)(2,1)S(1)}, bf16[64,3072]{1,0:T(8,128)(2,1)S(1)}, u32[]{:S(2)}, u32[]{:S(2)}) %collective-permute-start.3) | collective-permute-done | bytes 393248 | tf_op jit(solution)/shard_map/ppermute | solution.py:362
  66.6 1.1 collective-permute-done.4.refs_4_
  67.8 4.0 %products.1 = (bf16[512,3072]{1,0:T(8,128)(2,1)S(1)}, bf16[8,64,3712]{2,1,0:T(8,128)(2,1)S(1)}) custom-call(s32[1,1]{1,0:T(1,128)} %bitcast.1.me_ref, bf16[128,3072]{1,0:T(8,128)(2,1)S(1)} %pad_maximum_fusion.refs_0_, bf16[128,3072]{1,0:T(8,128)(2,1)} %collective-permute-done.1.refs_1_, ...), custom_call_target="tpu_custom_call", output_to_operand_aliasing={{1}: (7, {})} | custom-call | flops 2000000000 | bytes 10000000 | tf_op jit(solution)/shard_map/products/pallas_call | solution.py:506
  71.8 1.9 %copy-done = bf16[8,64,3712]{2,1,0:T(8,128)(2,1)} copy-done((bf16[8,64,3712]{2,1,0:T(8,128)(2,1)}, bf16[8,64,3712]{2,1,0:T(8,128)(2,1)S(1)}, u32[]{:S(2)}) %copy-start) | copy-done | bytes 3801112
  73.6 1.7 copy-done.4
  75.4 6.0 %all-to-all-start.2 = ((bf16[8,64,3712]{2,1,0:T(8,128)(2,1)}), bf16[8,64,3712]{2,1,0:T(8,128)(2,1)}, u32[]{:S(2)}, u32[]{:S(2)}) async-start(bf16[8,64,3712]{2,1,0:T(8,128)(2,1)} %copy-done), calls=%async_computation.2 | async-start | bytes 7602176 | tf_op jit(solution)/shard_map/all_to_all | solution.py:521
  81.4 37.9 %solve_grad.1 = (bf16[512,3072]{1,0:T(8,128)(2,1)}, f32[256,128]{1,0:T(8,128)}) custom-call(f32[1,1]{1,0:T(1,128)} %bitcast.13.damping_ref, bf16[512,3072]{1,0:T(8,128)(2,1)} %copy-done.4, f32[512,512]{1,0:T(8,128)} %copy-done.10), custom_call_target="tpu_custom_call" | custom-call | flops 44999999488 | bytes 7471104 | tf_op jit(solution)/shard_map/solve_grad/pallas_call | solution.py:333
  119.2 4.4 %all-to-all-done.2.parts_ref = bf16[8,64,3712]{2,1,0:T(8,128)(2,1)} async-done(((bf16[8,64,3712]{2,1,0:T(8,128)(2,1)}), bf16[8,64,3712]{2,1,0:T(8,128)(2,1)}, u32[]{:S(2)}, u32[]{:S(2)}) %all-to-all-start.2) | async-done | bytes 3801120 | tf_op jit(solution)/shard_map/all_to_all | solution.py:521
  123.6 4.6 %finish.1 = (bf16[1,64,5120]{2,1,0:T(8,128)(2,1)}, bf16[1,64,5120]{2,1,0:T(8,128)(2,1)}) custom-call(bf16[8,64,3712]{2,1,0:T(8,128)(2,1)} %all-to-all-done.2.parts_ref, bf16[64,5120]{1,0:T(8,128)(2,1)} %bitcast.20, bf16[64,5120]{1,0:T(8,128)(2,1)} %bitcast.22, bf16[64,5120]{1,0:T(8,128)(2,1)} %bitcast.24, f32[1,5120]{1,0:T(1,128)} %gain_ref.3), custom_call_target="tpu_custom_call" | custom-call | flops 10000000 | bytes 8000000 | tf_op jit(solution)/shard_map/finish/pallas_call | solution.py:544
  128.2 1.9 %collective-permute-start.5 = (bf16[1,64,5120]{2,1,0:T(8,128)(2,1)}, bf16[1,64,5120]{2,1,0:T(8,128)(2,1)S(1)}, u32[]{:S(2)}, u32[]{:S(2)}) collective-permute-start(bf16[1,64,5120]{2,1,0:T(8,128)(2,1)} %get-tuple-element.48), channel_id=1, source_target_pairs={{0,8},{8,16},{16,24},{24,32},{32,40},{40,48},{48,56},{56,64},{64,7... | collective-permute-start | bytes 1966088 | tf_op jit(solution)/shard_map/ppermute | solution.py:28
  130.2 1.3 collective-permute-start.6
  132.2 1.9 %collective-permute-start.8 = (bf16[512,256]{1,0:T(8,128)(2,1)S(1)}, bf16[512,256]{1,0:T(8,128)(2,1)S(1)}, u32[]{:S(2)}, u32[]{:S(2)}) collective-permute-start(bf16[512,256]{1,0:T(8,128)(2,1)S(1)} %get-tuple-element.53), channel_id=1, source_target_pairs={{2,1},{5,6},{10,9},{13,14},{18,17},{21,22},{26,25},{29,30},{34,33}... | collective-permute-start | bytes 786440 | tf_op jit(solution)/shard_map/ppermute | solution.py:524
  134.1 19.4 %all-to-all-start.1 = ((f32[256,1,128]{2,1,0:T(1,128)}), f32[256,1,128]{2,1,0:T(1,128)S(1)}, u32[]{:S(2)}, u32[]{:S(2)}) async-start(f32[256,1,128]{2,1,0:T(1,128)} %bitcast.8), calls=%async_computation.1 | async-start | bytes 262144 | tf_op jit(solution)/shard_map/all_to_all | solution.py:538
  153.6 2.4 %collective-permute-start.9 = (bf16[512,128]{1,0:T(8,128)(2,1)S(1)}, bf16[512,128]{1,0:T(8,128)(2,1)S(1)}, u32[]{:S(2)}, u32[]{:S(2)}) collective-permute-start(bf16[512,128]{1,0:T(8,128)(2,1)S(1)} %copy-done.8), channel_id=1, source_target_pairs={{2,3},{5,4},{10,11},{13,12},{18,19},{21,20},{26,27},{29,28},{34,35... | collective-permute-start | bytes 393224 | tf_op jit(solution)/shard_map/ppermute | solution.py:524
  156.0 3.6 %collective-permute-done.9.refs_3_ = bf16[512,128]{1,0:T(8,128)(2,1)S(1)} collective-permute-done((bf16[512,128]{1,0:T(8,128)(2,1)S(1)}, bf16[512,128]{1,0:T(8,128)(2,1)S(1)}, u32[]{:S(2)}, u32[]{:S(2)}) %collective-permute-start.9) | collective-permute-done | bytes 131104 | tf_op jit(solution)/shard_map/ppermute | solution.py:524
  160.6 2.6 %assemble.1.refs_1_ = bf16[640,512]{1,0:T(8,128)(2,1)} custom-call(s32[1,1]{1,0:T(1,128)} %bitcast.1.me_ref, bf16[512,640]{1,0:T(8,128)(2,1)} %copy-done.2, bf16[512,512]{1,0:T(8,128)(2,1)} %copy-done.11, bf16[512,256]{1,0:T(8,128)(2,1)} %copy-done.12, bf16[512,128]{1,0:T(8,128)(2,1)} %copy-done.13), custom_call_target="tpu_custom_call" | custom-call | flops 10000000 | bytes 2228224 | tf_op jit(solution)/shard_map/assemble/pallas_call | solution.py:333
  163.2 10.5 %all-to-all-done.1 = f32[256,1,128]{2,1,0:T(1,128)S(1)} async-done(((f32[256,1,128]{2,1,0:T(1,128)}), f32[256,1,128]{2,1,0:T(1,128)S(1)}, u32[]{:S(2)}, u32[]{:S(2)}) %all-to-all-start.1) | async-done | bytes 131104 | tf_op jit(solution)/shard_map/all_to_all | solution.py:538
  173.7 1.1 copy-done.3
  174.8 1.9 %copy-done.9 = bf16[512,3072]{1,0:T(8,128)(2,1)S(1)} copy-done((bf16[512,3072]{1,0:T(8,128)(2,1)S(1)}, bf16[512,3072]{1,0:T(8,128)(2,1)}, u32[]{:S(2)}) %copy-start.9) | copy-done | bytes 3145752
  176.7 4.2 %update.1 = (bf16[640,3072]{1,0:T(8,128)(2,1)}, bf16[1,64,5120]{2,1,0:T(8,128)(2,1)}, bf16[1,64,5120]{2,1,0:T(8,128)(2,1)}) custom-call(f32[256,128]{1,0:T(8,128)S(1)} %bitcast.18, bf16[640,512]{1,0:T(8,128)(2,1)S(1)} %copy-done.3, bf16[512,3072]{1,0:T(8,128)(2,1)S(1)} %copy-done.9, bf16[1,64,5120]{2,1,0:T(8,128)(2,1)S(1)} %collective-permute-done.5.refs_3_, ...), custom_call_target="tpu_custom_call" | custom-call | flops 2000000000 | bytes 8000000 | tf_op jit(solution)/shard_map/update/pallas_call | solution.py:568
  (34 shorter events, 3.6 us)
Async XLA Ops:
  1.7 10.9 %collective-permute-start = (bf16[64,3072]{1,0:T(8,128)(2,1)S(1)}, bf16[64,3072]{1,0:T(8,128)(2,1)S(1)}, u32[]{:S(2)}, u32[]{:S(2)}) collective-permute-start(bf16[64,3072]{1,0:T(8,128)(2,1)S(1)} %slice.12), channel_id=1, source_target_pairs={{0,4},{1,5},{2,6},{3,7},{4,0},{5,1},{6,2},{7,3},{8,12},{9,13},{10,... | collective-permute-start | bytes 1179656 | tf_op jit(solution)/shard_map/ppermute | solution.py:362
  12.6 26.4 %all-to-all-start = ((bf16[8,64,1664]{2,1,0:T(8,128)(2,1)}), bf16[8,64,1664]{2,1,0:T(8,128)(2,1)S(1)}, u32[]{:S(2)}, u32[]{:S(2)}) async-start(bf16[8,64,1664]{2,1,0:T(8,128)(2,1)} %normalize.1), calls=%async_computation | async-start | bytes 3407872 | tf_op jit(solution)/shard_map/all_to_all | solution.py:483
  19.1 35.3 %collective-permute-start.2 = (bf16[128,3072]{1,0:T(8,128)(2,1)S(1)}, bf16[128,3072]{1,0:T(8,128)(2,1)S(1)}, u32[]{:S(2)}, u32[]{:S(2)}) collective-permute-start(bf16[128,3072]{1,0:T(8,128)(2,1)S(1)} %pad_maximum_fusion.refs_0_), channel_id=1, source_target_pairs={{0,3},{1,2},{2,1},{3,0},{4,7},{5,6},{6,5},{7,4},{8,11},{9,10},{10,... | collective-permute-start | bytes 2359304 | tf_op jit(solution)/shard_map/ppermute | solution.py:362
  20.7 33.8 %collective-permute-start.1 = (bf16[128,3072]{1,0:T(8,128)(2,1)S(1)}, bf16[128,3072]{1,0:T(8,128)(2,1)}, u32[]{:S(2)}, u32[]{:S(2)}) collective-permute-start(bf16[128,3072]{1,0:T(8,128)(2,1)S(1)} %pad_maximum_fusion.refs_0_), channel_id=1, source_target_pairs={{0,1},{1,0},{2,3},{3,2},{4,5},{5,4},{6,7},{7,6},{8,9},{9,8},{10,11... | collective-permute-start | bytes 2359304 | tf_op jit(solution)/shard_map/ppermute | solution.py:362
  39.0 19.0 %copy-start.1 = (bf16[1,640,3072]{2,1,0:T(8,128)(2,1)S(1)}, bf16[1,640,3072]{2,1,0:T(8,128)(2,1)}, u32[]{:S(2)}) copy-start(bf16[1,640,3072]{2,1,0:T(8,128)(2,1)} %param.10) | copy-start | bytes 11796484
  52.5 1.0 copy-start.10
  53.5 8.4 %copy-start.2 = (bf16[512,640]{1,0:T(8,128)(2,1)}, bf16[512,640]{1,0:T(8,128)(2,1)S(1)}, u32[]{:S(2)}) copy-start(bf16[512,640]{1,0:T(8,128)(2,1)S(1)} %get-tuple-element.51.refs_0_) | copy-start | bytes 1966084
  53.5 8.4 %copy-start.5 = (bf16[512,512]{1,0:T(8,128)(2,1)}, bf16[512,512]{1,0:T(8,128)(2,1)S(1)}, u32[]{:S(2)}) copy-start(bf16[512,512]{1,0:T(8,128)(2,1)S(1)} %get-tuple-element.52) | copy-start | bytes 1572868
  53.5 8.4 %copy-start.7 = (bf16[512,128]{1,0:T(8,128)(2,1)}, bf16[512,128]{1,0:T(8,128)(2,1)S(1)}, u32[]{:S(2)}) copy-start(bf16[512,128]{1,0:T(8,128)(2,1)S(1)} %get-tuple-element.54) | copy-start | bytes 393220
  55.5 11.1 %collective-permute-start.3 = (bf16[64,3072]{1,0:T(8,128)(2,1)S(1)}, bf16[64,3072]{1,0:T(8,128)(2,1)S(1)}, u32[]{:S(2)}, u32[]{:S(2)}) collective-permute-start(bf16[64,3072]{1,0:T(8,128)(2,1)S(1)} %slice.10), channel_id=1, source_target_pairs={{0,1},{1,0},{2,3},{3,2},{4,5},{5,4},{6,7},{7,6},{8,9},{9,8},{10,11... | collective-permute-start | bytes 1179656 | tf_op jit(solution)/shard_map/ppermute | solution.py:362
  57.4 10.4 %collective-permute-start.4 = (bf16[64,3072]{1,0:T(8,128)(2,1)S(1)}, bf16[64,3072]{1,0:T(8,128)(2,1)S(1)}, u32[]{:S(2)}, u32[]{:S(2)}) collective-permute-start(bf16[64,3072]{1,0:T(8,128)(2,1)S(1)} %slice.11), channel_id=1, source_target_pairs={{0,3},{1,2},{2,1},{3,0},{4,7},{5,6},{6,5},{7,4},{8,11},{9,10},{10,... | collective-permute-start | bytes 1179656 | tf_op jit(solution)/shard_map/ppermute | solution.py:362
  71.8 1.9 %copy-start = (bf16[8,64,3712]{2,1,0:T(8,128)(2,1)}, bf16[8,64,3712]{2,1,0:T(8,128)(2,1)S(1)}, u32[]{:S(2)}) copy-start(bf16[8,64,3712]{2,1,0:T(8,128)(2,1)S(1)} %get-tuple-element.46) | copy-start | bytes 11403268
  73.6 1.7 copy-start.4
  75.4 48.3 %all-to-all-start.2 = ((bf16[8,64,3712]{2,1,0:T(8,128)(2,1)}), bf16[8,64,3712]{2,1,0:T(8,128)(2,1)}, u32[]{:S(2)}, u32[]{:S(2)}) async-start(bf16[8,64,3712]{2,1,0:T(8,128)(2,1)} %copy-done), calls=%async_computation.2 | async-start | bytes 7602176 | tf_op jit(solution)/shard_map/all_to_all | solution.py:521
  119.2 12.3 %copy-start.6 = (bf16[512,512]{1,0:T(8,128)(2,1)S(1)}, bf16[512,512]{1,0:T(8,128)(2,1)}, u32[]{:S(2)}) copy-start(bf16[512,512]{1,0:T(8,128)(2,1)} %copy-done.5) | copy-start | bytes 1572868
  119.2 34.4 %copy-start.8 = (bf16[512,128]{1,0:T(8,128)(2,1)S(1)}, bf16[512,128]{1,0:T(8,128)(2,1)}, u32[]{:S(2)}) copy-start(bf16[512,128]{1,0:T(8,128)(2,1)} %copy-done.7) | copy-start | bytes 393220
  128.2 45.5 %collective-permute-start.5 = (bf16[1,64,5120]{2,1,0:T(8,128)(2,1)}, bf16[1,64,5120]{2,1,0:T(8,128)(2,1)S(1)}, u32[]{:S(2)}, u32[]{:S(2)}) collective-permute-start(bf16[1,64,5120]{2,1,0:T(8,128)(2,1)} %get-tuple-element.48), channel_id=1, source_target_pairs={{0,8},{8,16},{16,24},{24,32},{32,40},{40,48},{48,56},{56,64},{64,7... | collective-permute-start | bytes 1966088 | tf_op jit(solution)/shard_map/ppermute | solution.py:28
  130.2 43.5 %collective-permute-start.6 = (bf16[1,64,5120]{2,1,0:T(8,128)(2,1)}, bf16[1,64,5120]{2,1,0:T(8,128)(2,1)S(1)}, u32[]{:S(2)}, u32[]{:S(2)}) collective-permute-start(bf16[1,64,5120]{2,1,0:T(8,128)(2,1)} %get-tuple-element.49), channel_id=1, source_target_pairs={{8,0},{16,8},{24,16},{32,24},{40,32},{48,40},{56,48},{64,56},{72,6... | collective-permute-start | bytes 1966088 | tf_op jit(solution)/shard_map/ppermute | solution.py:28
  131.5 28.2 %collective-permute-start.7 = (bf16[512,512]{1,0:T(8,128)(2,1)S(1)}, bf16[512,512]{1,0:T(8,128)(2,1)S(1)}, u32[]{:S(2)}, u32[]{:S(2)}) collective-permute-start(bf16[512,512]{1,0:T(8,128)(2,1)S(1)} %copy-done.6), channel_id=1, source_target_pairs={{0,1},{4,3},{7,6},{8,9},{12,11},{15,14},{16,17},{20,19},{23,22},{2... | collective-permute-start | bytes 1572872 | tf_op jit(solution)/shard_map/ppermute | solution.py:524
  132.2 27.5 %collective-permute-start.8 = (bf16[512,256]{1,0:T(8,128)(2,1)S(1)}, bf16[512,256]{1,0:T(8,128)(2,1)S(1)}, u32[]{:S(2)}, u32[]{:S(2)}) collective-permute-start(bf16[512,256]{1,0:T(8,128)(2,1)S(1)} %get-tuple-element.53), channel_id=1, source_target_pairs={{2,1},{5,6},{10,9},{13,14},{18,17},{21,22},{26,25},{29,30},{34,33}... | collective-permute-start | bytes 786440 | tf_op jit(solution)/shard_map/ppermute | solution.py:524
  134.1 39.6 %all-to-all-start.1 = ((f32[256,1,128]{2,1,0:T(1,128)}), f32[256,1,128]{2,1,0:T(1,128)S(1)}, u32[]{:S(2)}, u32[]{:S(2)}) async-start(f32[256,1,128]{2,1,0:T(1,128)} %bitcast.8), calls=%async_computation.1 | async-start | bytes 262144 | tf_op jit(solution)/shard_map/all_to_all | solution.py:538
  153.6 6.1 %collective-permute-start.9 = (bf16[512,128]{1,0:T(8,128)(2,1)S(1)}, bf16[512,128]{1,0:T(8,128)(2,1)S(1)}, u32[]{:S(2)}, u32[]{:S(2)}) collective-permute-start(bf16[512,128]{1,0:T(8,128)(2,1)S(1)} %copy-done.8), channel_id=1, source_target_pairs={{2,3},{5,4},{10,11},{13,12},{18,19},{21,20},{26,27},{29,28},{34,35... | collective-permute-start | bytes 393224 | tf_op jit(solution)/shard_map/ppermute | solution.py:524
  159.6 0.7 copy-start.13
  159.6 0.8 copy-start.12
  159.7 0.9 copy-start.11
  173.7 1.1 copy-start.3
  174.8 1.9 %copy-start.9 = (bf16[512,3072]{1,0:T(8,128)(2,1)S(1)}, bf16[512,3072]{1,0:T(8,128)(2,1)}, u32[]{:S(2)}) copy-start(bf16[512,3072]{1,0:T(8,128)(2,1)} %get-tuple-element.55.refs_2_) | copy-start | bytes 9437188
